TPU v7x, 512 devices: a whole 4x8x8 slice. The times are simulated.
512 devices in a mesh: mode: 8 (over y_hi, core), row: 64 (over z, y_lo, x).
Axes of the slice: x: 4, y: 8 (y_hi: 4, y_lo: 2; y = y_hi * 2 + y_lo), z: 8, core: 2. Of those that a mesh axis runs over, the one named last changes fastest.
Arguments:
- load_windows: bfloat16 [64, 2048, 128], P('row'), may hold values from -6 to 6
- owner_id: int32 [1], replicated, may hold values from 0 to 63
- participation: bfloat16 [24576, 2048], P(('mode', 'row')), may hold values from -0.125 to 0.125
- frequency: float32 [24576], P(('mode', 'row')), may hold values from 0.05 to 1.5
- damping: float32 [24576], P(('mode', 'row')), may hold values from 0.01 to 0.3
- recovery: bfloat16 [8, 64, 24, 4, 128, 128], P('mode', 'row'), may hold values from -0.25 to 0.25
- pattern: int32 [8, 64, 24, 4], P('mode', 'row'), may hold values from 0 to 23, as said below
- plane_table: int32 [64, 8, 64, 8], P('row', 'mode'), may hold values from 0 to 63
Outputs:
- stress: float32 [64, 8, 6, 64, 128], P('row', 'mode')
- plane_range: float32 [64, 8, 64, 8], P('row', 'mode')
Inputs may be any that keep to these rules, and one draw needn't show every extreme that they name: `pattern`: the 4 entries of one row block are different mode blocks of its group.
All inputs are finite; a program needn't handle non-finite values.
Results may differ from a plain program's by a relative error of at most 0.0003.
Values may be sent and summed in bfloat16 or wider, within the bound.
No kernel may reach another device: no remote copies, remote signals or barrier semaphores. Data moves between devices by JAX's collectives and lax.ppermute only.
A program may use at most 64 MiB of HBM per device.

v0:
```python
import jax
import jax.numpy as jnp
from jax import lax
from jax.sharding import PartitionSpec as P

PLANES = 64


def spread(value, axis, source):
    kept = jnp.where(lax.axis_index(axis) == source, value, 0).astype(value.dtype)
    return lax.psum(kept, axis)


def plane_coeffs():
    index = jnp.arange(PLANES).astype(jnp.float32)
    height = (index + 0.5) / PLANES
    azimuth = index * 2.399963229728653
    radius = jnp.sqrt(1.0 - height * height)
    normal_x = radius * jnp.cos(azimuth)
    normal_y = radius * jnp.sin(azimuth)
    return jnp.stack(
        [
            normal_x * normal_x,
            normal_y * normal_y,
            height * height,
            2.0 * normal_x * normal_y,
            2.0 * normal_y * height,
            2.0 * normal_x * height,
        ],
        axis=-1,
    )


def integrate_block(loading, rates, decays):
    steps = loading.shape[-1]
    later = jnp.arange(steps)[:, None]
    earlier = jnp.arange(steps)[None, :]
    delay = (later - earlier).astype(jnp.float32)
    clipped = jnp.maximum(delay, 0.0)
    impulse = (
        rates[:, None, None]
        * jnp.exp(-decays[:, None, None] * rates[:, None, None] * clipped)
        * jnp.sin(rates[:, None, None] * (clipped + 1.0))
    )
    impulse = jnp.where(delay >= 0.0, impulse, 0.0)
    return jnp.einsum("mts,ms->mt", impulse, loading, precision=lax.Precision.HIGHEST)


def integrate(loading, rates, decays):
    return integrate_block(loading, rates, decays)


def body(load_windows, owner_id, participation, frequency, damping, recovery, pattern, plane_table):
    window = spread(load_windows[0], "row", owner_id[0])
    forces = jnp.dot(participation, window, preferred_element_type=jnp.float32)
    modal_hist = integrate(forces, frequency, damping)
    group_hist = lax.all_gather(modal_hist, "row", axis=0, tiled=True)
    coeff_blocks = recovery[0, 0]
    picks = pattern[0, 0]
    row_block = coeff_blocks.shape[2]
    mode_width = coeff_blocks.shape[3]
    steps = group_hist.shape[1]
    mode_blocks = group_hist.reshape(group_hist.shape[0] // mode_width, mode_width, steps)
    elements = plane_table.shape[2]
    block_count = 6 * elements * lax.axis_size("mode") // row_block
    chosen = mode_blocks[picks]
    summed = jnp.einsum(
        "bkrc,bkct->brt",
        coeff_blocks.astype(jnp.float32),
        chosen,
        preferred_element_type=jnp.float32,
        precision=lax.Precision.HIGHEST,
    )
    stress_rows = lax.psum_scatter(
        summed.reshape(block_count * row_block, steps), "mode", scatter_dimension=0, tiled=True
    )
    stress = stress_rows.reshape(6, elements, steps)
    chosen_planes = plane_table[0, 0]
    one_hot = (chosen_planes[..., None] == jnp.arange(PLANES)[None, None, :]).astype(jnp.float32)
    coeffs = jnp.einsum("elp,pq->elq", one_hot, plane_coeffs(), precision=lax.Precision.HIGHEST)
    normal_stress = jnp.einsum("elq,qet->elt", coeffs, stress, precision=lax.Precision.HIGHEST)
    plane_range = jnp.max(normal_stress, axis=-1) - jnp.min(normal_stress, axis=-1)
    return (stress[None, None], plane_range[None, None])


def solution(mesh):
    placed = (
        P("row", None, None),
        P(),
        P(("mode", "row"), None),
        P(("mode", "row")),
        P(("mode", "row")),
        P("mode", "row", None, None, None, None),
        P("mode", "row", None, None),
        P("row", "mode", None, None),
    )
    return jax.shard_map(
        body,
        mesh=mesh,
        in_specs=placed,
        out_specs=(P("row", "mode", None, None, None), P("row", "mode", None, None)),
        check_vma=False,
    )
```

profile of v0, /device:TPU:23, one launch (start us, length us, event | category | flops | bytes accessed | tf_op | source)
XLA Modules:
  0.0 1004.2 jit_solution(12670949599006529232)
XLA Ops:
  7.2 0.0 copy-start
  7.2 0.0 all-reduce.2.cloned.1.call-start
  8.0 0.8 select_bitcast_fusion
  8.9 0.0 all-reduce.2.cloned.1.call-update
  8.9 0.0 all-gather.2.cloned.1.call-start
  9.0 0.7 negate_multiply_fusion
  9.7 567.6 %all-reduce.2.cloned.1.call-done = bf16[2048,128]{1,0:T(8,128)(2,1)} async-done(((bf16[2048,128]{1,0:T(8,128)(2,1)}), bf16[2048,128]{1,0:T(8,128)(2,1)}) %all-reduce.2.cloned.1.call-update) | async-done | bytes 524304 | tf_op jit(solution)/shard_map/psum | solution.py:11
  577.3 1.4 fusion.26
  578.6 0.0 copy-start.1
  578.6 17.1 %fusion.2 = f32[48,1,128]{2,1,0:T(1,128)} fusion(f32[48,128,1]{1,2,0:T(1,128)S(1)} %bitcast.44, f32[128,128]{1,0:T(8,128)S(1)} %get-tuple-element.7, f32[128,128]{1,0:T(8,128)S(1)} %get-tuple-element.6, f32[48]{0:T(128)S(1)} %negate_multiply_fusion, f32[48]{0:T(128)} %param.11, pred[128,128]{1,0:T(8,128)(4,1)S(1)} %convert_compare_fusion), kind=kOutput, calls=%fused_computation.3 | convolution fusion | flops 13369344 | bytes 196992 | tf_op jit(solution)/shard_map/mts,ms->mt/dot_general | solution.py:46
  595.7 0.0 all-gather.2.cloned.1.call-update
  595.8 0.2 reduce-scatter.2.cloned.1.call-start
  596.0 0.0 copy-done.1
  596.0 0.1 copy.15
  596.1 0.1 reshape.153
  596.2 295.2 %all-gather.2.cloned.1.call-done = f32[3072,128]{1,0:T(8,128)} async-done(((f32[48,128]{1,0:T(8,128)}), f32[3072,128]{1,0:T(8,128)}) %all-gather.2.cloned.1.call-update) | async-done | bytes 1572880 | tf_op jit(solution)/shard_map/all_gather | solution.py:57
  891.5 5.0 gather_fusion
  896.5 0.0 copy-done
  896.5 0.0 copy-start.2
  896.5 7.4 fusion
  903.9 0.0 reduce-scatter.2.cloned.1.call-update
  904.1 0.0 copy-done.2
  904.1 0.5 fusion.18
  904.5 0.2 copy.16
  904.7 90.5 %reduce-scatter.2.cloned.1.call-done = f32[384,128]{1,0:T(8,128)} async-done(((f32[3072,128]{1,0:T(8,128)}), f32[384,128]{1,0:T(8,128)}) %reduce-scatter.2.cloned.1.call-update) | async-done | bytes 196624 | tf_op jit(solution)/shard_map/reduce_scatter | solution.py:74
  995.3 1.7 fusion.25
  997.0 0.7 copy.18
  (9 shorter events, 0.2 us)
Async XLA Ops:
  7.2 889.3 %copy-start = (bf16[1,1,24,4,128,128]{5,4,3,2,1,0:T(8,128)(2,1)S(1)}, bf16[1,1,24,4,128,128]{5,4,3,2,1,0:T(8,128)(2,1)}, u32[]{:S(2)}) copy-start(bf16[1,1,24,4,128,128]{5,4,3,2,1,0:T(8,128)(2,1)} %param.13) | copy-start | bytes 9437188
  7.2 570.1 %all-reduce.2.cloned.1.call-start = ((), (), s32[]{:S(2)}) async-start(), calls=%async_computation.1 | async-start | bytes 1048576 | tf_op jit(solution)/shard_map/psum | solution.py:11
  8.9 882.6 %all-gather.2.cloned.1.call-start = ((), (), s32[]{:S(2)}) async-start(), calls=%async_computation.2 | async-start | bytes 1597440 | tf_op jit(solution)/shard_map/all_gather | solution.py:57
  578.6 17.4 %copy-start.1 = (s32[1,1,24,4]{2,3,1,0:T(4,128)S(1)}, s32[1,1,24,4]{2,3,1,0:T(4,128)}, u32[]{:S(2)}) copy-start(s32[1,1,24,4]{2,3,1,0:T(4,128)} %param.14) | copy-start | bytes 1156
  595.8 399.5 %reduce-scatter.2.cloned.1.call-start = ((), (), s32[]{:S(2)}) async-start(), calls=%async_computation.3 | async-start | bytes 1769472 | tf_op jit(solution)/shard_map/reduce_scatter | solution.py:74
  896.5 7.6 copy-start.2
Sparse Core Ops, SparseCore 0:
  10.9 566.2 all-reduce.1
  595.9 295.5 all-gather.1
  904.0 91.2 reduce-scatter.1
where the time goes:
time: 1000 us
  waiting for transfers between devices  953 us (95%)
  matrix products  28 us (3%)
  between operations  14.6 us (1%)
    psum x1, waiting for transfers between devices, spread(): return lax.psum(kept, axis)  568 us
    all_gather x1, waiting for transfers between devices, body(): group_hist = lax.all_gather(modal_hist, 'row', axis=0, tiled=True)  295 us
    reduce_scatter x1, waiting for transfers between devices, body(): lax.psum_scatter(summed.reshape(block_count * row_block, steps), 'mode',...  90.5 us
  transfers between devices with their start and end apart: 3, of which 3 were waited for; matrix products, arithmetic and copies ran while one was open for 0% of the time, Pallas kernels for 0%

commit v1 on v0

v1 whole, which is shorter than its diff:
```python
import jax
import jax.numpy as jnp
from jax import lax
from jax.sharding import Mesh
from jax.sharding import PartitionSpec as P

PLANES = 64
ROW = ("z", "yl", "x")


def plane_coeffs():
    index = jnp.arange(PLANES).astype(jnp.float32)
    height = (index + 0.5) / PLANES
    azimuth = index * 2.399963229728653
    radius = jnp.sqrt(1.0 - height * height)
    normal_x = radius * jnp.cos(azimuth)
    normal_y = radius * jnp.sin(azimuth)
    return jnp.stack(
        [
            normal_x * normal_x,
            normal_y * normal_y,
            height * height,
            2.0 * normal_x * normal_y,
            2.0 * normal_y * height,
            2.0 * normal_x * height,
        ],
        axis=-1,
    )


def integrate(loading, rates, decays):
    steps = loading.shape[-1]
    later = jnp.arange(steps)[:, None]
    earlier = jnp.arange(steps)[None, :]
    delay = (later - earlier).astype(jnp.float32)
    clipped = jnp.maximum(delay, 0.0)
    impulse = (
        rates[:, None, None]
        * jnp.exp(-decays[:, None, None] * rates[:, None, None] * clipped)
        * jnp.sin(rates[:, None, None] * (clipped + 1.0))
    )
    impulse = jnp.where(delay >= 0.0, impulse, 0.0)
    return jnp.einsum("mts,ms->mt", impulse, loading, precision=lax.Precision.HIGHEST)


def gather_row(part, count):
    copies = jnp.broadcast_to(part[None], (count,) + part.shape)
    return lax.all_to_all(copies, ROW, 0, 0)


def fetch_window(windows, owner):
    channels, steps = windows.shape[1:]
    count = lax.axis_size(ROW)
    half = channels // 2
    mine = lax.dynamic_slice_in_dim(windows[0], lax.axis_index("core") * half, half, 0)
    offered = lax.all_to_all(mine.reshape(count, half // count, steps), ROW, 0, 0)
    piece = lax.dynamic_index_in_dim(offered, owner, 0, keepdims=False)
    whole_half = gather_row(piece, count).reshape(half, steps)
    return lax.all_gather(whole_half, "core", axis=0, tiled=True)


def sum_over_mode(partial):
    slabs, rows, steps = partial.shape
    by_core = partial.reshape(slabs // 2, 2, rows, steps).transpose(1, 0, 2, 3)
    both = lax.all_to_all(by_core, "core", 0, 0)
    pair = both[0] + both[1]
    parts = lax.all_to_all(pair, "yh", 0, 0)
    return parts.sum(axis=0)


def body(load_windows, owner_id, participation, frequency, damping, recovery, pattern, plane_table):
    window = fetch_window(load_windows, owner_id[0])
    forces = jnp.dot(participation, window, preferred_element_type=jnp.float32)
    modal_hist = integrate(forces, frequency, damping)
    group_hist = gather_row(modal_hist, lax.axis_size(ROW))
    coeff_blocks = recovery[0, 0]
    picks = pattern[0, 0]
    mode_width = coeff_blocks.shape[3]
    steps = modal_hist.shape[1]
    mode_blocks = group_hist.reshape(-1, mode_width, steps)
    elements = plane_table.shape[2]
    chosen = mode_blocks[picks]
    summed = jnp.einsum(
        "bkrc,bkct->brt",
        coeff_blocks.astype(jnp.float32),
        chosen,
        preferred_element_type=jnp.float32,
        precision=lax.Precision.HIGHEST,
    )
    slabs = lax.axis_size(("yh", "core"))
    stress = sum_over_mode(summed.reshape(slabs, 6 * elements, steps)).reshape(6, elements, steps)
    chosen_planes = plane_table[0, 0]
    one_hot = (chosen_planes[..., None] == jnp.arange(PLANES)[None, None, :]).astype(jnp.float32)
    coeffs = jnp.einsum("elp,pq->elq", one_hot, plane_coeffs(), precision=lax.Precision.HIGHEST)
    normal_stress = jnp.einsum("elq,qet->elt", coeffs, stress, precision=lax.Precision.HIGHEST)
    plane_range = jnp.max(normal_stress, axis=-1) - jnp.min(normal_stress, axis=-1)
    return (stress[None, None], plane_range[None, None])


def solution(mesh):
    fine = Mesh(mesh.devices.reshape(4, 2, 8, 2, 4), ("yh", "core") + ROW)
    mode = ("yh", "core")
    placed = (
        P(ROW, None, None),
        P(),
        P(mode + ROW, None),
        P(mode + ROW),
        P(mode + ROW),
        P(mode, ROW, None, None, None, None),
        P(mode, ROW, None, None),
        P(ROW, mode, None, None),
    )
    return jax.shard_map(
        body,
        mesh=fine,
        in_specs=placed,
        out_specs=(P(ROW, mode, None, None, None), P(ROW, mode, None, None)),
        check_vma=False,
    )
```

time: 1000 us -> 166 us (0.17)
  the two profiles are of different devices: /device:TPU:23 before, /device:TPU:8 now
where the time goes in v1:
time: 166 us; the launch traced here: 165 us
  waiting for transfers between devices  85.8 us (52%)
  starting transfers between devices  31.4 us (19%)
  matrix products  25.4 us (15%)
  local copies, waits for them, and re-layouts  10.7 us (6%)
  blocking collectives  7.17 us (4%)
  other arithmetic  3.56 us (2%)
    all_to_all x2, waiting for transfers between devices, gather_row(): return lax.all_to_all(copies, ROW, 0, 0)  51.8 us
    all_to_all x1, waiting for transfers between devices, sum_over_mode(): parts = lax.all_to_all(pair, 'yh', 0, 0)  21.5 us
    dot_general x1, matrix products, integrate(): jnp.einsum('mts,ms->mt', impulse, loading, precision=lax.Precision.HIGHEST)  16.5 us
    all_to_all x1, starting transfers between devices, fetch_window(): lax.all_to_all(mine.reshape(count, half // count, steps), ROW, 0, 0)  14.8 us
    all_to_all x1, waiting for transfers between devices, fetch_window(): lax.all_to_all(mine.reshape(count, half // count, steps), ROW, 0, 0)  12.4 us
    all_to_all x2, starting transfers between devices, gather_row(): return lax.all_to_all(copies, ROW, 0, 0)  10.4 us
    all_to_all x1, starting transfers between devices, sum_over_mode(): parts = lax.all_to_all(pair, 'yh', 0, 0)  6.19 us
    dot_general x1, matrix products, body(): jnp.einsum('bkrc,bkct->brt', coeff_blocks.astype(jnp.float32), chosen, pr...  5.51 us
  transfers between devices with their start and end apart: 4, of which 4 were waited for; matrix products, arithmetic and copies ran while one was open for 2% of the time, Pallas kernels for 0%

profile of v1, /device:TPU:8, one launch (start us, length us, event | category | flops | bytes accessed | tf_op | source)
XLA Modules:
  0.0 165.5 jit_solution(14221329668653708267)
XLA Ops:
  0.6 0.0 copy-start
  0.6 1.8 %constant_dynamic-slice_fusion = bf16[1,1024,128]{2,1,0:T(8,128)(2,1)} fusion(bf16[1,2048,128]{2,1,0:T(8,128)(2,1)} %param.8, s32[]{:T(128)S(6)} %select_n.22), kind=kLoop, calls=%fused_computation.40 | loop fusion | bytes 524292 | tf_op jit(solution)/shard_map/dynamic_slice | solution.py:55
  2.5 14.8 %all-to-all-start = ((bf16[64,16,128]{2,1,0:T(8,128)(2,1)}), bf16[64,16,128]{2,1,0:T(8,128)(2,1)S(1)}, u32[]{:S(2)}, u32[]{:S(2)}) async-start(bf16[64,16,128]{2,1,0:T(8,128)(2,1)} %bitcast), calls=%async_computation | async-start | bytes 524288 | tf_op jit(solution)/shard_map/all_to_all | solution.py:56
  17.9 12.4 %all-to-all-done = bf16[64,16,128]{2,1,0:T(8,128)(2,1)S(1)} async-done(((bf16[64,16,128]{2,1,0:T(8,128)(2,1)}), bf16[64,16,128]{2,1,0:T(8,128)(2,1)S(1)}, u32[]{:S(2)}, u32[]{:S(2)}) %all-to-all-start) | async-done | bytes 262176 | tf_op jit(solution)/shard_map/all_to_all | solution.py:56
  30.3 0.7 broadcast_in_dim.17
  31.1 4.9 %all-to-all-start.1 = ((bf16[64,16,128]{2,1,0:T(8,128)(2,1)}), bf16[64,16,128]{2,1,0:T(8,128)(2,1)S(1)}, u32[]{:S(2)}, u32[]{:S(2)}) async-start(bf16[64,16,128]{2,1,0:T(8,128)(2,1)} %broadcast_in_dim.17), calls=%async_computation.1 | async-start | bytes 524288 | tf_op jit(solution)/shard_map/all_to_all | solution.py:48
  36.0 1.2 negate_multiply_fusion
  37.2 11.6 %all-to-all-done.1 = bf16[64,16,128]{2,1,0:T(8,128)(2,1)S(1)} async-done(((bf16[64,16,128]{2,1,0:T(8,128)(2,1)}), bf16[64,16,128]{2,1,0:T(8,128)(2,1)S(1)}, u32[]{:S(2)}, u32[]{:S(2)}) %all-to-all-start.1) | async-done | bytes 262176 | tf_op jit(solution)/shard_map/all_to_all | solution.py:48
  48.8 2.2 %all_gather.3 = bf16[2048,128]{1,0:T(8,128)(2,1)S(1)} all-gather(bf16[1024,128]{1,0:T(8,128)(2,1)S(1)} %bitcast.53), channel_id=1, replica_groups=mesh['yh'=4,'core'=2,'z'=8,'yl'=2,'x'=4] {'core'}, dimensions={0}, use_global_device_ids=true | all-gather | bytes 786432 | tf_op jit(solution)/shard_map/all_gather | solution.py:59
  51.0 1.1 fusion.27
  52.2 16.5 %fusion.2 = f32[48,1,128]{2,1,0:T(1,128)S(1)} fusion(f32[48,128,1]{1,2,0:T(1,128)S(1)} %bitcast.54, f32[128,128]{1,0:T(8,128)S(1)} %get-tuple-element.7, f32[128,128]{1,0:T(8,128)S(1)} %get-tuple-element.6, f32[48]{0:T(128)} %negate_multiply_fusion, f32[48]{0:T(128)} %param.11, pred[128,128]{1,0:T(8,128)(4,1)S(1)} %convert_compare_fusion), kind=kOutput, calls=%fused_computation.3 | convolution fusion | flops 13369344 | bytes 196992 | tf_op jit(solution)/shard_map/mts,ms->mt/dot_general | solution.py:43
  68.7 0.0 copy-start.2
  68.7 1.3 broadcast_in_dim.18
  69.9 5.5 %all-to-all-start.2 = ((f32[64,48,128]{2,1,0:T(8,128)}), f32[64,48,128]{2,1,0:T(8,128)}, u32[]{:S(2)}, u32[]{:S(2)}) async-start(f32[64,48,128]{2,1,0:T(8,128)} %broadcast_in_dim.18), calls=%async_computation.2 | async-start | bytes 3145728 | tf_op jit(solution)/shard_map/all_to_all | solution.py:48
  75.5 0.0 copy-done.2
  75.5 0.1 copy.15
  75.6 0.1 reshape.158
  75.7 40.2 %all-to-all-done.2 = f32[64,48,128]{2,1,0:T(8,128)} async-done(((f32[64,48,128]{2,1,0:T(8,128)}), f32[64,48,128]{2,1,0:T(8,128)}, u32[]{:S(2)}, u32[]{:S(2)}) %all-to-all-start.2) | async-done | bytes 1572896 | tf_op jit(solution)/shard_map/all_to_all | solution.py:48
  115.9 5.0 %gather_fusion = f32[96,128,128]{2,1,0:T(8,128)} fusion(f32[24,128,128]{2,1,0:T(8,128)} %bitcast.9, s32[1024]{0:T(1024)S(1)} %pad_clamp_fusion), kind=kCustom, calls=%fused_computation | custom fusion | bytes 12583296 | tf_op jit(solution)/shard_map/gather | solution.py:82
  120.9 0.0 copy-done
  120.9 5.5 %fusion = f32[24,128,128,1]{1,2,3,0:T(8,128)S(1)} fusion(f32[24,4,128,128]{3,2,1,0:T(8,128)} %bitcast.48, bf16[1,1,24,4,128,128]{5,4,3,2,1,0:T(8,128)(2,1)S(1)} %copy-done), kind=kOutput, calls=%fused_computation.1 | convolution fusion | flops 2415919104 | bytes 11010048 | tf_op jit(solution)/shard_map/bkrc,bkct->brt/dot_general | solution.py:83
  126.4 0.1 copy.28
  126.5 0.0 copy-start.3
  126.5 5.0 %all_to_all.25 = f32[2,4,384,128]{3,2,1,0:T(8,128)S(1)} all-to-all(f32[2,4,384,128]{3,2,1,0:T(8,128)S(1)} %bitcast.49), channel_id=1, replica_groups=mesh['yh'=4,'core'=2,'z'=8,'yl'=2,'x'=4] {'core'}, dimensions={0} | all-to-all | bytes 3145728 | tf_op jit(solution)/shard_map/all_to_all | solution.py:65
  131.5 1.0 fusion.16
  132.5 6.2 %all-to-all-start.4 = ((f32[4,384,128]{2,1,0:T(8,128)}), f32[4,384,128]{2,1,0:T(8,128)}, u32[]{:S(2)}, u32[]{:S(2)}) async-start(f32[4,384,128]{2,1,0:T(8,128)} %fusion.16), calls=%async_computation.4 | async-start | bytes 1572864 | tf_op jit(solution)/shard_map/all_to_all | solution.py:67
  138.9 0.0 copy-done.3
  138.9 0.5 fusion.19
  139.4 0.9 copy.17
  140.2 21.5 %all-to-all-done.4 = f32[4,384,128]{2,1,0:T(8,128)} async-done(((f32[4,384,128]{2,1,0:T(8,128)}), f32[4,384,128]{2,1,0:T(8,128)}, u32[]{:S(2)}, u32[]{:S(2)}) %all-to-all-start.4) | async-done | bytes 786464 | tf_op jit(solution)/shard_map/all_to_all | solution.py:67
  161.8 1.2 reduce_sum.9
  163.0 0.0 copy-start.1
  163.0 1.8 %fusion.26 = (f32[64,8]{1,0:T(8,128)S(1)}, f32[64,8]{1,0:T(8,128)S(1)}) fusion(f32[64,8,6]{2,1,0:T(8,128)} %copy.17, f32[6,64,128]{2,1,0:T(8,128)S(1)} %bitcast.51), kind=kOutput, calls=%fused_computation.48 | convolution fusion | flops 4848640 | bytes 212992 | tf_op jit(solution)/shard_map/elq,qet->elt/dot_general | solution.py:95
  164.8 0.7 copy.19
  165.5 0.0 copy-done.1
  (10 shorter events, 0.2 us)
Async XLA Ops:
  0.6 120.3 %copy-start = (bf16[1,1,24,4,128,128]{5,4,3,2,1,0:T(8,128)(2,1)S(1)}, bf16[1,1,24,4,128,128]{5,4,3,2,1,0:T(8,128)(2,1)}, u32[]{:S(2)}) copy-start(bf16[1,1,24,4,128,128]{5,4,3,2,1,0:T(8,128)(2,1)} %param.13) | copy-start | bytes 9437188
  2.5 27.9 %all-to-all-start = ((bf16[64,16,128]{2,1,0:T(8,128)(2,1)}), bf16[64,16,128]{2,1,0:T(8,128)(2,1)S(1)}, u32[]{:S(2)}, u32[]{:S(2)}) async-start(bf16[64,16,128]{2,1,0:T(8,128)(2,1)} %bitcast), calls=%async_computation | async-start | bytes 524288 | tf_op jit(solution)/shard_map/all_to_all | solution.py:56
  31.1 17.8 %all-to-all-start.1 = ((bf16[64,16,128]{2,1,0:T(8,128)(2,1)}), bf16[64,16,128]{2,1,0:T(8,128)(2,1)S(1)}, u32[]{:S(2)}, u32[]{:S(2)}) async-start(bf16[64,16,128]{2,1,0:T(8,128)(2,1)} %broadcast_in_dim.17), calls=%async_computation.1 | async-start | bytes 524288 | tf_op jit(solution)/shard_map/all_to_all | solution.py:48
  68.7 6.8 %copy-start.2 = (s32[1,1,24,4]{2,3,1,0:T(4,128)S(1)}, s32[1,1,24,4]{2,3,1,0:T(4,128)}, u32[]{:S(2)}) copy-start(s32[1,1,24,4]{2,3,1,0:T(4,128)} %param.14) | copy-start | bytes 1156
  69.9 45.9 %all-to-all-start.2 = ((f32[64,48,128]{2,1,0:T(8,128)}), f32[64,48,128]{2,1,0:T(8,128)}, u32[]{:S(2)}, u32[]{:S(2)}) async-start(f32[64,48,128]{2,1,0:T(8,128)} %broadcast_in_dim.18), calls=%async_computation.2 | async-start | bytes 3145728 | tf_op jit(solution)/shard_map/all_to_all | solution.py:48
  126.5 12.4 %copy-start.3 = (s32[1,1,64,8]{2,3,1,0:T(8,128)S(1)}, s32[1,1,64,8]{2,3,1,0:T(8,128)}, u32[]{:S(2)}) copy-start(s32[1,1,64,8]{2,3,1,0:T(8,128)} %param.15) | copy-start | bytes 6148
  132.5 29.3 %all-to-all-start.4 = ((f32[4,384,128]{2,1,0:T(8,128)}), f32[4,384,128]{2,1,0:T(8,128)}, u32[]{:S(2)}, u32[]{:S(2)}) async-start(f32[4,384,128]{2,1,0:T(8,128)} %fusion.16), calls=%async_computation.4 | async-start | bytes 1572864 | tf_op jit(solution)/shard_map/all_to_all | solution.py:67
  163.0 2.5 %copy-start.1 = (f32[384,128]{1,0:T(8,128)}, f32[384,128]{1,0:T(8,128)S(1)}, u32[]{:S(2)}) copy-start(f32[384,128]{1,0:T(8,128)S(1)} %reduce_sum.9) | copy-start | bytes 589828

commit v2 on v1

v2 whole, which is shorter than its diff:
```python
import jax
import jax.numpy as jnp
from jax import lax
from jax.experimental import pallas as pl
from jax.experimental.pallas import tpu as pltpu
from jax.sharding import Mesh
from jax.sharding import PartitionSpec as P

PLANES = 64
ROW = ("z", "yl", "x")
CODE_ROWS = 8
CHUNKS = 4


def plane_coeffs():
    index = jnp.arange(PLANES).astype(jnp.float32)
    height = (index + 0.5) / PLANES
    azimuth = index * 2.399963229728653
    radius = jnp.sqrt(1.0 - height * height)
    normal_x = radius * jnp.cos(azimuth)
    normal_y = radius * jnp.sin(azimuth)
    return jnp.stack(
        [
            normal_x * normal_x,
            normal_y * normal_y,
            height * height,
            2.0 * normal_x * normal_y,
            2.0 * normal_y * height,
            2.0 * normal_x * height,
        ],
        axis=-1,
    )


def mode_table(rates, decays, steps):
    doublings = steps.bit_length() - 1
    shifts = 2.0 ** jnp.arange(doublings, dtype=jnp.float32)
    angle = rates[:, None] * shifts
    shrink = jnp.exp(-decays[:, None] * rates[:, None] * shifts)
    last = jnp.stack([rates * jnp.sin(rates), rates * jnp.cos(rates)], axis=-1)
    return jnp.concatenate([shrink * jnp.cos(angle), shrink * jnp.sin(angle), last], axis=-1)


def code_scale(code):
    return jnp.exp2(code * (1.0 / 32.0) - 15.0)


def quantize(values):
    largest = jnp.max(jnp.abs(values), axis=-1, keepdims=True)
    code = jnp.ceil(jnp.log2(jnp.maximum(largest, 1e-30)) * 32.0)
    inverse = jnp.exp2(15.0 - code * (1.0 / 32.0))
    whole = jnp.clip(jnp.round(values * inverse), -32767.0, 32767.0).astype(jnp.int32)
    return whole, code


def as_row(column):
    n = column.shape[0]
    at = lax.broadcasted_iota(jnp.int32, (n, 128), 0) == lax.broadcasted_iota(jnp.int32, (n, 128), 1)
    return jnp.sum(jnp.where(at, column, 0.0), axis=0, keepdims=True)


def history_kernel(window_ref, part_ref, table_ref, out_ref):
    forces = jnp.dot(part_ref[...], window_ref[...], preferred_element_type=jnp.float32)
    modes, steps = forces.shape
    doublings = steps.bit_length() - 1
    table = table_ref[...]
    lane = lax.broadcasted_iota(jnp.int32, forces.shape, 1)
    re, im = forces, jnp.zeros_like(forces)
    for d in range(doublings):
        shift = 1 << d
        p_re, p_im = table[:, d : d + 1], table[:, doublings + d : doublings + d + 1]
        keep = lane >= shift
        old_re = jnp.where(keep, pltpu.roll(re, shift, 1), 0.0)
        if d == 0:
            re, im = re + p_re * old_re, p_im * old_re
            continue
        old_im = jnp.where(keep, pltpu.roll(im, shift, 1), 0.0)
        re, im = re + p_re * old_re - p_im * old_im, im + p_re * old_im + p_im * old_re
    hist = table[:, 2 * doublings : 2 * doublings + 1] * re + table[:, 2 * doublings + 1 : 2 * doublings + 2] * im
    whole, code = quantize(hist)
    codes = jnp.broadcast_to(as_row(code), (CODE_ROWS, 128)).astype(jnp.int32)
    block = jnp.concatenate([whole, codes], axis=0).astype(jnp.int16)
    for i in range(out_ref.shape[0]):
        out_ref[i] = block


def make_history(window, participation, table, count):
    modes, channels = participation.shape
    steps = window.shape[1]
    return pl.pallas_call(
        history_kernel,
        out_shape=jax.ShapeDtypeStruct((count, modes + CODE_ROWS, steps), jnp.int16),
        in_specs=[pl.BlockSpec(memory_space=pltpu.VMEM)] * 3,
        out_specs=pl.BlockSpec(memory_space=pltpu.VMEM),
        compiler_params=pltpu.CompilerParams(vmem_limit_bytes=16 << 20),
        cost_estimate=pl.CostEstimate(
            flops=2 * modes * channels * steps, bytes_accessed=2 * (channels * (modes + steps)), transcendentals=0
        ),
        name="history",
    )(window, participation, table)


def recover_kernel(picks_ref, hist_ref, far_ref, out_ref, split_ref, coeff_ref, sems):
    chunks = sems.shape[0]
    per = coeff_ref.shape[0] // chunks
    fetches = [
        pltpu.make_async_copy(far_ref.at[pl.ds(i * per, per)], coeff_ref.at[pl.ds(i * per, per)], sems.at[i])
        for i in range(chunks)
    ]
    for fetch in fetches:
        fetch.start()
    sources, rows, steps = hist_ref.shape
    modes = rows - CODE_ROWS
    sub = lax.broadcasted_iota(jnp.int32, (8, 128), 0)
    tiles = []
    for base in range(0, sources, 8):
        tile = jnp.zeros((8, 128), jnp.int32)
        for i in range(8):
            codes = hist_ref[base + i, modes : modes + CODE_ROWS, :].astype(jnp.int32)[:8]
            tile = jnp.where(sub == i, codes, tile)
        tiles.append(tile)
    scales = code_scale(jnp.concatenate(tiles, axis=0).astype(jnp.float32))
    scales = jnp.concatenate([scales, jnp.zeros((128 - sources, 128), jnp.float32)], axis=0).T
    for s in range(sources):
        value = hist_ref[s, :modes, :].astype(jnp.int32).astype(jnp.float32) * scales[:modes, s : s + 1]
        high = value.astype(jnp.bfloat16)
        low = (value - high.astype(jnp.float32)).astype(jnp.bfloat16)
        split_ref[s * modes : (s + 1) * modes, :steps] = high
        split_ref[s * modes : (s + 1) * modes, steps:] = low
    blocks, picked, height, width = coeff_ref.shape
    slab = blocks // (2 * out_ref.shape[1])
    for b in range(blocks):
        if b % per == 0:
            fetches[b // per].wait()
        left = jnp.concatenate([coeff_ref[b, k] for k in range(picked)], axis=1)
        right = jnp.concatenate(
            [split_ref[pl.ds(pl.multiple_of(picks_ref[b, k] * width, width), width), :] for k in range(picked)], axis=0
        )
        both = jnp.dot(left, right, preferred_element_type=jnp.float32)
        owner = b // slab
        out_ref[owner % 2, owner // 2, (b % slab) * height : (b % slab + 1) * height, :] = both[:, :steps] + both[:, steps:]


def recover(hist, coeff_blocks, picks, groups):
    sources, rows, steps = hist.shape
    blocks, picked, height, width = coeff_blocks.shape
    return pl.pallas_call(
        recover_kernel,
        out_shape=jax.ShapeDtypeStruct((2, groups // 2, blocks // groups * height, steps), jnp.float32),
        in_specs=[
            pl.BlockSpec(memory_space=pltpu.SMEM),
            pl.BlockSpec(memory_space=pltpu.VMEM),
            pl.BlockSpec(memory_space=pltpu.HBM),
        ],
        out_specs=pl.BlockSpec(memory_space=pltpu.VMEM),
        scratch_shapes=[
            pltpu.VMEM((sources * (rows - CODE_ROWS), 2 * steps), jnp.bfloat16),
            pltpu.VMEM(coeff_blocks.shape, jnp.bfloat16),
            pltpu.SemaphoreType.DMA((CHUNKS,)),
        ],
        compiler_params=pltpu.CompilerParams(vmem_limit_bytes=50 << 20),
        cost_estimate=pl.CostEstimate(
            flops=4 * blocks * picked * height * width * steps,
            bytes_accessed=2 * blocks * picked * height * width,
            transcendentals=0,
        ),
        name="recover",
    )(picks, hist, coeff_blocks)


def range_kernel(parts_ref, coeff_ref, stress_ref, range_ref):
    total = parts_ref[0]
    for i in range(1, parts_ref.shape[0]):
        total = total + parts_ref[i]
    components, elements, steps = stress_ref.shape
    stress = total.reshape(components, elements, steps)
    stress_ref[...] = stress
    looked = range_ref.shape[0]
    lane = lax.broadcasted_iota(jnp.int32, (elements, 128), 1)
    coeffs = coeff_ref[...]
    result = jnp.zeros((elements, 128), jnp.float32)
    for p in range(looked):
        normal = coeffs[:, p * components : p * components + 1] * stress[0]
        for q in range(1, components):
            at = p * components + q
            normal = normal + coeffs[:, at : at + 1] * stress[q]
        spread = jnp.max(normal, axis=-1, keepdims=True) - jnp.min(normal, axis=-1, keepdims=True)
        result = jnp.where(lane == p, spread, result)
    range_ref[...] = result.T[:looked, :]


def finish(parts, coeffs, looked):
    groups, rows, steps = parts.shape
    elements = coeffs.shape[0]
    stress, ranges = pl.pallas_call(
        range_kernel,
        out_shape=(
            jax.ShapeDtypeStruct((rows // elements, elements, steps), jnp.float32),
            jax.ShapeDtypeStruct((looked, elements), jnp.float32),
        ),
        in_specs=[pl.BlockSpec(memory_space=pltpu.VMEM)] * 2,
        out_specs=(pl.BlockSpec(memory_space=pltpu.VMEM),) * 2,
        compiler_params=pltpu.CompilerParams(vmem_limit_bytes=8 << 20),
        name="ranges",
    )(parts, coeffs)
    return stress, ranges.T


def gather_row(part, count):
    copies = jnp.broadcast_to(part[None], (count,) + part.shape)
    return lax.all_to_all(copies, ROW, 0, 0)


def fetch_window(windows, owner):
    channels, steps = windows.shape[1:]
    count = lax.axis_size(ROW)
    half = channels // 2
    mine = lax.dynamic_slice_in_dim(windows[0], lax.axis_index("core") * half, half, 0)
    offered = lax.all_to_all(mine.reshape(count, half // count, steps), ROW, 0, 0)
    piece = lax.dynamic_index_in_dim(offered, owner, 0, keepdims=False)
    whole_half = gather_row(piece, count).reshape(half, steps)
    return lax.all_gather(whole_half, "core", axis=0, tiled=True)


def sum_over_mode(by_core):
    both = lax.all_to_all(by_core, "core", 0, 0)
    pair = both[0] + both[1]
    return lax.all_to_all(pair, "yh", 0, 0)


def body(load_windows, owner_id, participation, frequency, damping, recovery, pattern, plane_table):
    steps = load_windows.shape[2]
    chosen_planes = plane_table[0, 0]
    elements, looked = chosen_planes.shape
    one_hot = (chosen_planes[..., None] == jnp.arange(PLANES)[None, None, :]).astype(jnp.float32)
    coeffs = jnp.einsum("elp,pq->elq", one_hot, plane_coeffs(), precision=lax.Precision.HIGHEST)
    coeffs = coeffs.reshape(elements, looked * 6)
    table = mode_table(frequency, damping, steps)
    window = fetch_window(load_windows, owner_id[0])
    copies = make_history(window, participation, table, lax.axis_size(ROW))
    hist = lax.all_to_all(copies, ROW, 0, 0)
    partial = recover(hist, recovery[0, 0], pattern[0, 0], lax.axis_size(("yh", "core")))
    parts = sum_over_mode(partial)
    stress, plane_range = finish(parts, coeffs, looked)
    return (stress[None, None], plane_range[None, None])


def solution(mesh):
    fine = Mesh(mesh.devices.reshape(4, 2, 8, 2, 4), ("yh", "core") + ROW)
    mode = ("yh", "core")
    placed = (
        P(ROW, None, None),
        P(),
        P(mode + ROW, None),
        P(mode + ROW),
        P(mode + ROW),
        P(mode, ROW, None, None, None, None),
        P(mode, ROW, None, None),
        P(ROW, mode, None, None),
    )
    return jax.shard_map(
        body,
        mesh=fine,
        in_specs=placed,
        out_specs=(P(ROW, mode, None, None, None), P(ROW, mode, None, None)),
        check_vma=False,
    )
```

time: 166 us -> 125 us (0.75)
  matrix products: 25.4 us -> 0.46 us
  waiting for transfers between devices: 85.8 us -> 73.2 us
  local copies, waits for them, and re-layouts: 10.7 us -> 2.77 us
  Pallas kernels: 0 us -> 7.15 us
  other arithmetic: 3.56 us -> 1.27 us
    all_to_all x2 -> x1, waiting for transfers between devices: 51.8 us -> 12.6 us  [gather_row(): return lax.all_to_all(copies, ROW, 0, 0)]
    all_to_all x1 -> x2, waiting for transfers between devices: 21.5 us -> 48.2 us  [the longest x1 26.5 us: body(): hist = lax.all_to_all(copies, ROW, 0, 0)]
    dot_general x4 -> x0, matrix products: 24.9 us -> none  [the longest x1 16.5 us: integrate(): jnp.einsum('mts,ms->mt', impulse, loading, precision=lax.Precision.HIGHEST)]
    pallas_call x0 -> x3, Pallas kernels: none -> 7.15 us  [the longest x1 3.45 us: recover(): pl.pallas_call(recover_kernel, out_shape=jax.ShapeDtypeStruct((2, groups...]
    all_to_all x2 -> x1, starting transfers between devices: 10.4 us -> 4.92 us  [gather_row(): return lax.all_to_all(copies, ROW, 0, 0)]
    gather x1 -> x0, local copies, waits for them, and re-layouts: 5.03 us -> none  [body(): chosen = mode_blocks[picks]]
    all_to_all x1 -> x2, starting transfers between devices: 6.19 us -> 11.1 us  [the longest x1 6.18 us: sum_over_mode(): return lax.all_to_all(pair, 'yh', 0, 0)]
  transfers between devices with their start and end apart: 4 -> 4, of which waited for: 4 -> 4; matrix products, arithmetic and copies ran while one was open for 2% -> 1% of each run, Pallas kernels for 0% -> 0%
where the time goes in v2:
time: 125 us; the launch traced here: 124 us
  waiting for transfers between devices  73.2 us (59%)
  starting transfers between devices  30.8 us (25%)
  blocking collectives  7.17 us (6%)
  Pallas kernels  7.15 us (6%)
  local copies, waits for them, and re-layouts  2.77 us (2%)
  between operations  1.42 us (1%)
  other arithmetic  1.27 us (1%)
    all_to_all x1, waiting for transfers between devices, body(): hist = lax.all_to_all(copies, ROW, 0, 0)  26.5 us
    all_to_all x1, waiting for transfers between devices, sum_over_mode(): return lax.all_to_all(pair, 'yh', 0, 0)  21.7 us
    all_to_all x1, starting transfers between devices, fetch_window(): lax.all_to_all(mine.reshape(count, half // count, steps), ROW, 0, 0)  14.8 us
    all_to_all x1, waiting for transfers between devices, gather_row(): return lax.all_to_all(copies, ROW, 0, 0)  12.6 us
    all_to_all x1, waiting for transfers between devices, fetch_window(): lax.all_to_all(mine.reshape(count, half // count, steps), ROW, 0, 0)  12.4 us
    all_to_all x1, starting transfers between devices, sum_over_mode(): return lax.all_to_all(pair, 'yh', 0, 0)  6.18 us
    all_to_all x1, blocking collectives, sum_over_mode(): both = lax.all_to_all(by_core, 'core', 0, 0)  5 us
    all_to_all x1, starting transfers between devices, gather_row(): return lax.all_to_all(copies, ROW, 0, 0)  4.92 us
  transfers between devices with their start and end apart: 4, of which 4 were waited for; matrix products, arithmetic and copies ran while one was open for 1% of the time, Pallas kernels for 0%

profile of v2, /device:TPU:8, one launch (start us, length us, event | category | flops | bytes accessed | tf_op | source)
XLA Modules:
  0.0 124.2 jit_solution(14218851627766086703)
XLA Ops:
  0.6 0.0 copy-start
  0.6 0.0 copy-start.3
  0.7 0.0 copy-start.4
  0.7 0.0 copy-start.1
  0.7 1.0 copy-done
  1.7 0.7 constant_dynamic-slice_fusion
  2.4 14.8 %all-to-all-start = ((bf16[64,16,128]{2,1,0:T(8,128)(2,1)}), bf16[64,16,128]{2,1,0:T(8,128)(2,1)S(1)}, u32[]{:S(2)}, u32[]{:S(2)}) async-start(bf16[64,16,128]{2,1,0:T(8,128)(2,1)} %bitcast.1), calls=%async_computation | async-start | bytes 524288 | tf_op jit(solution)/shard_map/all_to_all | solution.py:219
  17.9 12.4 %all-to-all-done = bf16[64,16,128]{2,1,0:T(8,128)(2,1)S(1)} async-done(((bf16[64,16,128]{2,1,0:T(8,128)(2,1)}), bf16[64,16,128]{2,1,0:T(8,128)(2,1)S(1)}, u32[]{:S(2)}, u32[]{:S(2)}) %all-to-all-start) | async-done | bytes 262176 | tf_op jit(solution)/shard_map/all_to_all | solution.py:219
  30.3 0.7 broadcast_in_dim.9
  31.0 4.9 %all-to-all-start.1 = ((bf16[64,16,128]{2,1,0:T(8,128)(2,1)}), bf16[64,16,128]{2,1,0:T(8,128)(2,1)S(1)}, u32[]{:S(2)}, u32[]{:S(2)}) async-start(bf16[64,16,128]{2,1,0:T(8,128)(2,1)} %broadcast_in_dim.9), calls=%async_computation.1 | async-start | bytes 524288 | tf_op jit(solution)/shard_map/all_to_all | solution.py:211
  35.9 0.0 copy-done.3
  35.9 0.0 copy-done.4
  36.0 0.1 fusion.3
  36.1 0.1 copy.18.table_ref
  36.2 12.6 %all-to-all-done.1 = bf16[64,16,128]{2,1,0:T(8,128)(2,1)S(1)} async-done(((bf16[64,16,128]{2,1,0:T(8,128)(2,1)}), bf16[64,16,128]{2,1,0:T(8,128)(2,1)S(1)}, u32[]{:S(2)}, u32[]{:S(2)}) %all-to-all-start.1) | async-done | bytes 262176 | tf_op jit(solution)/shard_map/all_to_all | solution.py:211
  48.8 2.2 %all_gather.3.window_ref = bf16[2048,128]{1,0:T(8,128)(2,1)S(1)} all-gather(bf16[1024,128]{1,0:T(8,128)(2,1)S(1)} %bitcast.27), channel_id=1, replica_groups=mesh['yh'=4,'core'=2,'z'=8,'yl'=2,'x'=4] {'core'}, dimensions={0}, use_global_device_ids=true | all-gather | bytes 786432 | tf_op jit(solution)/shard_map/all_gather | solution.py:222
  50.9 0.0 copy-done.1
  50.9 0.0 copy-start.2
  50.9 1.9 %history.1 = s16[64,56,128]{2,1,0:T(8,128)(2,1)} custom-call(bf16[2048,128]{1,0:T(8,128)(2,1)S(1)} %all_gather.3.window_ref, bf16[48,2048]{1,0:T(8,128)(2,1)S(1)} %copy-done.1, f32[48,16]{1,0:T(8,128)S(1)} %copy.18.table_ref), custom_call_target="tpu_custom_call" | custom-call | flops 25165824 | bytes 720896 | tf_op jit(solution)/shard_map/history/pallas_call | solution.py:90
  52.8 4.9 %all-to-all-start.2 = ((s16[64,56,128]{2,1,0:T(8,128)(2,1)}), s16[64,56,128]{2,1,0:T(8,128)(2,1)S(1)}, u32[]{:S(2)}, u32[]{:S(2)}) async-start(s16[64,56,128]{2,1,0:T(8,128)(2,1)} %history.1), calls=%async_computation.2 | async-start | bytes 1835008 | tf_op jit(solution)/shard_map/all_to_all | solution.py:241
  57.7 0.0 copy-done.2
  57.7 0.1 copy.19.picks_ref
  57.8 26.5 %all-to-all-done.2.hist_ref = s16[64,56,128]{2,1,0:T(8,128)(2,1)S(1)} async-done(((s16[64,56,128]{2,1,0:T(8,128)(2,1)}), s16[64,56,128]{2,1,0:T(8,128)(2,1)S(1)}, u32[]{:S(2)}, u32[]{:S(2)}) %all-to-all-start.2) | async-done | bytes 917536 | tf_op jit(solution)/shard_map/all_to_all | solution.py:241
  84.3 3.5 %recover.1 = f32[2,4,384,128]{3,2,1,0:T(8,128)S(1)} custom-call(s32[24,4]{1,0:T(8,128)S(1)} %copy.19.picks_ref, s16[64,56,128]{2,1,0:T(8,128)(2,1)S(1)} %all-to-all-done.2.hist_ref, bf16[24,4,128,128]{3,2,1,0:T(8,128)(2,1)} %bitcast.26), custom_call_target="tpu_custom_call" | custom-call | flops 805306368 | bytes 3145728 | tf_op jit(solution)/shard_map/recover/pallas_call | solution.py:147
  87.8 5.0 %all_to_all.25 = f32[2,4,384,128]{3,2,1,0:T(8,128)S(1)} all-to-all(f32[2,4,384,128]{3,2,1,0:T(8,128)S(1)} %recover.1), channel_id=1, replica_groups=mesh['yh'=4,'core'=2,'z'=8,'yl'=2,'x'=4] {'core'}, dimensions={0} | all-to-all | bytes 3145728 | tf_op jit(solution)/shard_map/all_to_all | solution.py:226
  92.8 0.0 copy-start.5
  92.8 1.0 fusion
  93.7 6.2 %all-to-all-start.4 = ((f32[4,384,128]{2,1,0:T(8,128)}), f32[4,384,128]{2,1,0:T(8,128)S(1)}, u32[]{:S(2)}, u32[]{:S(2)}) async-start(f32[4,384,128]{2,1,0:T(8,128)} %fusion), calls=%async_computation.4 | async-start | bytes 1572864 | tf_op jit(solution)/shard_map/all_to_all | solution.py:228
  100.1 0.0 copy-done.5
  100.1 0.5 fusion.1
  100.6 0.1 copy.20.coeff_ref
  100.7 21.7 %all-to-all-done.4.parts_ref = f32[4,384,128]{2,1,0:T(8,128)S(1)} async-done(((f32[4,384,128]{2,1,0:T(8,128)}), f32[4,384,128]{2,1,0:T(8,128)S(1)}, u32[]{:S(2)}, u32[]{:S(2)}) %all-to-all-start.4) | async-done | bytes 786464 | tf_op jit(solution)/shard_map/all_to_all | solution.py:228
  122.3 1.9 %ranges.1 = (f32[6,64,128]{2,1,0:T(8,128)}, f32[8,64]{1,0:T(8,128)}) custom-call(f32[4,384,128]{2,1,0:T(8,128)S(1)} %all-to-all-done.4.parts_ref, f32[64,48]{1,0:T(8,128)S(1)} %copy.20.coeff_ref), custom_call_target="tpu_custom_call" | custom-call | tf_op jit(solution)/shard_map/ranges/pallas_call | solution.py:195
  (9 shorter events, 0.2 us)
Async XLA Ops:
  0.6 1.0 copy-start
  0.6 35.3 %copy-start.3 = (f32[48]{0:T(128)S(1)}, f32[48]{0:T(128)}, u32[]{:S(2)}) copy-start(f32[48]{0:T(128)} %param.11) | copy-start | bytes 580
  0.7 35.3 %copy-start.4 = (f32[48]{0:T(128)S(1)}, f32[48]{0:T(128)}, u32[]{:S(2)}) copy-start(f32[48]{0:T(128)} %param.12) | copy-start | bytes 580
  0.7 50.3 %copy-start.1 = (bf16[48,2048]{1,0:T(8,128)(2,1)S(1)}, bf16[48,2048]{1,0:T(8,128)(2,1)}, u32[]{:S(2)}) copy-start(bf16[48,2048]{1,0:T(8,128)(2,1)} %part_ref.1) | copy-start | bytes 589828
  2.4 27.9 %all-to-all-start = ((bf16[64,16,128]{2,1,0:T(8,128)(2,1)}), bf16[64,16,128]{2,1,0:T(8,128)(2,1)S(1)}, u32[]{:S(2)}, u32[]{:S(2)}) async-start(bf16[64,16,128]{2,1,0:T(8,128)(2,1)} %bitcast.1), calls=%async_computation | async-start | bytes 524288 | tf_op jit(solution)/shard_map/all_to_all | solution.py:219
  31.0 17.8 %all-to-all-start.1 = ((bf16[64,16,128]{2,1,0:T(8,128)(2,1)}), bf16[64,16,128]{2,1,0:T(8,128)(2,1)S(1)}, u32[]{:S(2)}, u32[]{:S(2)}) async-start(bf16[64,16,128]{2,1,0:T(8,128)(2,1)} %broadcast_in_dim.9), calls=%async_computation.1 | async-start | bytes 524288 | tf_op jit(solution)/shard_map/all_to_all | solution.py:211
  50.9 6.8 %copy-start.2 = (s32[1,1,24,4]{2,3,1,0:T(4,128)S(1)}, s32[1,1,24,4]{2,3,1,0:T(4,128)}, u32[]{:S(2)}) copy-start(s32[1,1,24,4]{2,3,1,0:T(4,128)} %param.14) | copy-start | bytes 1156
  52.8 31.5 %all-to-all-start.2 = ((s16[64,56,128]{2,1,0:T(8,128)(2,1)}), s16[64,56,128]{2,1,0:T(8,128)(2,1)S(1)}, u32[]{:S(2)}, u32[]{:S(2)}) async-start(s16[64,56,128]{2,1,0:T(8,128)(2,1)} %history.1), calls=%async_computation.2 | async-start | bytes 1835008 | tf_op jit(solution)/shard_map/all_to_all | solution.py:241
  92.8 7.3 %copy-start.5 = (s32[1,1,64,8]{2,3,1,0:T(8,128)S(1)}, s32[1,1,64,8]{2,3,1,0:T(8,128)}, u32[]{:S(2)}) copy-start(s32[1,1,64,8]{2,3,1,0:T(8,128)} %param.15) | copy-start | bytes 6148
  93.7 28.6 %all-to-all-start.4 = ((f32[4,384,128]{2,1,0:T(8,128)}), f32[4,384,128]{2,1,0:T(8,128)S(1)}, u32[]{:S(2)}, u32[]{:S(2)}) async-start(f32[4,384,128]{2,1,0:T(8,128)} %fusion), calls=%async_computation.4 | async-start | bytes 1572864 | tf_op jit(solution)/shard_map/all_to_all | solution.py:228

commit v3 on v2

--- a/solution.py
+++ b/solution.py
@@ -168,12 +168,58 @@
     )(picks, hist, coeff_blocks)
 
 
+def pack_kernel(both_ref, out_ref):
+    groups, rows, steps = out_ref.shape
+    rows -= CODE_ROWS
+    tiles = rows // 128
+    at = lax.broadcasted_iota(jnp.int32, (128, 128), 0) == lax.broadcasted_iota(jnp.int32, (128, 128), 1)
+    for g in range(groups):
+        sums, largest = [], []
+        for i in range(tiles):
+            here = pl.ds(g * rows + i * 128, 128)
+            pair = both_ref[0, here, :] + both_ref[1, here, :]
+            top = jnp.max(jnp.abs(pair), axis=-1, keepdims=True)
+            sums.append(pair)
+            largest.append(jnp.sum(jnp.where(at, top, 0.0), axis=0, keepdims=True))
+        largest.append(jnp.zeros((8 - tiles, 128), jnp.float32))
+        code = jnp.ceil(jnp.log2(jnp.maximum(jnp.concatenate(largest, axis=0), 1e-30)) * 32.0)
+        out_ref[g, rows:, :] = code.astype(jnp.int32).astype(jnp.int16)
+        inverse = jnp.exp2(15.0 - code * (1.0 / 32.0))
+        inverse = jnp.concatenate([inverse, jnp.zeros((120, 128), jnp.float32)], axis=0).T
+        for i in range(tiles):
+            whole = jnp.clip(jnp.round(sums[i] * inverse[:, i : i + 1]), -32767.0, 32767.0)
+            out_ref[g, i * 128 : (i + 1) * 128, :] = whole.astype(jnp.int32).astype(jnp.int16)
+
+
+def pack_sums(both, groups):
+    rows, steps = both.shape[1:]
+    return pl.pallas_call(
+        pack_kernel,
+        out_shape=jax.ShapeDtypeStruct((groups, rows // groups + CODE_ROWS, steps), jnp.int16),
+        in_specs=[pl.BlockSpec(memory_space=pltpu.VMEM)],
+        out_specs=pl.BlockSpec(memory_space=pltpu.VMEM),
+        compiler_params=pltpu.CompilerParams(vmem_limit_bytes=16 << 20),
+        name="pack",
+    )(both)
+
+
 def range_kernel(parts_ref, coeff_ref, stress_ref, range_ref):
-    total = parts_ref[0]
-    for i in range(1, parts_ref.shape[0]):
-        total = total + parts_ref[i]
+    groups, rows, steps = parts_ref.shape
+    rows -= CODE_ROWS
+    codes = [parts_ref[g, rows:, :].astype(jnp.int32).astype(jnp.float32) for g in range(groups)]
+    scales = code_scale(jnp.concatenate(codes, axis=0))
+    scales = jnp.concatenate([scales, jnp.zeros((128 - groups * CODE_ROWS, 128), jnp.float32)], axis=0).T
+    pieces = []
+    for i in range(rows // 128):
+        piece = None
+        for g in range(groups):
+            value = parts_ref[g, i * 128 : (i + 1) * 128, :].astype(jnp.int32).astype(jnp.float32)
+            at = g * CODE_ROWS + i
+            value = value * scales[:, at : at + 1]
+            piece = value if piece is None else piece + value
+        pieces.append(piece)
     components, elements, steps = stress_ref.shape
-    stress = total.reshape(components, elements, steps)
+    stress = jnp.concatenate(pieces, axis=0).reshape(components, elements, steps)
     stress_ref[...] = stress
     looked = range_ref.shape[0]
     lane = lax.broadcasted_iota(jnp.int32, (elements, 128), 1)
@@ -191,6 +237,7 @@
 
 def finish(parts, coeffs, looked):
     groups, rows, steps = parts.shape
+    rows -= CODE_ROWS
     elements = coeffs.shape[0]
     stress, ranges = pl.pallas_call(
         range_kernel,
@@ -224,8 +271,8 @@
 
 def sum_over_mode(by_core):
     both = lax.all_to_all(by_core, "core", 0, 0)
-    pair = both[0] + both[1]
-    return lax.all_to_all(pair, "yh", 0, 0)
+    groups, rows, steps = by_core.shape[1:]
+    return lax.all_to_all(pack_sums(both.reshape(2, groups * rows, steps), groups), "yh", 0, 0)
 
 
 def body(load_windows, owner_id, participation, frequency, damping, recovery, pattern, plane_table):

time: 125 us -> 117 us (0.936)
  waiting for transfers between devices: 73.2 us -> 64.7 us
  Pallas kernels: 7.15 us -> 9.31 us
    all_to_all x1, waiting for transfers between devices: 21.7 us -> 13.2 us  [sum_over_mode(): lax.all_to_all(pack_sums(both.reshape(2, groups * rows, steps), groups),...]
    pallas_call x0 -> x1, Pallas kernels: none -> 1.77 us  [pack_sums(): pl.pallas_call(pack_kernel, out_shape=jax.ShapeDtypeStruct((groups, rows...]
where the time goes in v3:
time: 117 us
  waiting for transfers between devices  64.7 us (55%)
  starting transfers between devices  30.8 us (26%)
  Pallas kernels  9.31 us (8%)
  blocking collectives  7.17 us (6%)
  local copies, waits for them, and re-layouts  2.77 us (2%)
  between operations  1.42 us (1%)
    all_to_all x1, waiting for transfers between devices, body(): hist = lax.all_to_all(copies, ROW, 0, 0)  26.5 us
    all_to_all x1, starting transfers between devices, fetch_window(): lax.all_to_all(mine.reshape(count, half // count, steps), ROW, 0, 0)  14.8 us
    all_to_all x1, waiting for transfers between devices, sum_over_mode(): lax.all_to_all(pack_sums(both.reshape(2, groups * rows, steps), groups),...  13.2 us
    all_to_all x1, waiting for transfers between devices, gather_row(): return lax.all_to_all(copies, ROW, 0, 0)  12.6 us
    all_to_all x1, waiting for transfers between devices, fetch_window(): lax.all_to_all(mine.reshape(count, half // count, steps), ROW, 0, 0)  12.4 us
    all_to_all x1, starting transfers between devices, sum_over_mode(): lax.all_to_all(pack_sums(both.reshape(2, groups * rows, steps), groups),...  6.18 us
    all_to_all x1, blocking collectives, sum_over_mode(): both = lax.all_to_all(by_core, 'core', 0, 0)  5 us
    all_to_all x1, starting transfers between devices, gather_row(): return lax.all_to_all(copies, ROW, 0, 0)  4.92 us
  transfers between devices with their start and end apart: 4, of which 4 were waited for; matrix products, arithmetic and copies ran while one was open for 1% of the time, Pallas kernels for 0%

profile of v3, /device:TPU:8, one launch (start us, length us, event | category | flops | bytes accessed | tf_op | source)
XLA Modules:
  0.0 116.9 jit_solution(7861592424724957814)
XLA Ops:
  0.6 0.0 copy-start
  0.6 0.0 copy-start.3
  0.7 0.0 copy-start.4
  0.7 0.0 copy-start.1
  0.7 1.0 copy-done
  1.7 0.7 constant_dynamic-slice_fusion
  2.4 14.8 %all-to-all-start = ((bf16[64,16,128]{2,1,0:T(8,128)(2,1)}), bf16[64,16,128]{2,1,0:T(8,128)(2,1)S(1)}, u32[]{:S(2)}, u32[]{:S(2)}) async-start(bf16[64,16,128]{2,1,0:T(8,128)(2,1)} %bitcast.1), calls=%async_computation | async-start | bytes 524288 | tf_op jit(solution)/shard_map/all_to_all | solution.py:266
  17.9 12.4 %all-to-all-done = bf16[64,16,128]{2,1,0:T(8,128)(2,1)S(1)} async-done(((bf16[64,16,128]{2,1,0:T(8,128)(2,1)}), bf16[64,16,128]{2,1,0:T(8,128)(2,1)S(1)}, u32[]{:S(2)}, u32[]{:S(2)}) %all-to-all-start) | async-done | bytes 262176 | tf_op jit(solution)/shard_map/all_to_all | solution.py:266
  30.3 0.7 broadcast_in_dim.9
  31.0 4.9 %all-to-all-start.1 = ((bf16[64,16,128]{2,1,0:T(8,128)(2,1)}), bf16[64,16,128]{2,1,0:T(8,128)(2,1)S(1)}, u32[]{:S(2)}, u32[]{:S(2)}) async-start(bf16[64,16,128]{2,1,0:T(8,128)(2,1)} %broadcast_in_dim.9), calls=%async_computation.1 | async-start | bytes 524288 | tf_op jit(solution)/shard_map/all_to_all | solution.py:258
  35.9 0.0 copy-done.3
  35.9 0.0 copy-done.4
  36.0 0.1 fusion.2
  36.1 0.1 copy.18.table_ref
  36.2 12.6 %all-to-all-done.1 = bf16[64,16,128]{2,1,0:T(8,128)(2,1)S(1)} async-done(((bf16[64,16,128]{2,1,0:T(8,128)(2,1)}), bf16[64,16,128]{2,1,0:T(8,128)(2,1)S(1)}, u32[]{:S(2)}, u32[]{:S(2)}) %all-to-all-start.1) | async-done | bytes 262176 | tf_op jit(solution)/shard_map/all_to_all | solution.py:258
  48.8 2.2 %all_gather.3.window_ref = bf16[2048,128]{1,0:T(8,128)(2,1)S(1)} all-gather(bf16[1024,128]{1,0:T(8,128)(2,1)S(1)} %bitcast.27), channel_id=1, replica_groups=mesh['yh'=4,'core'=2,'z'=8,'yl'=2,'x'=4] {'core'}, dimensions={0}, use_global_device_ids=true | all-gather | bytes 786432 | tf_op jit(solution)/shard_map/all_gather | solution.py:269
  50.9 0.0 copy-done.1
  50.9 0.0 copy-start.2
  50.9 1.9 %history.1 = s16[64,56,128]{2,1,0:T(8,128)(2,1)} custom-call(bf16[2048,128]{1,0:T(8,128)(2,1)S(1)} %all_gather.3.window_ref, bf16[48,2048]{1,0:T(8,128)(2,1)S(1)} %copy-done.1, f32[48,16]{1,0:T(8,128)S(1)} %copy.18.table_ref), custom_call_target="tpu_custom_call" | custom-call | flops 25165824 | bytes 720896 | tf_op jit(solution)/shard_map/history/pallas_call | solution.py:90
  52.8 4.9 %all-to-all-start.2 = ((s16[64,56,128]{2,1,0:T(8,128)(2,1)}), s16[64,56,128]{2,1,0:T(8,128)(2,1)S(1)}, u32[]{:S(2)}, u32[]{:S(2)}) async-start(s16[64,56,128]{2,1,0:T(8,128)(2,1)} %history.1), calls=%async_computation.2 | async-start | bytes 1835008 | tf_op jit(solution)/shard_map/all_to_all | solution.py:288
  57.7 0.0 copy-done.2
  57.7 0.1 copy.19.picks_ref
  57.8 26.5 %all-to-all-done.2.hist_ref = s16[64,56,128]{2,1,0:T(8,128)(2,1)S(1)} async-done(((s16[64,56,128]{2,1,0:T(8,128)(2,1)}), s16[64,56,128]{2,1,0:T(8,128)(2,1)S(1)}, u32[]{:S(2)}, u32[]{:S(2)}) %all-to-all-start.2) | async-done | bytes 917536 | tf_op jit(solution)/shard_map/all_to_all | solution.py:288
  84.3 3.5 %recover.1 = f32[2,4,384,128]{3,2,1,0:T(8,128)S(1)} custom-call(s32[24,4]{1,0:T(8,128)S(1)} %copy.19.picks_ref, s16[64,56,128]{2,1,0:T(8,128)(2,1)S(1)} %all-to-all-done.2.hist_ref, bf16[24,4,128,128]{3,2,1,0:T(8,128)(2,1)} %bitcast.26), custom_call_target="tpu_custom_call" | custom-call | flops 805306368 | bytes 3145728 | tf_op jit(solution)/shard_map/recover/pallas_call | solution.py:147
  87.8 5.0 %all_to_all.25 = f32[2,4,384,128]{3,2,1,0:T(8,128)S(1)} all-to-all(f32[2,4,384,128]{3,2,1,0:T(8,128)S(1)} %recover.1), channel_id=1, replica_groups=mesh['yh'=4,'core'=2,'z'=8,'yl'=2,'x'=4] {'core'}, dimensions={0} | all-to-all | bytes 3145728 | tf_op jit(solution)/shard_map/all_to_all | solution.py:273
  92.8 0.0 copy-start.5
  92.8 1.8 %pack.1 = s16[4,392,128]{2,1,0:T(8,128)(2,1)} custom-call(f32[2,1536,128]{2,1,0:T(8,128)S(1)} %bitcast.25), custom_call_target="tpu_custom_call" | custom-call | tf_op jit(solution)/shard_map/pack/pallas_call | solution.py:196
  94.5 6.2 %all-to-all-start.4 = ((s16[4,392,128]{2,1,0:T(8,128)(2,1)}), s16[4,392,128]{2,1,0:T(8,128)(2,1)S(1)}, u32[]{:S(2)}, u32[]{:S(2)}) async-start(s16[4,392,128]{2,1,0:T(8,128)(2,1)} %pack.1), calls=%async_computation.4 | async-start | bytes 802816 | tf_op jit(solution)/shard_map/all_to_all | solution.py:275
  100.9 0.0 copy-done.5
  100.9 0.5 fusion
  101.4 0.1 copy.20.coeff_ref
  101.5 13.2 %all-to-all-done.4.parts_ref = s16[4,392,128]{2,1,0:T(8,128)(2,1)S(1)} async-done(((s16[4,392,128]{2,1,0:T(8,128)(2,1)}), s16[4,392,128]{2,1,0:T(8,128)(2,1)S(1)}, u32[]{:S(2)}, u32[]{:S(2)}) %all-to-all-start.4) | async-done | bytes 401440 | tf_op jit(solution)/shard_map/all_to_all | solution.py:275
  114.6 2.2 %ranges.1 = (f32[6,64,128]{2,1,0:T(8,128)}, f32[8,64]{1,0:T(8,128)}) custom-call(s16[4,392,128]{2,1,0:T(8,128)(2,1)S(1)} %all-to-all-done.4.parts_ref, f32[64,48]{1,0:T(8,128)S(1)} %copy.20.coeff_ref), custom_call_target="tpu_custom_call" | custom-call | tf_op jit(solution)/shard_map/ranges/pallas_call | solution.py:242
  (9 shorter events, 0.2 us)
Async XLA Ops:
  0.6 1.0 copy-start
  0.6 35.3 %copy-start.3 = (f32[48]{0:T(128)S(1)}, f32[48]{0:T(128)}, u32[]{:S(2)}) copy-start(f32[48]{0:T(128)} %param.11) | copy-start | bytes 580
  0.7 35.3 %copy-start.4 = (f32[48]{0:T(128)S(1)}, f32[48]{0:T(128)}, u32[]{:S(2)}) copy-start(f32[48]{0:T(128)} %param.12) | copy-start | bytes 580
  0.7 50.3 %copy-start.1 = (bf16[48,2048]{1,0:T(8,128)(2,1)S(1)}, bf16[48,2048]{1,0:T(8,128)(2,1)}, u32[]{:S(2)}) copy-start(bf16[48,2048]{1,0:T(8,128)(2,1)} %part_ref.1) | copy-start | bytes 589828
  2.4 27.9 %all-to-all-start = ((bf16[64,16,128]{2,1,0:T(8,128)(2,1)}), bf16[64,16,128]{2,1,0:T(8,128)(2,1)S(1)}, u32[]{:S(2)}, u32[]{:S(2)}) async-start(bf16[64,16,128]{2,1,0:T(8,128)(2,1)} %bitcast.1), calls=%async_computation | async-start | bytes 524288 | tf_op jit(solution)/shard_map/all_to_all | solution.py:266
  31.0 17.8 %all-to-all-start.1 = ((bf16[64,16,128]{2,1,0:T(8,128)(2,1)}), bf16[64,16,128]{2,1,0:T(8,128)(2,1)S(1)}, u32[]{:S(2)}, u32[]{:S(2)}) async-start(bf16[64,16,128]{2,1,0:T(8,128)(2,1)} %broadcast_in_dim.9), calls=%async_computation.1 | async-start | bytes 524288 | tf_op jit(solution)/shard_map/all_to_all | solution.py:258
  50.9 6.8 %copy-start.2 = (s32[1,1,24,4]{2,3,1,0:T(4,128)S(1)}, s32[1,1,24,4]{2,3,1,0:T(4,128)}, u32[]{:S(2)}) copy-start(s32[1,1,24,4]{2,3,1,0:T(4,128)} %param.14) | copy-start | bytes 1156
  52.8 31.5 %all-to-all-start.2 = ((s16[64,56,128]{2,1,0:T(8,128)(2,1)}), s16[64,56,128]{2,1,0:T(8,128)(2,1)S(1)}, u32[]{:S(2)}, u32[]{:S(2)}) async-start(s16[64,56,128]{2,1,0:T(8,128)(2,1)} %history.1), calls=%async_computation.2 | async-start | bytes 1835008 | tf_op jit(solution)/shard_map/all_to_all | solution.py:288
  92.8 8.1 %copy-start.5 = (s32[1,1,64,8]{2,3,1,0:T(8,128)S(1)}, s32[1,1,64,8]{2,3,1,0:T(8,128)}, u32[]{:S(2)}) copy-start(s32[1,1,64,8]{2,3,1,0:T(8,128)} %param.15) | copy-start | bytes 6148
  94.5 20.1 %all-to-all-start.4 = ((s16[4,392,128]{2,1,0:T(8,128)(2,1)}), s16[4,392,128]{2,1,0:T(8,128)(2,1)S(1)}, u32[]{:S(2)}, u32[]{:S(2)}) async-start(s16[4,392,128]{2,1,0:T(8,128)(2,1)} %pack.1), calls=%async_computation.4 | async-start | bytes 802816 | tf_op jit(solution)/shard_map/all_to_all | solution.py:275

commit v4 on v3

--- a/solution.py
+++ b/solution.py
@@ -9,6 +9,7 @@
 PLANES = 64
 ROW = ("z", "yl", "x")
 CODE_ROWS = 8
+LEVELS = 32760.0
 CHUNKS = 4
 
 
@@ -42,14 +43,14 @@
 
 
 def code_scale(code):
-    return jnp.exp2(code * (1.0 / 32.0) - 15.0)
+    return jnp.exp2(code * (1.0 / 32.0)) * (1.0 / LEVELS)
 
 
 def quantize(values):
     largest = jnp.max(jnp.abs(values), axis=-1, keepdims=True)
     code = jnp.ceil(jnp.log2(jnp.maximum(largest, 1e-30)) * 32.0)
-    inverse = jnp.exp2(15.0 - code * (1.0 / 32.0))
-    whole = jnp.clip(jnp.round(values * inverse), -32767.0, 32767.0).astype(jnp.int32)
+    inverse = jnp.exp2(code * (-1.0 / 32.0)) * LEVELS
+    whole = jnp.round(values * inverse).astype(jnp.int32)
     return whole, code
 
 
@@ -109,20 +110,21 @@
     ]
     for fetch in fetches:
         fetch.start()
-    sources, rows, steps = hist_ref.shape
+    across, along, rows, steps = hist_ref.shape
+    sources = across * along
     modes = rows - CODE_ROWS
     sub = lax.broadcasted_iota(jnp.int32, (8, 128), 0)
     tiles = []
     for base in range(0, sources, 8):
         tile = jnp.zeros((8, 128), jnp.int32)
         for i in range(8):
-            codes = hist_ref[base + i, modes : modes + CODE_ROWS, :].astype(jnp.int32)[:8]
+            codes = hist_ref[(base + i) % across, (base + i) // across, modes : modes + CODE_ROWS, :].astype(jnp.int32)[:8]
             tile = jnp.where(sub == i, codes, tile)
         tiles.append(tile)
     scales = code_scale(jnp.concatenate(tiles, axis=0).astype(jnp.float32))
     scales = jnp.concatenate([scales, jnp.zeros((128 - sources, 128), jnp.float32)], axis=0).T
     for s in range(sources):
-        value = hist_ref[s, :modes, :].astype(jnp.int32).astype(jnp.float32) * scales[:modes, s : s + 1]
+        value = hist_ref[s % across, s // across, :modes, :].astype(jnp.int32).astype(jnp.float32) * scales[:modes, s : s + 1]
         high = value.astype(jnp.bfloat16)
         low = (value - high.astype(jnp.float32)).astype(jnp.bfloat16)
         split_ref[s * modes : (s + 1) * modes, :steps] = high
@@ -142,7 +144,8 @@
 
 
 def recover(hist, coeff_blocks, picks, groups):
-    sources, rows, steps = hist.shape
+    across, along, rows, steps = hist.shape
+    sources = across * along
     blocks, picked, height, width = coeff_blocks.shape
     return pl.pallas_call(
         recover_kernel,
@@ -184,10 +187,10 @@
         largest.append(jnp.zeros((8 - tiles, 128), jnp.float32))
         code = jnp.ceil(jnp.log2(jnp.maximum(jnp.concatenate(largest, axis=0), 1e-30)) * 32.0)
         out_ref[g, rows:, :] = code.astype(jnp.int32).astype(jnp.int16)
-        inverse = jnp.exp2(15.0 - code * (1.0 / 32.0))
+        inverse = jnp.exp2(code * (-1.0 / 32.0)) * LEVELS
         inverse = jnp.concatenate([inverse, jnp.zeros((120, 128), jnp.float32)], axis=0).T
         for i in range(tiles):
-            whole = jnp.clip(jnp.round(sums[i] * inverse[:, i : i + 1]), -32767.0, 32767.0)
+            whole = jnp.round(sums[i] * inverse[:, i : i + 1])
             out_ref[g, i * 128 : (i + 1) * 128, :] = whole.astype(jnp.int32).astype(jnp.int16)
 
 
@@ -253,9 +256,9 @@
     return stress, ranges.T
 
 
-def gather_row(part, count):
-    copies = jnp.broadcast_to(part[None], (count,) + part.shape)
-    return lax.all_to_all(copies, ROW, 0, 0)
+def gather_over(part, axes):
+    copies = jnp.broadcast_to(part[None], (lax.axis_size(axes),) + part.shape)
+    return lax.all_to_all(copies, axes, 0, 0)
 
 
 def fetch_window(windows, owner):
@@ -265,7 +268,7 @@
     mine = lax.dynamic_slice_in_dim(windows[0], lax.axis_index("core") * half, half, 0)
     offered = lax.all_to_all(mine.reshape(count, half // count, steps), ROW, 0, 0)
     piece = lax.dynamic_index_in_dim(offered, owner, 0, keepdims=False)
-    whole_half = gather_row(piece, count).reshape(half, steps)
+    whole_half = gather_over(piece, ROW).reshape(half, steps)
     return lax.all_gather(whole_half, "core", axis=0, tiled=True)
 
 
@@ -284,8 +287,9 @@
     coeffs = coeffs.reshape(elements, looked * 6)
     table = mode_table(frequency, damping, steps)
     window = fetch_window(load_windows, owner_id[0])
-    copies = make_history(window, participation, table, lax.axis_size(ROW))
-    hist = lax.all_to_all(copies, ROW, 0, 0)
+    copies = make_history(window, participation, table, lax.axis_size(ROW[:2]))
+    column = lax.all_to_all(copies, ROW[:2], 0, 0)
+    hist = gather_over(column, ROW[2])
     partial = recover(hist, recovery[0, 0], pattern[0, 0], lax.axis_size(("yh", "core")))
     parts = sum_over_mode(partial)
     stress, plane_range = finish(parts, coeffs, looked)

time: 117 us -> 115 us (0.983)
  waiting for transfers between devices: 64.7 us -> 49.8 us
  blocking collectives: 7.17 us -> 21.2 us
  starting transfers between devices: 30.8 us -> 29.4 us
    all_to_all x0 -> x1, blocking collectives: none -> 14 us  [body(): column = lax.all_to_all(copies, ROW[:2], 0, 0)]
    all_to_all x2, waiting for transfers between devices: 39.1 us -> 26 us  [gather_over(): return lax.all_to_all(copies, axes, 0, 0)]
    all_to_all x1, waiting for transfers between devices: 13.2 us -> 11.5 us  [sum_over_mode(): lax.all_to_all(pack_sums(both.reshape(2, groups * rows, steps), groups),...]
    all_to_all x2, starting transfers between devices: 9.81 us -> 8.42 us  [gather_over(): return lax.all_to_all(copies, axes, 0, 0)]
where the time goes in v4:
time: 115 us
  waiting for transfers between devices  49.8 us (43%)
  starting transfers between devices  29.4 us (26%)
  blocking collectives  21.2 us (18%)
  Pallas kernels  8.3 us (7%)
  local copies, waits for them, and re-layouts  3.81 us (3%)
  between operations  1.43 us (1%)
    all_to_all x2, waiting for transfers between devices, gather_over(): return lax.all_to_all(copies, axes, 0, 0)  26 us
    all_to_all x1, starting transfers between devices, fetch_window(): lax.all_to_all(mine.reshape(count, half // count, steps), ROW, 0, 0)  14.8 us
    all_to_all x1, blocking collectives, body(): column = lax.all_to_all(copies, ROW[:2], 0, 0)  14 us
    all_to_all x1, waiting for transfers between devices, fetch_window(): lax.all_to_all(mine.reshape(count, half // count, steps), ROW, 0, 0)  12.4 us
    all_to_all x1, waiting for transfers between devices, sum_over_mode(): lax.all_to_all(pack_sums(both.reshape(2, groups * rows, steps), groups),...  11.5 us
    all_to_all x2, starting transfers between devices, gather_over(): return lax.all_to_all(copies, axes, 0, 0)  8.42 us
    all_to_all x1, starting transfers between devices, sum_over_mode(): lax.all_to_all(pack_sums(both.reshape(2, groups * rows, steps), groups),...  6.2 us
    all_to_all x1, blocking collectives, sum_over_mode(): both = lax.all_to_all(by_core, 'core', 0, 0)  5 us
  transfers between devices with their start and end apart: 4, of which 4 were waited for; matrix products, arithmetic and copies ran while one was open for 1% of the time, Pallas kernels for 0%

profile of v4, /device:TPU:8, one launch (start us, length us, event | category | flops | bytes accessed | tf_op | source)
XLA Modules:
  0.0 114.7 jit_solution(1264441517643535396)
XLA Ops:
  0.6 0.0 copy-start
  0.6 0.0 copy-start.3
  0.7 0.0 copy-start.4
  0.7 0.0 copy-start.1
  0.7 1.0 copy-done
  1.7 0.7 constant_dynamic-slice_fusion
  2.4 14.8 %all-to-all-start = ((bf16[64,16,128]{2,1,0:T(8,128)(2,1)}), bf16[64,16,128]{2,1,0:T(8,128)(2,1)S(1)}, u32[]{:S(2)}, u32[]{:S(2)}) async-start(bf16[64,16,128]{2,1,0:T(8,128)(2,1)} %bitcast.1), calls=%async_computation | async-start | bytes 524288 | tf_op jit(solution)/shard_map/all_to_all | solution.py:269
  17.9 12.4 %all-to-all-done = bf16[64,16,128]{2,1,0:T(8,128)(2,1)S(1)} async-done(((bf16[64,16,128]{2,1,0:T(8,128)(2,1)}), bf16[64,16,128]{2,1,0:T(8,128)(2,1)S(1)}, u32[]{:S(2)}, u32[]{:S(2)}) %all-to-all-start) | async-done | bytes 262176 | tf_op jit(solution)/shard_map/all_to_all | solution.py:269
  30.3 0.7 broadcast_in_dim.11
  31.0 4.9 %all-to-all-start.1 = ((bf16[64,16,128]{2,1,0:T(8,128)(2,1)}), bf16[64,16,128]{2,1,0:T(8,128)(2,1)S(1)}, u32[]{:S(2)}, u32[]{:S(2)}) async-start(bf16[64,16,128]{2,1,0:T(8,128)(2,1)} %broadcast_in_dim.11), calls=%async_computation.1 | async-start | bytes 524288 | tf_op jit(solution)/shard_map/all_to_all | solution.py:261
  35.9 0.0 copy-done.3
  35.9 0.0 copy-done.4
  36.0 0.1 fusion.2
  36.1 0.1 copy.18.table_ref
  36.2 12.6 %all-to-all-done.1 = bf16[64,16,128]{2,1,0:T(8,128)(2,1)S(1)} async-done(((bf16[64,16,128]{2,1,0:T(8,128)(2,1)}), bf16[64,16,128]{2,1,0:T(8,128)(2,1)S(1)}, u32[]{:S(2)}, u32[]{:S(2)}) %all-to-all-start.1) | async-done | bytes 262176 | tf_op jit(solution)/shard_map/all_to_all | solution.py:261
  48.8 2.2 %all_gather.3.window_ref = bf16[2048,128]{1,0:T(8,128)(2,1)S(1)} all-gather(bf16[1024,128]{1,0:T(8,128)(2,1)S(1)} %bitcast.27), channel_id=1, replica_groups=mesh['yh'=4,'core'=2,'z'=8,'yl'=2,'x'=4] {'core'}, dimensions={0}, use_global_device_ids=true | all-gather | bytes 786432 | tf_op jit(solution)/shard_map/all_gather | solution.py:272
  50.9 0.0 copy-done.1
  50.9 0.8 history.1
  51.8 14.0 %all_to_all.30 = s16[16,56,128]{2,1,0:T(8,128)(2,1)S(1)} all-to-all(s16[16,56,128]{2,1,0:T(8,128)(2,1)S(1)} %history.1), channel_id=1, replica_groups=mesh['yh'=4,'core'=2,'z'=8,'yl'=2,'x'=4] {'z','yl'}, dimensions={0} | all-to-all | bytes 458752 | tf_op jit(solution)/shard_map/all_to_all | solution.py:291
  65.8 0.0 copy-start.2
  65.8 1.0 broadcast_in_dim.12
  66.8 3.5 %all-to-all-start.3 = ((s16[4,16,56,128]{3,2,1,0:T(8,128)(2,1)}), s16[4,16,56,128]{3,2,1,0:T(8,128)(2,1)S(1)}, u32[]{:S(2)}, u32[]{:S(2)}) async-start(s16[4,16,56,128]{3,2,1,0:T(8,128)(2,1)} %broadcast_in_dim.12), calls=%async_computation.3 | async-start | bytes 1835008 | tf_op jit(solution)/shard_map/all_to_all | solution.py:261
  70.3 0.0 copy-done.2
  70.3 0.1 copy.19.picks_ref
  70.4 13.4 %all-to-all-done.3.hist_ref = s16[4,16,56,128]{3,2,1,0:T(8,128)(2,1)S(1)} async-done(((s16[4,16,56,128]{3,2,1,0:T(8,128)(2,1)}), s16[4,16,56,128]{3,2,1,0:T(8,128)(2,1)S(1)}, u32[]{:S(2)}, u32[]{:S(2)}) %all-to-all-start.3) | async-done | bytes 917536 | tf_op jit(solution)/shard_map/all_to_all | solution.py:261
  83.8 3.4 %recover.1 = f32[2,4,384,128]{3,2,1,0:T(8,128)S(1)} custom-call(s32[24,4]{1,0:T(8,128)S(1)} %copy.19.picks_ref, s16[4,16,56,128]{3,2,1,0:T(8,128)(2,1)S(1)} %all-to-all-done.3.hist_ref, bf16[24,4,128,128]{3,2,1,0:T(8,128)(2,1)} %bitcast.26), custom_call_target="tpu_custom_call" | custom-call | flops 805306368 | bytes 3145728 | tf_op jit(solution)/shard_map/recover/pallas_call | solution.py:150
  87.3 5.0 %all_to_all.31 = f32[2,4,384,128]{3,2,1,0:T(8,128)S(1)} all-to-all(f32[2,4,384,128]{3,2,1,0:T(8,128)S(1)} %recover.1), channel_id=1, replica_groups=mesh['yh'=4,'core'=2,'z'=8,'yl'=2,'x'=4] {'core'}, dimensions={0} | all-to-all | bytes 3145728 | tf_op jit(solution)/shard_map/all_to_all | solution.py:276
  92.3 0.0 copy-start.5
  92.3 1.8 %pack.1 = s16[4,392,128]{2,1,0:T(8,128)(2,1)} custom-call(f32[2,1536,128]{2,1,0:T(8,128)S(1)} %bitcast.25), custom_call_target="tpu_custom_call" | custom-call | tf_op jit(solution)/shard_map/pack/pallas_call | solution.py:199
  94.1 6.2 %all-to-all-start.5 = ((s16[4,392,128]{2,1,0:T(8,128)(2,1)}), s16[4,392,128]{2,1,0:T(8,128)(2,1)S(1)}, u32[]{:S(2)}, u32[]{:S(2)}) async-start(s16[4,392,128]{2,1,0:T(8,128)(2,1)} %pack.1), calls=%async_computation.5 | async-start | bytes 802816 | tf_op jit(solution)/shard_map/all_to_all | solution.py:278
  100.4 0.0 copy-done.5
  100.4 0.5 fusion
  100.9 0.1 copy.20.coeff_ref
  101.0 11.5 %all-to-all-done.5.parts_ref = s16[4,392,128]{2,1,0:T(8,128)(2,1)S(1)} async-done(((s16[4,392,128]{2,1,0:T(8,128)(2,1)}), s16[4,392,128]{2,1,0:T(8,128)(2,1)S(1)}, u32[]{:S(2)}, u32[]{:S(2)}) %all-to-all-start.5) | async-done | bytes 401440 | tf_op jit(solution)/shard_map/all_to_all | solution.py:278
  112.5 2.2 %ranges.1 = (f32[6,64,128]{2,1,0:T(8,128)}, f32[8,64]{1,0:T(8,128)}) custom-call(s16[4,392,128]{2,1,0:T(8,128)(2,1)S(1)} %all-to-all-done.5.parts_ref, f32[64,48]{1,0:T(8,128)S(1)} %copy.20.coeff_ref), custom_call_target="tpu_custom_call" | custom-call | tf_op jit(solution)/shard_map/ranges/pallas_call | solution.py:245
  (9 shorter events, 0.2 us)
Async XLA Ops:
  0.6 1.0 copy-start
  0.6 35.3 %copy-start.3 = (f32[48]{0:T(128)S(1)}, f32[48]{0:T(128)}, u32[]{:S(2)}) copy-start(f32[48]{0:T(128)} %param.11) | copy-start | bytes 580
  0.7 35.3 %copy-start.4 = (f32[48]{0:T(128)S(1)}, f32[48]{0:T(128)}, u32[]{:S(2)}) copy-start(f32[48]{0:T(128)} %param.12) | copy-start | bytes 580
  0.7 50.3 %copy-start.1 = (bf16[48,2048]{1,0:T(8,128)(2,1)S(1)}, bf16[48,2048]{1,0:T(8,128)(2,1)}, u32[]{:S(2)}) copy-start(bf16[48,2048]{1,0:T(8,128)(2,1)} %part_ref.1) | copy-start | bytes 589828
  2.4 27.9 %all-to-all-start = ((bf16[64,16,128]{2,1,0:T(8,128)(2,1)}), bf16[64,16,128]{2,1,0:T(8,128)(2,1)S(1)}, u32[]{:S(2)}, u32[]{:S(2)}) async-start(bf16[64,16,128]{2,1,0:T(8,128)(2,1)} %bitcast.1), calls=%async_computation | async-start | bytes 524288 | tf_op jit(solution)/shard_map/all_to_all | solution.py:269
  31.0 17.8 %all-to-all-start.1 = ((bf16[64,16,128]{2,1,0:T(8,128)(2,1)}), bf16[64,16,128]{2,1,0:T(8,128)(2,1)S(1)}, u32[]{:S(2)}, u32[]{:S(2)}) async-start(bf16[64,16,128]{2,1,0:T(8,128)(2,1)} %broadcast_in_dim.11), calls=%async_computation.1 | async-start | bytes 524288 | tf_op jit(solution)/shard_map/all_to_all | solution.py:261
  65.8 4.6 %copy-start.2 = (s32[1,1,24,4]{2,3,1,0:T(4,128)S(1)}, s32[1,1,24,4]{2,3,1,0:T(4,128)}, u32[]{:S(2)}) copy-start(s32[1,1,24,4]{2,3,1,0:T(4,128)} %param.14) | copy-start | bytes 1156
  66.8 17.0 %all-to-all-start.3 = ((s16[4,16,56,128]{3,2,1,0:T(8,128)(2,1)}), s16[4,16,56,128]{3,2,1,0:T(8,128)(2,1)S(1)}, u32[]{:S(2)}, u32[]{:S(2)}) async-start(s16[4,16,56,128]{3,2,1,0:T(8,128)(2,1)} %broadcast_in_dim.12), calls=%async_computation.3 | async-start | bytes 1835008 | tf_op jit(solution)/shard_map/all_to_all | solution.py:261
  92.3 8.2 %copy-start.5 = (s32[1,1,64,8]{2,3,1,0:T(8,128)S(1)}, s32[1,1,64,8]{2,3,1,0:T(8,128)}, u32[]{:S(2)}) copy-start(s32[1,1,64,8]{2,3,1,0:T(8,128)} %param.15) | copy-start | bytes 6148
  94.1 18.4 %all-to-all-start.5 = ((s16[4,392,128]{2,1,0:T(8,128)(2,1)}), s16[4,392,128]{2,1,0:T(8,128)(2,1)S(1)}, u32[]{:S(2)}, u32[]{:S(2)}) async-start(s16[4,392,128]{2,1,0:T(8,128)(2,1)} %pack.1), calls=%async_computation.5 | async-start | bytes 802816 | tf_op jit(solution)/shard_map/all_to_all | solution.py:278

commit v5 on v4

v5 whole, which is shorter than its diff:
```python
import jax
import jax.numpy as jnp
from jax import lax
from jax.experimental import pallas as pl
from jax.experimental.pallas import tpu as pltpu
from jax.sharding import Mesh
from jax.sharding import PartitionSpec as P

ROW = ("z", "yl", "x")
CODE_ROWS = 8
LEVELS = 32760.0
PLANES = 64


def code_scale(code):
    return jnp.exp2(code * (1.0 / 32.0)) * (1.0 / LEVELS)


def quantize(values):
    largest = jnp.max(jnp.abs(values), axis=-1, keepdims=True)
    code = jnp.ceil(jnp.log2(jnp.maximum(largest, 1e-30)) * 32.0)
    inverse = jnp.exp2(code * (-1.0 / 32.0)) * LEVELS
    whole = jnp.round(values * inverse).astype(jnp.int32)
    return whole, code


def as_row(column):
    n = column.shape[0]
    at = lax.broadcasted_iota(jnp.int32, (n, 128), 0) == lax.broadcasted_iota(jnp.int32, (n, 128), 1)
    return jnp.sum(jnp.where(at, column, 0.0), axis=0, keepdims=True)


def mode_table(rates, decays, rows_ref):
    modes = rates.shape[1]
    shifts = (1 << lax.broadcasted_iota(jnp.int32, (8, modes), 0)).astype(jnp.float32)
    angle = rates * shifts
    cos, sin = jnp.cos(angle), jnp.sin(angle)
    shrink = jnp.exp(-decays * rates * shifts)
    rows_ref[0:8, :modes] = shrink * cos
    rows_ref[8:16, :modes] = shrink * sin
    rows_ref[16:24, :modes] = rates * jnp.broadcast_to(sin[0:1], (8, modes))
    rows_ref[24:32, :modes] = rates * jnp.broadcast_to(cos[0:1], (8, modes))
    return rows_ref[...].T[:modes]


def history_kernel(window_ref, part_ref, rate_ref, decay_ref, out_ref, rows_ref):
    forces = jnp.dot(part_ref[...], window_ref[...], preferred_element_type=jnp.float32)
    modes, steps = forces.shape
    doublings = steps.bit_length() - 1
    table = mode_table(rate_ref[...], decay_ref[...], rows_ref)
    lane = lax.broadcasted_iota(jnp.int32, forces.shape, 1)
    re, im = forces, jnp.zeros_like(forces)
    for d in range(doublings):
        shift = 1 << d
        p_re, p_im = table[:, d : d + 1], table[:, 8 + d : 9 + d]
        keep = lane >= shift
        old_re = jnp.where(keep, pltpu.roll(re, shift, 1), 0.0)
        if d == 0:
            re, im = re + p_re * old_re, p_im * old_re
            continue
        old_im = jnp.where(keep, pltpu.roll(im, shift, 1), 0.0)
        re, im = re + p_re * old_re - p_im * old_im, im + p_re * old_im + p_im * old_re
    hist = table[:, 16:17] * re + table[:, 24:25] * im
    whole, code = quantize(hist)
    codes = jnp.broadcast_to(as_row(code), (CODE_ROWS, 128)).astype(jnp.int32)
    block = jnp.concatenate([whole, codes], axis=0).astype(jnp.int16)
    for i in range(out_ref.shape[0]):
        out_ref[i] = block


def make_history(window, participation, frequency, damping, count):
    modes, channels = participation.shape
    steps = window.shape[1]
    return pl.pallas_call(
        history_kernel,
        out_shape=jax.ShapeDtypeStruct((count, modes + CODE_ROWS, steps), jnp.int16),
        in_specs=[pl.BlockSpec(memory_space=pltpu.VMEM)] * 4,
        out_specs=pl.BlockSpec(memory_space=pltpu.VMEM),
        scratch_shapes=[pltpu.VMEM((128, 128), jnp.float32)],
        compiler_params=pltpu.CompilerParams(vmem_limit_bytes=16 << 20),
        cost_estimate=pl.CostEstimate(
            flops=2 * modes * channels * steps, bytes_accessed=2 * (channels * (modes + steps)), transcendentals=0
        ),
        name="history",
    )(window, participation, frequency, damping)


def recover_kernel(picks_ref, core_ref, hist_ref, far_ref, own_ref, other_ref, split_ref, coeff_ref, sems):
    fetches = [[], []]
    for i, side in enumerate([1 - core_ref[0], core_ref[0]]):
        for g in range(coeff_ref.shape[0] // 2):
            slab = 2 * g + side
            fetch = pltpu.make_async_copy(far_ref.at[slab], coeff_ref.at[slab], sems.at[i, g])
            fetch.start()
            fetches[i].append(fetch)
    across, along, rows, steps = hist_ref.shape
    sources = across * along
    modes = rows - CODE_ROWS
    sub = lax.broadcasted_iota(jnp.int32, (8, 128), 0)
    tiles = []
    for base in range(0, sources, 8):
        tile = jnp.zeros((8, 128), jnp.int32)
        for i in range(8):
            codes = hist_ref[(base + i) % across, (base + i) // across, modes : modes + CODE_ROWS, :].astype(jnp.int32)[:8]
            tile = jnp.where(sub == i, codes, tile)
        tiles.append(tile)
    scales = code_scale(jnp.concatenate(tiles, axis=0).astype(jnp.float32))
    scales = jnp.concatenate([scales, jnp.zeros((128 - sources, 128), jnp.float32)], axis=0).T
    for s in range(sources):
        value = hist_ref[s % across, s // across, :modes, :].astype(jnp.int32).astype(jnp.float32) * scales[:modes, s : s + 1]
        high = value.astype(jnp.bfloat16)
        low = (value - high.astype(jnp.float32)).astype(jnp.bfloat16)
        split_ref[s * modes : (s + 1) * modes, :steps] = high
        split_ref[s * modes : (s + 1) * modes, steps:] = low
    slabs, per_slab, picked, height, width = coeff_ref.shape
    core = core_ref[0]
    for i, (ref, side) in enumerate([(other_ref, 1 - core), (own_ref, core)]):
        for g in range(slabs // 2):
            slab = 2 * g + side
            fetches[i][g].wait()
            for r in range(per_slab):
                left = jnp.concatenate([coeff_ref[slab, r, k] for k in range(picked)], axis=1)
                starts = [pl.multiple_of(picks_ref[k, slab * per_slab + r] * width, width) for k in range(picked)]
                right = jnp.concatenate([split_ref[pl.ds(start, width), :] for start in starts], axis=0)
                both = jnp.dot(left, right, preferred_element_type=jnp.float32)
                ref[g, r * height : (r + 1) * height, :] = both[:, :steps] + both[:, steps:]


def recover(hist, coeff_blocks, picks, core, groups):
    across, along, rows, steps = hist.shape
    blocks, picked, height, width = coeff_blocks.shape
    slabs = coeff_blocks.reshape(groups, blocks // groups, picked, height, width)
    half = jax.ShapeDtypeStruct((groups // 2, blocks // groups * height, steps), jnp.float32)
    return pl.pallas_call(
        recover_kernel,
        out_shape=(half, half),
        in_specs=[
            pl.BlockSpec(memory_space=pltpu.SMEM),
            pl.BlockSpec(memory_space=pltpu.SMEM),
            pl.BlockSpec(memory_space=pltpu.VMEM),
            pl.BlockSpec(memory_space=pl.ANY),
        ],
        out_specs=(pl.BlockSpec(memory_space=pltpu.VMEM),) * 2,
        scratch_shapes=[
            pltpu.VMEM((across * along * (rows - CODE_ROWS), 2 * steps), jnp.bfloat16),
            pltpu.VMEM(slabs.shape, jnp.bfloat16),
            pltpu.SemaphoreType.DMA((2, groups // 2)),
        ],
        compiler_params=pltpu.CompilerParams(vmem_limit_bytes=24 << 20),
        cost_estimate=pl.CostEstimate(
            flops=4 * blocks * picked * height * width * steps,
            bytes_accessed=2 * blocks * picked * height * width,
            transcendentals=0,
        ),
        name="recover",
    )(picks, core, hist, pltpu.with_memory_space_constraint(slabs, pltpu.HBM))


def pack_kernel(own_ref, come_ref, out_ref):
    groups, rows, steps = out_ref.shape
    rows -= CODE_ROWS
    tiles = rows // 128
    at = lax.broadcasted_iota(jnp.int32, (128, 128), 0) == lax.broadcasted_iota(jnp.int32, (128, 128), 1)
    for g in range(groups):
        sums, largest = [], []
        for i in range(tiles):
            here = pl.ds(i * 128, 128)
            pair = own_ref[g, here, :] + come_ref[g, here, :]
            top = jnp.max(jnp.abs(pair), axis=-1, keepdims=True)
            sums.append(pair)
            largest.append(jnp.sum(jnp.where(at, top, 0.0), axis=0, keepdims=True))
        largest.append(jnp.zeros((8 - tiles, 128), jnp.float32))
        code = jnp.ceil(jnp.log2(jnp.maximum(jnp.concatenate(largest, axis=0), 1e-30)) * 32.0)
        out_ref[g, rows:, :] = code.astype(jnp.int32).astype(jnp.int16)
        inverse = jnp.exp2(code * (-1.0 / 32.0)) * LEVELS
        inverse = jnp.concatenate([inverse, jnp.zeros((120, 128), jnp.float32)], axis=0).T
        for i in range(tiles):
            whole = jnp.round(sums[i] * inverse[:, i : i + 1])
            out_ref[g, i * 128 : (i + 1) * 128, :] = whole.astype(jnp.int32).astype(jnp.int16)


def pack_sums(own, come):
    groups, rows, steps = own.shape
    return pl.pallas_call(
        pack_kernel,
        out_shape=jax.ShapeDtypeStruct((groups, rows + CODE_ROWS, steps), jnp.int16),
        in_specs=[pl.BlockSpec(memory_space=pltpu.VMEM)] * 2,
        out_specs=pl.BlockSpec(memory_space=pltpu.VMEM),
        compiler_params=pltpu.CompilerParams(vmem_limit_bytes=16 << 20),
        name="pack",
    )(own, come)


def plane_columns(planes, rows_ref):
    looked, elements = planes.shape
    index = planes.astype(jnp.float32)
    height = (index + 0.5) * (1.0 / PLANES)
    azimuth = index * 2.399963229728653
    radius = jnp.sqrt(1.0 - height * height)
    normal_x = radius * jnp.cos(azimuth)
    normal_y = radius * jnp.sin(azimuth)
    coeffs = [
        normal_x * normal_x,
        normal_y * normal_y,
        height * height,
        2.0 * normal_x * normal_y,
        2.0 * normal_y * height,
        2.0 * normal_x * height,
    ]
    for q, coeff in enumerate(coeffs):
        rows_ref[q * looked : (q + 1) * looked, :elements] = coeff
    return rows_ref[...].T[:elements]


def range_kernel(parts_ref, plane_ref, stress_ref, range_ref, rows_ref):
    groups, rows, steps = parts_ref.shape
    rows -= CODE_ROWS
    codes = [parts_ref[g, rows:, :].astype(jnp.int32).astype(jnp.float32) for g in range(groups)]
    scales = code_scale(jnp.concatenate(codes, axis=0))
    scales = jnp.concatenate([scales, jnp.zeros((128 - groups * CODE_ROWS, 128), jnp.float32)], axis=0).T
    pieces = []
    for i in range(rows // 128):
        piece = None
        for g in range(groups):
            value = parts_ref[g, i * 128 : (i + 1) * 128, :].astype(jnp.int32).astype(jnp.float32)
            at = g * CODE_ROWS + i
            value = value * scales[:, at : at + 1]
            piece = value if piece is None else piece + value
        pieces.append(piece)
    components, elements, steps = stress_ref.shape
    stress = jnp.concatenate(pieces, axis=0).reshape(components, elements, steps)
    stress_ref[...] = stress
    looked = range_ref.shape[0]
    lane = lax.broadcasted_iota(jnp.int32, (elements, 128), 1)
    coeffs = plane_columns(plane_ref[...], rows_ref)
    result = jnp.zeros((elements, 128), jnp.float32)
    for p in range(looked):
        normal = coeffs[:, p : p + 1] * stress[0]
        for q in range(1, components):
            at = q * looked + p
            normal = normal + coeffs[:, at : at + 1] * stress[q]
        spread = jnp.max(normal, axis=-1, keepdims=True) - jnp.min(normal, axis=-1, keepdims=True)
        result = jnp.where(lane == p, spread, result)
    range_ref[...] = result.T[:looked, :]


def finish(parts, planes):
    groups, rows, steps = parts.shape
    rows -= CODE_ROWS
    looked, elements = planes.shape
    stress, ranges = pl.pallas_call(
        range_kernel,
        out_shape=(
            jax.ShapeDtypeStruct((rows // elements, elements, steps), jnp.float32),
            jax.ShapeDtypeStruct((looked, elements), jnp.float32),
        ),
        in_specs=[pl.BlockSpec(memory_space=pltpu.VMEM)] * 2,
        out_specs=(pl.BlockSpec(memory_space=pltpu.VMEM),) * 2,
        scratch_shapes=[pltpu.VMEM((128, 128), jnp.float32)],
        compiler_params=pltpu.CompilerParams(vmem_limit_bytes=8 << 20),
        name="ranges",
    )(parts, planes)
    return stress, ranges.T


def gather_over(part, axes):
    copies = jnp.broadcast_to(part[None], (lax.axis_size(axes),) + part.shape)
    return lax.all_to_all(copies, axes, 0, 0)


def stage_kernel(core_ref, owner_ref, whole_ref, *refs):
    count = (len(refs) - 3) // 2
    far, (half_ref, *near, same_ref, sems) = refs[:count], refs[count:]
    rows = half_ref.shape[0]
    start = pl.multiple_of(core_ref[0] * rows, rows)
    fetches = [pltpu.make_async_copy(whole_ref.at[pl.ds(start, rows)], half_ref, sems.at[count])]
    fetches += [pltpu.make_async_copy(a, b, sems.at[i]) for i, (a, b) in enumerate(zip(far, near))]
    for fetch in fetches:
        fetch.start()
    same_ref[0] = owner_ref[0]
    for fetch in fetches:
        fetch.wait()


def stage(whole, core, owner, *others):
    channels, steps = whole.shape
    copied = [jax.ShapeDtypeStruct((channels // 2, steps), whole.dtype)]
    copied += [jax.ShapeDtypeStruct(x.shape, x.dtype) for x in others]
    return pl.pallas_call(
        stage_kernel,
        out_shape=(*copied, jax.ShapeDtypeStruct(owner.shape, owner.dtype)),
        in_specs=[pl.BlockSpec(memory_space=pltpu.SMEM)] * 2 + [pl.BlockSpec(memory_space=pl.ANY)] * len(copied),
        out_specs=(pl.BlockSpec(memory_space=pltpu.VMEM),) * len(copied) + (pl.BlockSpec(memory_space=pltpu.SMEM),),
        scratch_shapes=[pltpu.SemaphoreType.DMA((len(copied),))],
        compiler_params=pltpu.CompilerParams(vmem_limit_bytes=8 << 20),
        name="stage",
    )(core, owner, *(pltpu.with_memory_space_constraint(x, pltpu.HBM) for x in (whole, *others)))


def pick_kernel(owner_ref, offered_ref, out_ref):
    piece = offered_ref[owner_ref[0]]
    for i in range(out_ref.shape[0]):
        out_ref[i] = piece


def pick_piece(offered, owner):
    return pl.pallas_call(
        pick_kernel,
        out_shape=jax.ShapeDtypeStruct(offered.shape, offered.dtype),
        in_specs=[pl.BlockSpec(memory_space=pltpu.SMEM), pl.BlockSpec(memory_space=pltpu.VMEM)],
        out_specs=pl.BlockSpec(memory_space=pltpu.VMEM),
        compiler_params=pltpu.CompilerParams(vmem_limit_bytes=8 << 20),
        name="pick",
    )(owner, offered)


def fetch_window(half, owner):
    count = lax.axis_size(ROW)
    pieces = half.reshape(count, half.shape[0] // count, half.shape[1])
    offered = lax.all_to_all(pieces, ROW, 0, 0)
    whole_half = lax.all_to_all(pick_piece(offered, owner), ROW, 0, 0).reshape(half.shape)
    return lax.all_gather(whole_half, "core", axis=0, tiled=True)


def body(load_windows, owner_id, participation, frequency, damping, recovery, pattern, plane_table):
    core = lax.axis_index("core")[None].astype(jnp.int32)
    half, part, rates, decays, owner = stage(
        load_windows[0], core, owner_id, participation, frequency[None], damping[None]
    )
    window = fetch_window(half, owner)
    copies = make_history(window, part, rates, decays, lax.axis_size(ROW[:2]))
    column = lax.all_to_all(copies, ROW[:2], 0, 0)
    hist = gather_over(column, ROW[2])
    own, other = recover(hist, recovery[0, 0], pattern[0, 0].T, core, lax.axis_size(("yh", "core")))
    come = lax.ppermute(other, "core", [(0, 1), (1, 0)])
    parts = lax.all_to_all(pack_sums(own, come), "yh", 0, 0)
    stress, plane_range = finish(parts, plane_table[0, 0].T)
    return (stress[None, None], plane_range[None, None])


def solution(mesh):
    fine = Mesh(mesh.devices.reshape(4, 2, 8, 2, 4), ("yh", "core") + ROW)
    mode = ("yh", "core")
    placed = (
        P(ROW, None, None),
        P(),
        P(mode + ROW, None),
        P(mode + ROW),
        P(mode + ROW),
        P(mode, ROW, None, None, None, None),
        P(mode, ROW, None, None),
        P(ROW, mode, None, None),
    )
    return jax.shard_map(
        body,
        mesh=fine,
        in_specs=placed,
        out_specs=(P(ROW, mode, None, None, None), P(ROW, mode, None, None)),
        check_vma=False,
    )
```

time: 115 us -> 113 us (0.983)
  blocking collectives: 21.2 us -> 96.3 us
  waiting for transfers between devices: 49.8 us -> 2.25 us
  starting transfers between devices: 29.4 us -> 1.92 us
  local copies, waits for them, and re-layouts: 3.81 us -> 0.13 us
  Pallas kernels: 8.3 us -> 10.5 us
    all_to_all x1 -> x4, blocking collectives: 5 us -> 80.2 us  [the longest x1 27.7 us: fetch_window(): offered = lax.all_to_all(pieces, ROW, 0, 0)]
    all_to_all x4 -> x0, waiting for transfers between devices: 49.8 us -> none  [the longest x2 26 us: gather_over(): return lax.all_to_all(copies, axes, 0, 0)]
    all_to_all x4 -> x0, starting transfers between devices: 29.4 us -> none  [the longest x1 14.8 us: fetch_window(): lax.all_to_all(mine.reshape(count, half // count, steps), ROW, 0, 0)]
    pallas_call x1 -> x3, Pallas kernels: 3.45 us -> 6.36 us  [the longest x1 4.1 us: recover(): pl.pallas_call(recover_kernel, out_shape=(half, half), in_specs=[pl.Block...]
    ppermute x0 -> x1, waiting for transfers between devices: none -> 2.25 us  [body(): come = lax.ppermute(other, 'core', [(0, 1), (1, 0)])]
    ppermute x0 -> x1, starting transfers between devices: none -> 1.92 us  [body(): come = lax.ppermute(other, 'core', [(0, 1), (1, 0)])]
    broadcast_in_dim x3 -> x1, local copies, waits for them, and re-layouts: 1.77 us -> 0.12 us  [gather_over(): copies = jnp.broadcast_to(part[None], (lax.axis_size(axes),) + part.shape)]
  transfers between devices with their start and end apart: 4 -> 1, of which waited for: 4 -> 1; matrix products, arithmetic and copies ran while one was open for 1% -> 0% of each run, Pallas kernels for 0% -> 0%
where the time goes in v5:
time: 113 us; the launch traced here: 112 us
  blocking collectives  96.3 us (85%)
  Pallas kernels  10.5 us (9%)
  waiting for transfers between devices  2.25 us (2%)
  starting transfers between devices  1.92 us (2%)
  between operations  1.33 us (1%)
    all_to_all x1, blocking collectives, fetch_window(): offered = lax.all_to_all(pieces, ROW, 0, 0)  27.7 us
    all_to_all x1, blocking collectives, body(): parts = lax.all_to_all(pack_sums(own, come), 'yh', 0, 0)  19 us
    all_to_all x1, blocking collectives, fetch_window(): lax.all_to_all(pick_piece(offered, owner), ROW, 0, 0).reshape(half.shape)  17.6 us
    all_to_all x1, blocking collectives, gather_over(): return lax.all_to_all(copies, axes, 0, 0)  15.9 us
    all_to_all x1, blocking collectives, body(): column = lax.all_to_all(copies, ROW[:2], 0, 0)  14 us
    pallas_call x1, Pallas kernels, recover(): pl.pallas_call(recover_kernel, out_shape=(half, half), in_specs=[pl.Block...  4.1 us
  transfers between devices with their start and end apart: 1, of which 1 were waited for; matrix products, arithmetic and copies ran while one was open for 0% of the time, Pallas kernels for 0%

profile of v5, /device:TPU:8, one launch (start us, length us, event | category | flops | bytes accessed | tf_op | source)
XLA Modules:
  0.0 112.4 jit_solution(8082452289407244896)
XLA Ops:
  1.3 1.6 %stage.1 = (bf16[1024,128]{1,0:T(8,128)(2,1)S(1)}, bf16[48,2048]{1,0:T(8,128)(2,1)S(1)}, f32[1,48]{1,0:T(1,128)S(1)}, f32[1,48]{1,0:T(1,128)S(1)}, s32[1]{0:T(128)}) custom-call(s32[1]{0:T(128)} %bitcast.2.core_ref, s32[1]{0:T(128)S(6)} %copy.10.owner_ref, bf16[2048,128]{1,0:T(8,128)(2,1)} %bitcast.22, bf16[48,2048]{1,0:T(8,128)(2,1)} %refs_0_.1, ...), custom_call_target="tpu_custom_call" | custom-call | tf_op jit(solution)/shard_map/stage/pallas_call | solution.py:289
  2.9 27.7 %all_to_all.25.offered_ref = bf16[64,16,128]{2,1,0:T(8,128)(2,1)S(1)} all-to-all(bf16[64,16,128]{2,1,0:T(8,128)(2,1)S(1)} %bitcast.17), channel_id=1, replica_groups=mesh['yh'=4,'core'=2,'z'=8,'yl'=2,'x'=4] {'z','yl','x'}, dimensions={0} | all-to-all | bytes 524288 | tf_op jit(solution)/shard_map/all_to_all | solution.py:320
  30.5 0.0 copy-start.1
  30.5 0.7 pick.1
  31.2 17.6 %all_to_all.26 = bf16[64,16,128]{2,1,0:T(8,128)(2,1)S(1)} all-to-all(bf16[64,16,128]{2,1,0:T(8,128)(2,1)S(1)} %pick.1), channel_id=1, replica_groups=mesh['yh'=4,'core'=2,'z'=8,'yl'=2,'x'=4] {'z','yl','x'}, dimensions={0} | all-to-all | bytes 524288 | tf_op jit(solution)/shard_map/all_to_all | solution.py:321
  48.8 2.2 %all_gather.3.window_ref = bf16[2048,128]{1,0:T(8,128)(2,1)S(1)} all-gather(bf16[1024,128]{1,0:T(8,128)(2,1)S(1)} %bitcast.21), channel_id=1, replica_groups=mesh['yh'=4,'core'=2,'z'=8,'yl'=2,'x'=4] {'core'}, dimensions={0}, use_global_device_ids=true | all-gather | bytes 786432 | tf_op jit(solution)/shard_map/all_gather | solution.py:322
  51.0 0.9 history.1
  51.8 14.0 %all_to_all.27 = s16[16,56,128]{2,1,0:T(8,128)(2,1)S(1)} all-to-all(s16[16,56,128]{2,1,0:T(8,128)(2,1)S(1)} %history.1), channel_id=1, replica_groups=mesh['yh'=4,'core'=2,'z'=8,'yl'=2,'x'=4] {'z','yl'}, dimensions={0} | all-to-all | bytes 458752 | tf_op jit(solution)/shard_map/all_to_all | solution.py:332
  65.8 0.1 broadcast_in_dim.24
  66.0 15.9 %all_to_all.28.hist_ref = s16[4,16,56,128]{3,2,1,0:T(8,128)(2,1)S(1)} all-to-all(s16[4,16,56,128]{3,2,1,0:T(8,128)(2,1)S(1)} %broadcast_in_dim.24), channel_id=1, replica_groups=mesh['yh'=4,'core'=2,'z'=8,'yl'=2,'x'=4] {'x'}, dimensions={0} | all-to-all | bytes 1835008 | tf_op jit(solution)/shard_map/all_to_all | solution.py:268
  81.9 0.0 copy-done.1
  81.9 0.0 copy-start
  81.9 4.1 %recover.1 = (f32[4,384,128]{2,1,0:T(8,128)S(1)}, f32[4,384,128]{2,1,0:T(8,128)S(1)}) custom-call(s32[4,24]{1,0:T(4,128)S(1)} %bitcast.19, s32[1]{0:T(128)} %bitcast.2.core_ref, s16[4,16,56,128]{3,2,1,0:T(8,128)(2,1)S(1)} %all_to_all.28.hist_ref, bf16[8,3,4,128,128]{4,3,2,1,0:T(8,128)(2,1)} %bitcast.20), custom_call_target="tpu_custom_call" | custom-call | flops 805306368 | bytes 3145728 | tf_op jit(solution)/shard_map/recover/pallas_call | solution.py:134
  86.0 1.9 %collective-permute-start = (f32[4,384,128]{2,1,0:T(8,128)S(1)}, f32[4,384,128]{2,1,0:T(8,128)S(1)}, u32[]{:S(2)}, u32[]{:S(2)}) collective-permute-start(f32[4,384,128]{2,1,0:T(8,128)S(1)} %get-tuple-element.17), channel_id=1, source_target_pairs={{0,64},{64,0},{1,65},{65,1},{2,66},{66,2},{3,67},{67,3},{4,68},{68... | collective-permute-start | bytes 2359304 | tf_op jit(solution)/shard_map/ppermute | solution.py:335
  87.9 2.3 %collective-permute-done.come_ref = f32[4,384,128]{2,1,0:T(8,128)S(1)} collective-permute-done((f32[4,384,128]{2,1,0:T(8,128)S(1)}, f32[4,384,128]{2,1,0:T(8,128)S(1)}, u32[]{:S(2)}, u32[]{:S(2)}) %collective-permute-start) | collective-permute-done | bytes 786464 | tf_op jit(solution)/shard_map/ppermute | solution.py:335
  90.2 1.0 pack.1
  91.2 19.0 %all_to_all.29.parts_ref = s16[4,392,128]{2,1,0:T(8,128)(2,1)S(1)} all-to-all(s16[4,392,128]{2,1,0:T(8,128)(2,1)S(1)} %pack.1), channel_id=1, replica_groups=mesh['yh'=4,'core'=2,'z'=8,'yl'=2,'x'=4] {'yh'}, dimensions={0} | all-to-all | bytes 802816 | tf_op jit(solution)/shard_map/all_to_all | solution.py:336
  110.2 0.0 copy-done
  110.2 2.2 %ranges.1 = (f32[6,64,128]{2,1,0:T(8,128)}, f32[8,64]{1,0:T(8,128)}) custom-call(s16[4,392,128]{2,1,0:T(8,128)(2,1)S(1)} %all_to_all.29.parts_ref, s32[8,64]{1,0:T(8,128)S(1)} %bitcast.18), custom_call_target="tpu_custom_call" | custom-call | tf_op jit(solution)/shard_map/ranges/pallas_call | solution.py:251
Async XLA Ops:
  30.5 51.4 %copy-start.1 = (s32[1,1,24,4]{2,3,1,0:T(4,128)S(1)}, s32[1,1,24,4]{2,3,1,0:T(4,128)}, u32[]{:S(2)}) copy-start(s32[1,1,24,4]{2,3,1,0:T(4,128)} %param.14) | copy-start | bytes 1156
  81.9 28.3 %copy-start = (s32[1,1,64,8]{2,3,1,0:T(8,128)S(1)}, s32[1,1,64,8]{2,3,1,0:T(8,128)}, u32[]{:S(2)}) copy-start(s32[1,1,64,8]{2,3,1,0:T(8,128)} %param.15) | copy-start | bytes 6148
  86.0 4.2 %collective-permute-start = (f32[4,384,128]{2,1,0:T(8,128)S(1)}, f32[4,384,128]{2,1,0:T(8,128)S(1)}, u32[]{:S(2)}, u32[]{:S(2)}) collective-permute-start(f32[4,384,128]{2,1,0:T(8,128)S(1)} %get-tuple-element.17), channel_id=1, source_target_pairs={{0,64},{64,0},{1,65},{65,1},{2,66},{66,2},{3,67},{67,3},{4,68},{68... | collective-permute-start | bytes 2359304 | tf_op jit(solution)/shard_map/ppermute | solution.py:335

commit v6 on v5

--- a/solution.py
+++ b/solution.py
@@ -85,12 +85,30 @@
     )(window, participation, frequency, damping)
 
 
-def recover_kernel(picks_ref, core_ref, hist_ref, far_ref, own_ref, other_ref, split_ref, coeff_ref, sems):
+def product(picks_ref, side, coeff_ref, split_ref, out_ref, fetches):
+    groups, per_slab, picked, height, width = coeff_ref.shape
+    steps = out_ref.shape[2]
+    for g in range(groups):
+        if fetches:
+            fetches[g].wait()
+        for r in range(per_slab):
+            block = (2 * g + side) * per_slab + r
+            left = jnp.concatenate([coeff_ref[g, r, k] for k in range(picked)], axis=1)
+            starts = [pl.multiple_of(picks_ref[k, block] * width, width) for k in range(picked)]
+            right = jnp.concatenate([split_ref[pl.ds(start, width), :] for start in starts], axis=0)
+            both = jnp.dot(left, right, preferred_element_type=jnp.float32)
+            out_ref[g, r * height : (r + 1) * height, :] = both[:, :steps] + both[:, steps:]
+
+
+def first_kernel(hist_ref, picks_far, far_ref, other_ref, split_ref, mine_ref, theirs_ref, picks_ref, sems, picks_sem):
+    core = lax.axis_index("core")
+    groups = mine_ref.shape[0]
     fetches = [[], []]
-    for i, side in enumerate([1 - core_ref[0], core_ref[0]]):
-        for g in range(coeff_ref.shape[0] // 2):
-            slab = 2 * g + side
-            fetch = pltpu.make_async_copy(far_ref.at[slab], coeff_ref.at[slab], sems.at[i, g])
+    fetch_picks = pltpu.make_async_copy(picks_far, picks_ref, picks_sem)
+    fetch_picks.start()
+    for i, (near, side) in enumerate([(theirs_ref, 1 - core), (mine_ref, core)]):
+        for g in range(groups):
+            fetch = pltpu.make_async_copy(far_ref.at[2 * g + side], near.at[g], sems.at[i, g])
             fetch.start()
             fetches[i].append(fetch)
     across, along, rows, steps = hist_ref.shape
@@ -101,59 +119,78 @@
     for base in range(0, sources, 8):
         tile = jnp.zeros((8, 128), jnp.int32)
         for i in range(8):
-            codes = hist_ref[(base + i) % across, (base + i) // across, modes : modes + CODE_ROWS, :].astype(jnp.int32)[:8]
+            s = base + i
+            codes = hist_ref[s % across, s // across, modes : modes + CODE_ROWS, :].astype(jnp.int32)[:8]
             tile = jnp.where(sub == i, codes, tile)
         tiles.append(tile)
     scales = code_scale(jnp.concatenate(tiles, axis=0).astype(jnp.float32))
     scales = jnp.concatenate([scales, jnp.zeros((128 - sources, 128), jnp.float32)], axis=0).T
     for s in range(sources):
-        value = hist_ref[s % across, s // across, :modes, :].astype(jnp.int32).astype(jnp.float32) * scales[:modes, s : s + 1]
+        value = hist_ref[s % across, s // across, :modes, :].astype(jnp.int32).astype(jnp.float32)
+        value = value * scales[:modes, s : s + 1]
         high = value.astype(jnp.bfloat16)
         low = (value - high.astype(jnp.float32)).astype(jnp.bfloat16)
         split_ref[s * modes : (s + 1) * modes, :steps] = high
         split_ref[s * modes : (s + 1) * modes, steps:] = low
-    slabs, per_slab, picked, height, width = coeff_ref.shape
-    core = core_ref[0]
-    for i, (ref, side) in enumerate([(other_ref, 1 - core), (own_ref, core)]):
-        for g in range(slabs // 2):
-            slab = 2 * g + side
-            fetches[i][g].wait()
-            for r in range(per_slab):
-                left = jnp.concatenate([coeff_ref[slab, r, k] for k in range(picked)], axis=1)
-                starts = [pl.multiple_of(picks_ref[k, slab * per_slab + r] * width, width) for k in range(picked)]
-                right = jnp.concatenate([split_ref[pl.ds(start, width), :] for start in starts], axis=0)
-                both = jnp.dot(left, right, preferred_element_type=jnp.float32)
-                ref[g, r * height : (r + 1) * height, :] = both[:, :steps] + both[:, steps:]
-
-
-def recover(hist, coeff_blocks, picks, core, groups):
+    fetch_picks.wait()
+    product(picks_ref, 1 - core, theirs_ref, split_ref, other_ref, fetches[0])
+    for fetch in fetches[1]:
+        fetch.wait()
+
+
+def second_kernel(split_ref, mine_ref, plane_ref, picks_far, own_ref, coeffs_ref, picks_ref, rows_ref, picks_sem):
+    fetch_picks = pltpu.make_async_copy(picks_far, picks_ref, picks_sem)
+    fetch_picks.start()
+    coeffs_ref[...] = plane_columns(plane_ref[...], rows_ref)
+    fetch_picks.wait()
+    product(picks_ref, lax.axis_index("core"), mine_ref, split_ref, own_ref, [])
+
+
+def far(x):
+    return pltpu.with_memory_space_constraint(x, pltpu.HBM)
+
+
+def recover(hist, coeff_blocks, picks, planes, groups):
     across, along, rows, steps = hist.shape
     blocks, picked, height, width = coeff_blocks.shape
     slabs = coeff_blocks.reshape(groups, blocks // groups, picked, height, width)
     half = jax.ShapeDtypeStruct((groups // 2, blocks // groups * height, steps), jnp.float32)
-    return pl.pallas_call(
-        recover_kernel,
-        out_shape=(half, half),
-        in_specs=[
-            pl.BlockSpec(memory_space=pltpu.SMEM),
-            pl.BlockSpec(memory_space=pltpu.SMEM),
-            pl.BlockSpec(memory_space=pltpu.VMEM),
-            pl.BlockSpec(memory_space=pl.ANY),
-        ],
-        out_specs=(pl.BlockSpec(memory_space=pltpu.VMEM),) * 2,
-        scratch_shapes=[
-            pltpu.VMEM((across * along * (rows - CODE_ROWS), 2 * steps), jnp.bfloat16),
-            pltpu.VMEM(slabs.shape, jnp.bfloat16),
-            pltpu.SemaphoreType.DMA((2, groups // 2)),
-        ],
+    half_slabs = (groups // 2,) + slabs.shape[1:]
+    cost = pl.CostEstimate(
+        flops=2 * blocks * picked * height * width * steps,
+        bytes_accessed=blocks * picked * height * width,
+        transcendentals=0,
+    )
+    near, away = pl.BlockSpec(memory_space=pltpu.VMEM), pl.BlockSpec(memory_space=pl.ANY)
+    scratch = [pltpu.SMEM(picks.shape, picks.dtype)]
+    other, split, mine = pl.pallas_call(
+        first_kernel,
+        out_shape=(
+            half,
+            jax.ShapeDtypeStruct((across * along * (rows - CODE_ROWS), 2 * steps), jnp.bfloat16),
+            jax.ShapeDtypeStruct(half_slabs, slabs.dtype),
+        ),
+        in_specs=[near, away, away],
+        out_specs=(near,) * 3,
+        scratch_shapes=[pltpu.VMEM(half_slabs, slabs.dtype)]
+        + scratch
+        + [pltpu.SemaphoreType.DMA((2, groups // 2)), pltpu.SemaphoreType.DMA],
         compiler_params=pltpu.CompilerParams(vmem_limit_bytes=24 << 20),
-        cost_estimate=pl.CostEstimate(
-            flops=4 * blocks * picked * height * width * steps,
-            bytes_accessed=2 * blocks * picked * height * width,
-            transcendentals=0,
-        ),
-        name="recover",
-    )(picks, core, hist, pltpu.with_memory_space_constraint(slabs, pltpu.HBM))
+        cost_estimate=cost,
+        name="first",
+    )(hist, far(picks), far(slabs))
+    come = lax.ppermute(other, "core", [(0, 1), (1, 0)])
+    own, coeffs = pl.pallas_call(
+        second_kernel,
+        out_shape=(half, jax.ShapeDtypeStruct((planes.shape[1], 128), jnp.float32)),
+        in_specs=[near, near, near, away],
+        out_specs=(near,) * 2,
+        scratch_shapes=scratch + [pltpu.VMEM((128, 128), jnp.float32), pltpu.SemaphoreType.DMA],
+        compiler_params=pltpu.CompilerParams(vmem_limit_bytes=24 << 20),
+        cost_estimate=cost,
+        name="second",
+    )(split, mine, planes, far(picks))
+    return own, come, coeffs
 
 
 def pack_kernel(own_ref, come_ref, out_ref):
@@ -212,7 +249,7 @@
     return rows_ref[...].T[:elements]
 
 
-def range_kernel(parts_ref, plane_ref, stress_ref, range_ref, rows_ref):
+def range_kernel(parts_ref, coeffs_ref, far_ref, range_ref, stress_ref, sem):
     groups, rows, steps = parts_ref.shape
     rows -= CODE_ROWS
     codes = [parts_ref[g, rows:, :].astype(jnp.int32).astype(jnp.float32) for g in range(groups)]
@@ -230,9 +267,11 @@
     components, elements, steps = stress_ref.shape
     stress = jnp.concatenate(pieces, axis=0).reshape(components, elements, steps)
     stress_ref[...] = stress
+    leave = pltpu.make_async_copy(stress_ref, far_ref, sem)
+    leave.start()
     looked = range_ref.shape[0]
     lane = lax.broadcasted_iota(jnp.int32, (elements, 128), 1)
-    coeffs = plane_columns(plane_ref[...], rows_ref)
+    coeffs = coeffs_ref[...]
     result = jnp.zeros((elements, 128), jnp.float32)
     for p in range(looked):
         normal = coeffs[:, p : p + 1] * stress[0]
@@ -242,24 +281,26 @@
         spread = jnp.max(normal, axis=-1, keepdims=True) - jnp.min(normal, axis=-1, keepdims=True)
         result = jnp.where(lane == p, spread, result)
     range_ref[...] = result.T[:looked, :]
-
-
-def finish(parts, planes):
+    leave.wait()
+
+
+def finish(parts, coeffs, looked):
     groups, rows, steps = parts.shape
     rows -= CODE_ROWS
-    looked, elements = planes.shape
+    elements = coeffs.shape[0]
+    stress_shape = (rows // elements, elements, steps)
     stress, ranges = pl.pallas_call(
         range_kernel,
         out_shape=(
-            jax.ShapeDtypeStruct((rows // elements, elements, steps), jnp.float32),
+            jax.ShapeDtypeStruct(stress_shape, jnp.float32),
             jax.ShapeDtypeStruct((looked, elements), jnp.float32),
         ),
         in_specs=[pl.BlockSpec(memory_space=pltpu.VMEM)] * 2,
-        out_specs=(pl.BlockSpec(memory_space=pltpu.VMEM),) * 2,
-        scratch_shapes=[pltpu.VMEM((128, 128), jnp.float32)],
+        out_specs=(pl.BlockSpec(memory_space=pl.ANY), pl.BlockSpec(memory_space=pltpu.VMEM)),
+        scratch_shapes=[pltpu.VMEM(stress_shape, jnp.float32), pltpu.SemaphoreType.DMA],
         compiler_params=pltpu.CompilerParams(vmem_limit_bytes=8 << 20),
         name="ranges",
-    )(parts, planes)
+    )(parts, coeffs)
     return stress, ranges.T
 
 
@@ -268,73 +309,73 @@
     return lax.all_to_all(copies, axes, 0, 0)
 
 
-def stage_kernel(core_ref, owner_ref, whole_ref, *refs):
-    count = (len(refs) - 3) // 2
-    far, (half_ref, *near, same_ref, sems) = refs[:count], refs[count:]
+def stage_kernel(owner_far, whole_ref, *refs):
+    count = (len(refs) - 4) // 2
+    away, (half_ref, *near, tile_ref, owner_ref, sems) = refs[:count], refs[count:]
     rows = half_ref.shape[0]
-    start = pl.multiple_of(core_ref[0] * rows, rows)
-    fetches = [pltpu.make_async_copy(whole_ref.at[pl.ds(start, rows)], half_ref, sems.at[count])]
-    fetches += [pltpu.make_async_copy(a, b, sems.at[i]) for i, (a, b) in enumerate(zip(far, near))]
+    start = pl.multiple_of(lax.axis_index("core") * rows, rows)
+    fetches = [pltpu.make_async_copy(owner_far, owner_ref, sems.at[count + 1])]
+    fetches += [pltpu.make_async_copy(whole_ref.at[pl.ds(start, rows)], half_ref, sems.at[count])]
+    fetches += [pltpu.make_async_copy(a, b, sems.at[i]) for i, (a, b) in enumerate(zip(away, near))]
     for fetch in fetches:
         fetch.start()
-    same_ref[0] = owner_ref[0]
     for fetch in fetches:
         fetch.wait()
-
-
-def stage(whole, core, owner, *others):
+    tile_ref[...] = jnp.full(tile_ref.shape, owner_ref[0], jnp.int32)
+
+
+def stage(owner, whole, *others):
     channels, steps = whole.shape
     copied = [jax.ShapeDtypeStruct((channels // 2, steps), whole.dtype)]
     copied += [jax.ShapeDtypeStruct(x.shape, x.dtype) for x in others]
     return pl.pallas_call(
         stage_kernel,
-        out_shape=(*copied, jax.ShapeDtypeStruct(owner.shape, owner.dtype)),
-        in_specs=[pl.BlockSpec(memory_space=pltpu.SMEM)] * 2 + [pl.BlockSpec(memory_space=pl.ANY)] * len(copied),
-        out_specs=(pl.BlockSpec(memory_space=pltpu.VMEM),) * len(copied) + (pl.BlockSpec(memory_space=pltpu.SMEM),),
-        scratch_shapes=[pltpu.SemaphoreType.DMA((len(copied),))],
+        out_shape=(*copied, jax.ShapeDtypeStruct((8, 128), jnp.int32)),
+        in_specs=[pl.BlockSpec(memory_space=pl.ANY)] * (1 + len(copied)),
+        out_specs=(pl.BlockSpec(memory_space=pltpu.VMEM),) * (1 + len(copied)),
+        scratch_shapes=[pltpu.SMEM(owner.shape, jnp.int32), pltpu.SemaphoreType.DMA((len(copied) + 1,))],
         compiler_params=pltpu.CompilerParams(vmem_limit_bytes=8 << 20),
         name="stage",
-    )(core, owner, *(pltpu.with_memory_space_constraint(x, pltpu.HBM) for x in (whole, *others)))
-
-
-def pick_kernel(owner_ref, offered_ref, out_ref):
-    piece = offered_ref[owner_ref[0]]
+    )(owner, *(far(x) for x in (whole, *others)))
+
+
+def pick_kernel(tile_ref, offered_ref, out_ref):
+    piece = offered_ref[jnp.max(tile_ref[...])]
     for i in range(out_ref.shape[0]):
         out_ref[i] = piece
 
 
-def pick_piece(offered, owner):
+def pick_piece(offered, tile):
     return pl.pallas_call(
         pick_kernel,
         out_shape=jax.ShapeDtypeStruct(offered.shape, offered.dtype),
-        in_specs=[pl.BlockSpec(memory_space=pltpu.SMEM), pl.BlockSpec(memory_space=pltpu.VMEM)],
+        in_specs=[pl.BlockSpec(memory_space=pltpu.VMEM)] * 2,
         out_specs=pl.BlockSpec(memory_space=pltpu.VMEM),
         compiler_params=pltpu.CompilerParams(vmem_limit_bytes=8 << 20),
         name="pick",
-    )(owner, offered)
-
-
-def fetch_window(half, owner):
+    )(tile, offered)
+
+
+def fetch_window(half, tile):
     count = lax.axis_size(ROW)
     pieces = half.reshape(count, half.shape[0] // count, half.shape[1])
     offered = lax.all_to_all(pieces, ROW, 0, 0)
-    whole_half = lax.all_to_all(pick_piece(offered, owner), ROW, 0, 0).reshape(half.shape)
+    whole_half = lax.all_to_all(pick_piece(offered, tile), ROW, 0, 0).reshape(half.shape)
     return lax.all_gather(whole_half, "core", axis=0, tiled=True)
 
 
 def body(load_windows, owner_id, participation, frequency, damping, recovery, pattern, plane_table):
-    core = lax.axis_index("core")[None].astype(jnp.int32)
-    half, part, rates, decays, owner = stage(
-        load_windows[0], core, owner_id, participation, frequency[None], damping[None]
+    planes = plane_table[0, 0].T
+    half, part, rates, decays, planes, tile = stage(
+        owner_id, load_windows[0], participation, frequency[None], damping[None], planes
     )
-    window = fetch_window(half, owner)
+    window = fetch_window(half, tile)
     copies = make_history(window, part, rates, decays, lax.axis_size(ROW[:2]))
     column = lax.all_to_all(copies, ROW[:2], 0, 0)
     hist = gather_over(column, ROW[2])
-    own, other = recover(hist, recovery[0, 0], pattern[0, 0].T, core, lax.axis_size(("yh", "core")))
-    come = lax.ppermute(other, "core", [(0, 1), (1, 0)])
+    own, come, coeffs = recover(hist, recovery[0, 0], pattern[0, 0].T, planes, lax.axis_size(("yh", "core")))
     parts = lax.all_to_all(pack_sums(own, come), "yh", 0, 0)
-    stress, plane_range = finish(parts, plane_table[0, 0].T)
+    stress, plane_range = finish(parts, coeffs, planes.shape[0])
     return (stress[None, None], plane_range[None, None])
 
 

time: 113 us -> 110 us (0.973)
  waiting for transfers between devices: 2.25 us -> 0.94 us
  Pallas kernels: 10.5 us -> 9.32 us
    ppermute x1, waiting for transfers between devices: 2.25 us -> 0.94 us  [recover(): come = lax.ppermute(other, 'core', [(0, 1), (1, 0)])]
    pallas_call x3 -> x4, Pallas kernels: 7.86 us -> 7.2 us  [the longest x1 2.49 us: finish(): pl.pallas_call(range_kernel, out_shape=(jax.ShapeDtypeStruct(stress_shape...]
  transfers between devices with their start and end apart: 1 -> 1, of which waited for: 1 -> 1; matrix products, arithmetic and copies ran while one was open for 0% -> 0% of each run, Pallas kernels for 0% -> 1%
where the time goes in v6:
time: 110 us
  blocking collectives  96.3 us (88%)
  Pallas kernels  9.32 us (8%)
  starting transfers between devices  1.92 us (2%)
  between operations  1.33 us (1%)
    all_to_all x1, blocking collectives, fetch_window(): offered = lax.all_to_all(pieces, ROW, 0, 0)  27.7 us
    all_to_all x1, blocking collectives, body(): parts = lax.all_to_all(pack_sums(own, come), 'yh', 0, 0)  19 us
    all_to_all x1, blocking collectives, fetch_window(): lax.all_to_all(pick_piece(offered, tile), ROW, 0, 0).reshape(half.shape)  17.6 us
    all_to_all x1, blocking collectives, gather_over(): return lax.all_to_all(copies, axes, 0, 0)  15.9 us
    all_to_all x1, blocking collectives, body(): column = lax.all_to_all(copies, ROW[:2], 0, 0)  14 us
    pallas_call x1, Pallas kernels, finish(): pl.pallas_call(range_kernel, out_shape=(jax.ShapeDtypeStruct(stress_shape...  2.49 us
    pallas_call x1, Pallas kernels, recover(): pl.pallas_call(first_kernel, out_shape=(half, jax.ShapeDtypeStruct((acros...  2.33 us
  transfers between devices with their start and end apart: 1, of which 1 were waited for; matrix products, arithmetic and copies ran while one was open for 0% of the time, Pallas kernels for 1%

profile of v6, /device:TPU:8, one launch (start us, length us, event | category | flops | bytes accessed | tf_op | source)
XLA Modules:
  0.0 110.0 jit_solution(9868060376989312478)
XLA Ops:
  1.3 1.1 stage.1
  2.4 27.7 %all_to_all.25.offered_ref = bf16[64,16,128]{2,1,0:T(8,128)(2,1)S(1)} all-to-all(bf16[64,16,128]{2,1,0:T(8,128)(2,1)S(1)} %bitcast.16), channel_id=1, replica_groups=mesh['yh'=4,'core'=2,'z'=8,'yl'=2,'x'=4] {'z','yl','x'}, dimensions={0} | all-to-all | bytes 524288 | tf_op jit(solution)/shard_map/all_to_all | solution.py:362
  30.0 0.2 pick.1
  30.3 17.6 %all_to_all.26 = bf16[64,16,128]{2,1,0:T(8,128)(2,1)S(1)} all-to-all(bf16[64,16,128]{2,1,0:T(8,128)(2,1)S(1)} %pick.1), channel_id=1, replica_groups=mesh['yh'=4,'core'=2,'z'=8,'yl'=2,'x'=4] {'z','yl','x'}, dimensions={0} | all-to-all | bytes 524288 | tf_op jit(solution)/shard_map/all_to_all | solution.py:363
  47.8 2.2 %all_gather.3.window_ref = bf16[2048,128]{1,0:T(8,128)(2,1)S(1)} all-gather(bf16[1024,128]{1,0:T(8,128)(2,1)S(1)} %bitcast.18), channel_id=1, replica_groups=mesh['yh'=4,'core'=2,'z'=8,'yl'=2,'x'=4] {'core'}, dimensions={0}, use_global_device_ids=true | all-gather | bytes 786432 | tf_op jit(solution)/shard_map/all_gather | solution.py:364
  50.0 0.9 history.1
  50.9 14.0 %all_to_all.27 = s16[16,56,128]{2,1,0:T(8,128)(2,1)S(1)} all-to-all(s16[16,56,128]{2,1,0:T(8,128)(2,1)S(1)} %history.1), channel_id=1, replica_groups=mesh['yh'=4,'core'=2,'z'=8,'yl'=2,'x'=4] {'z','yl'}, dimensions={0} | all-to-all | bytes 458752 | tf_op jit(solution)/shard_map/all_to_all | solution.py:374
  64.9 0.1 broadcast_in_dim.20
  65.0 15.9 %all_to_all.28.hist_ref = s16[4,16,56,128]{3,2,1,0:T(8,128)(2,1)S(1)} all-to-all(s16[4,16,56,128]{3,2,1,0:T(8,128)(2,1)S(1)} %broadcast_in_dim.20), channel_id=1, replica_groups=mesh['yh'=4,'core'=2,'z'=8,'yl'=2,'x'=4] {'x'}, dimensions={0} | all-to-all | bytes 1835008 | tf_op jit(solution)/shard_map/all_to_all | solution.py:309
  80.9 2.3 %first.1 = (f32[4,384,128]{2,1,0:T(8,128)S(1)}, bf16[3072,256]{1,0:T(8,128)(2,1)S(1)}, bf16[4,3,4,128,128]{4,3,2,1,0:T(8,128)(2,1)S(1)}) custom-call(s16[4,16,56,128]{3,2,1,0:T(8,128)(2,1)S(1)} %all_to_all.28.hist_ref, s32[4,24]{1,0:T(4,128)} %bitcast.20, bf16[8,3,4,128,128]{4,3,2,1,0:T(8,128)(2,1)} %bitcast.17), custom_call_target="tpu_custom_call" | custom-call | flops 402653184 | bytes 1572864 | tf_op jit(solution)/shard_map/first/pallas_call | solution.py:166
  83.3 1.9 %collective-permute-start = (f32[4,384,128]{2,1,0:T(8,128)S(1)}, f32[4,384,128]{2,1,0:T(8,128)S(1)}, u32[]{:S(2)}, u32[]{:S(2)}) collective-permute-start(f32[4,384,128]{2,1,0:T(8,128)S(1)} %get-tuple-element.24), channel_id=1, source_target_pairs={{0,64},{64,0},{1,65},{65,1},{2,66},{66,2},{3,67},{67,3},{4,68},{68... | collective-permute-start | bytes 2359304 | tf_op jit(solution)/shard_map/ppermute | solution.py:182
  85.2 1.3 %second.1 = (f32[4,384,128]{2,1,0:T(8,128)S(1)}, f32[64,128]{1,0:T(8,128)S(1)}) custom-call(bf16[3072,256]{1,0:T(8,128)(2,1)S(1)} %get-tuple-element.20.split_ref, bf16[4,3,4,128,128]{4,3,2,1,0:T(8,128)(2,1)S(1)} %get-tuple-element.21.mine_ref, s32[8,64]{1,0:T(8,128)S(1)} %get-tuple-element.22.plane_ref, s32[4,24]{1,0:T(4,128)} %bitcast.21), custom_call_target="tpu_custom_call" | custom-call | flops 402653184 | bytes 1572864 | tf_op jit(solution)/shard_map/second/pallas_call | solution.py:183
  86.5 0.9 collective-permute-done.come_ref
  87.5 1.0 pack.1
  88.5 19.0 %all_to_all.29.parts_ref = s16[4,392,128]{2,1,0:T(8,128)(2,1)S(1)} all-to-all(s16[4,392,128]{2,1,0:T(8,128)(2,1)S(1)} %pack.1), channel_id=1, replica_groups=mesh['yh'=4,'core'=2,'z'=8,'yl'=2,'x'=4] {'yh'}, dimensions={0} | all-to-all | bytes 802816 | tf_op jit(solution)/shard_map/all_to_all | solution.py:377
  107.5 2.5 %ranges.1 = (f32[6,64,128]{2,1,0:T(8,128)}, f32[8,64]{1,0:T(8,128)}) custom-call(s16[4,392,128]{2,1,0:T(8,128)(2,1)S(1)} %all_to_all.29.parts_ref, f32[64,128]{1,0:T(8,128)S(1)} %get-tuple-element.25.coeffs_ref), custom_call_target="tpu_custom_call" | custom-call | tf_op jit(solution)/shard_map/ranges/pallas_call | solution.py:292
Async XLA Ops:
  83.3 4.2 %collective-permute-start = (f32[4,384,128]{2,1,0:T(8,128)S(1)}, f32[4,384,128]{2,1,0:T(8,128)S(1)}, u32[]{:S(2)}, u32[]{:S(2)}) collective-permute-start(f32[4,384,128]{2,1,0:T(8,128)S(1)} %get-tuple-element.24), channel_id=1, source_target_pairs={{0,64},{64,0},{1,65},{65,1},{2,66},{66,2},{3,67},{67,3},{4,68},{68... | collective-permute-start | bytes 2359304 | tf_op jit(solution)/shard_map/ppermute | solution.py:182

commit v7 on v6

--- a/solution.py
+++ b/solution.py
@@ -141,7 +141,7 @@
 def second_kernel(split_ref, mine_ref, plane_ref, picks_far, own_ref, coeffs_ref, picks_ref, rows_ref, picks_sem):
     fetch_picks = pltpu.make_async_copy(picks_far, picks_ref, picks_sem)
     fetch_picks.start()
-    coeffs_ref[...] = plane_columns(plane_ref[...], rows_ref)
+    plane_rows(plane_ref[...], rows_ref, coeffs_ref)
     fetch_picks.wait()
     product(picks_ref, lax.axis_index("core"), mine_ref, split_ref, own_ref, [])
 
@@ -182,10 +182,10 @@
     come = lax.ppermute(other, "core", [(0, 1), (1, 0)])
     own, coeffs = pl.pallas_call(
         second_kernel,
-        out_shape=(half, jax.ShapeDtypeStruct((planes.shape[1], 128), jnp.float32)),
+        out_shape=(half, jax.ShapeDtypeStruct((6 * planes.shape[0], 128), jnp.float32)),
         in_specs=[near, near, near, away],
         out_specs=(near,) * 2,
-        scratch_shapes=scratch + [pltpu.VMEM((128, 128), jnp.float32), pltpu.SemaphoreType.DMA],
+        scratch_shapes=scratch + [pltpu.VMEM((6 * planes.shape[0], 128), jnp.float32), pltpu.SemaphoreType.DMA],
         compiler_params=pltpu.CompilerParams(vmem_limit_bytes=24 << 20),
         cost_estimate=cost,
         name="second",
@@ -197,22 +197,19 @@
     groups, rows, steps = out_ref.shape
     rows -= CODE_ROWS
     tiles = rows // 128
-    at = lax.broadcasted_iota(jnp.int32, (128, 128), 0) == lax.broadcasted_iota(jnp.int32, (128, 128), 1)
     for g in range(groups):
         sums, largest = [], []
         for i in range(tiles):
             here = pl.ds(i * 128, 128)
-            pair = own_ref[g, here, :] + come_ref[g, here, :]
-            top = jnp.max(jnp.abs(pair), axis=-1, keepdims=True)
-            sums.append(pair)
-            largest.append(jnp.sum(jnp.where(at, top, 0.0), axis=0, keepdims=True))
+            turned = (own_ref[g, here, :] + come_ref[g, here, :]).T
+            sums.append(turned)
+            largest.append(jnp.max(jnp.abs(turned), axis=0, keepdims=True))
         largest.append(jnp.zeros((8 - tiles, 128), jnp.float32))
         code = jnp.ceil(jnp.log2(jnp.maximum(jnp.concatenate(largest, axis=0), 1e-30)) * 32.0)
         out_ref[g, rows:, :] = code.astype(jnp.int32).astype(jnp.int16)
         inverse = jnp.exp2(code * (-1.0 / 32.0)) * LEVELS
-        inverse = jnp.concatenate([inverse, jnp.zeros((120, 128), jnp.float32)], axis=0).T
         for i in range(tiles):
-            whole = jnp.round(sums[i] * inverse[:, i : i + 1])
+            whole = jnp.round(sums[i] * inverse[i : i + 1])
             out_ref[g, i * 128 : (i + 1) * 128, :] = whole.astype(jnp.int32).astype(jnp.int16)
 
 
@@ -228,7 +225,7 @@
     )(own, come)
 
 
-def plane_columns(planes, rows_ref):
+def plane_rows(planes, pad_ref, out_ref):
     looked, elements = planes.shape
     index = planes.astype(jnp.float32)
     height = (index + 0.5) * (1.0 / PLANES)
@@ -244,60 +241,58 @@
         2.0 * normal_y * height,
         2.0 * normal_x * height,
     ]
+    pad_ref[...] = jnp.zeros_like(pad_ref)
+    lane = lax.broadcasted_iota(jnp.int32, (looked, 128), 1)
     for q, coeff in enumerate(coeffs):
-        rows_ref[q * looked : (q + 1) * looked, :elements] = coeff
-    return rows_ref[...].T[:elements]
-
-
-def range_kernel(parts_ref, coeffs_ref, far_ref, range_ref, stress_ref, sem):
+        pad_ref[q * looked : (q + 1) * looked, :elements] = coeff
+        left = pad_ref[q * looked : (q + 1) * looked, :]
+        right = pltpu.roll(pltpu.roll(left, elements, 1), looked // 2, 0)
+        out_ref[q * looked : (q + 1) * looked, :] = jnp.where(lane < elements, left, right)
+
+
+def range_kernel(parts_ref, coeffs_ref, stress_ref, range_ref):
     groups, rows, steps = parts_ref.shape
     rows -= CODE_ROWS
-    codes = [parts_ref[g, rows:, :].astype(jnp.int32).astype(jnp.float32) for g in range(groups)]
-    scales = code_scale(jnp.concatenate(codes, axis=0))
-    scales = jnp.concatenate([scales, jnp.zeros((128 - groups * CODE_ROWS, 128), jnp.float32)], axis=0).T
-    pieces = []
+    components, elements, steps = stress_ref.shape
+    looked = range_ref.shape[0]
+    scales = [code_scale(parts_ref[g, rows:, :].astype(jnp.int32).astype(jnp.float32)) for g in range(groups)]
+    low = lax.broadcasted_iota(jnp.int32, (steps, 128), 1) < elements
+    twice = []
     for i in range(rows // 128):
-        piece = None
+        total = None
         for g in range(groups):
             value = parts_ref[g, i * 128 : (i + 1) * 128, :].astype(jnp.int32).astype(jnp.float32)
-            at = g * CODE_ROWS + i
-            value = value * scales[:, at : at + 1]
-            piece = value if piece is None else piece + value
-        pieces.append(piece)
-    components, elements, steps = stress_ref.shape
-    stress = jnp.concatenate(pieces, axis=0).reshape(components, elements, steps)
-    stress_ref[...] = stress
-    leave = pltpu.make_async_copy(stress_ref, far_ref, sem)
-    leave.start()
-    looked = range_ref.shape[0]
-    lane = lax.broadcasted_iota(jnp.int32, (elements, 128), 1)
-    coeffs = coeffs_ref[...]
-    result = jnp.zeros((elements, 128), jnp.float32)
-    for p in range(looked):
-        normal = coeffs[:, p : p + 1] * stress[0]
+            value = value * scales[g][i : i + 1]
+            total = value if total is None else total + value
+        upright = total.T
+        stress_ref[2 * i] = upright[:elements]
+        stress_ref[2 * i + 1] = upright[elements:]
+        swapped = pltpu.roll(total, elements, 1)
+        twice.append(jnp.where(low, total, swapped))
+        twice.append(jnp.where(low, swapped, total))
+    spreads = []
+    for k in range(looked // 2):
+        normal = coeffs_ref[k : k + 1, :] * twice[0]
         for q in range(1, components):
-            at = q * looked + p
-            normal = normal + coeffs[:, at : at + 1] * stress[q]
-        spread = jnp.max(normal, axis=-1, keepdims=True) - jnp.min(normal, axis=-1, keepdims=True)
-        result = jnp.where(lane == p, spread, result)
-    range_ref[...] = result.T[:looked, :]
-    leave.wait()
+            normal = normal + coeffs_ref[q * looked + k : q * looked + k + 1, :] * twice[q]
+        spreads.append(jnp.max(normal, axis=0, keepdims=True) - jnp.min(normal, axis=0, keepdims=True))
+    spread = jnp.concatenate(spreads + spreads, axis=0)
+    first = lax.broadcasted_iota(jnp.int32, (looked, 128), 0) < looked // 2
+    range_ref[...] = jnp.where(first, spread, pltpu.roll(spread, elements, 1))[:, :elements]
 
 
 def finish(parts, coeffs, looked):
     groups, rows, steps = parts.shape
     rows -= CODE_ROWS
-    elements = coeffs.shape[0]
-    stress_shape = (rows // elements, elements, steps)
+    elements = 128 // 2
     stress, ranges = pl.pallas_call(
         range_kernel,
         out_shape=(
-            jax.ShapeDtypeStruct(stress_shape, jnp.float32),
+            jax.ShapeDtypeStruct((rows // elements, elements, steps), jnp.float32),
             jax.ShapeDtypeStruct((looked, elements), jnp.float32),
         ),
         in_specs=[pl.BlockSpec(memory_space=pltpu.VMEM)] * 2,
-        out_specs=(pl.BlockSpec(memory_space=pl.ANY), pl.BlockSpec(memory_space=pltpu.VMEM)),
-        scratch_shapes=[pltpu.VMEM(stress_shape, jnp.float32), pltpu.SemaphoreType.DMA],
+        out_specs=(pl.BlockSpec(memory_space=pltpu.VMEM),) * 2,
         compiler_params=pltpu.CompilerParams(vmem_limit_bytes=8 << 20),
         name="ranges",
     )(parts, coeffs)
@@ -309,19 +304,18 @@
     return lax.all_to_all(copies, axes, 0, 0)
 
 
-def stage_kernel(owner_far, whole_ref, *refs):
-    count = (len(refs) - 4) // 2
-    away, (half_ref, *near, tile_ref, owner_ref, sems) = refs[:count], refs[count:]
+def stage_kernel(owner_ref, whole_ref, *refs):
+    count = (len(refs) - 3) // 2
+    away, (half_ref, *near, tile_ref, sems) = refs[:count], refs[count:]
     rows = half_ref.shape[0]
     start = pl.multiple_of(lax.axis_index("core") * rows, rows)
-    fetches = [pltpu.make_async_copy(owner_far, owner_ref, sems.at[count + 1])]
-    fetches += [pltpu.make_async_copy(whole_ref.at[pl.ds(start, rows)], half_ref, sems.at[count])]
+    fetches = [pltpu.make_async_copy(whole_ref.at[pl.ds(start, rows)], half_ref, sems.at[count])]
     fetches += [pltpu.make_async_copy(a, b, sems.at[i]) for i, (a, b) in enumerate(zip(away, near))]
     for fetch in fetches:
         fetch.start()
+    tile_ref[...] = jnp.full(tile_ref.shape, owner_ref[0], jnp.int32)
     for fetch in fetches:
         fetch.wait()
-    tile_ref[...] = jnp.full(tile_ref.shape, owner_ref[0], jnp.int32)
 
 
 def stage(owner, whole, *others):
@@ -331,9 +325,9 @@
     return pl.pallas_call(
         stage_kernel,
         out_shape=(*copied, jax.ShapeDtypeStruct((8, 128), jnp.int32)),
-        in_specs=[pl.BlockSpec(memory_space=pl.ANY)] * (1 + len(copied)),
+        in_specs=[pl.BlockSpec(memory_space=pltpu.SMEM)] + [pl.BlockSpec(memory_space=pl.ANY)] * len(copied),
         out_specs=(pl.BlockSpec(memory_space=pltpu.VMEM),) * (1 + len(copied)),
-        scratch_shapes=[pltpu.SMEM(owner.shape, jnp.int32), pltpu.SemaphoreType.DMA((len(copied) + 1,))],
+        scratch_shapes=[pltpu.SemaphoreType.DMA((len(copied),))],
         compiler_params=pltpu.CompilerParams(vmem_limit_bytes=8 << 20),
         name="stage",
     )(owner, *(far(x) for x in (whole, *others)))

time: 110 us -> 108 us (0.982)
  Pallas kernels: 9.32 us -> 7.09 us
    pallas_call x2, Pallas kernels: 3.79 us -> 2.24 us  [the longest x1 1.31 us: recover(): pl.pallas_call(second_kernel, out_shape=(half, jax.ShapeDtypeStruct((6 *...]
where the time goes in v7:
time: 108 us
  blocking collectives  96.3 us (89%)
  Pallas kernels  7.09 us (7%)
  starting transfers between devices  1.92 us (2%)
  between operations  1.34 us (1%)
    all_to_all x1, blocking collectives, fetch_window(): offered = lax.all_to_all(pieces, ROW, 0, 0)  27.7 us
    all_to_all x1, blocking collectives, body(): parts = lax.all_to_all(pack_sums(own, come), 'yh', 0, 0)  19 us
    all_to_all x1, blocking collectives, fetch_window(): lax.all_to_all(pick_piece(offered, tile), ROW, 0, 0).reshape(half.shape)  17.6 us
    all_to_all x1, blocking collectives, gather_over(): return lax.all_to_all(copies, axes, 0, 0)  15.9 us
    all_to_all x1, blocking collectives, body(): column = lax.all_to_all(copies, ROW[:2], 0, 0)  14 us
    pallas_call x1, Pallas kernels, recover(): pl.pallas_call(first_kernel, out_shape=(half, jax.ShapeDtypeStruct((acros...  2.33 us
    all_gather x1, blocking collectives, fetch_window(): return lax.all_gather(whole_half, 'core', axis=0, tiled=True)  2.17 us
  transfers between devices with their start and end apart: 1, of which 1 were waited for; matrix products, arithmetic and copies ran while one was open for 0% of the time, Pallas kernels for 1%

profile of v7, /device:TPU:8, one launch (start us, length us, event | category | flops | bytes accessed | tf_op | source)
XLA Modules:
  0.0 107.7 jit_solution(11421516486942959160)
XLA Ops:
  1.3 1.1 stage.1
  2.4 27.7 %all_to_all.25.offered_ref = bf16[64,16,128]{2,1,0:T(8,128)(2,1)S(1)} all-to-all(bf16[64,16,128]{2,1,0:T(8,128)(2,1)S(1)} %bitcast.16), channel_id=1, replica_groups=mesh['yh'=4,'core'=2,'z'=8,'yl'=2,'x'=4] {'z','yl','x'}, dimensions={0} | all-to-all | bytes 524288 | tf_op jit(solution)/shard_map/all_to_all | solution.py:356
  30.0 0.2 pick.1
  30.2 17.6 %all_to_all.26 = bf16[64,16,128]{2,1,0:T(8,128)(2,1)S(1)} all-to-all(bf16[64,16,128]{2,1,0:T(8,128)(2,1)S(1)} %pick.1), channel_id=1, replica_groups=mesh['yh'=4,'core'=2,'z'=8,'yl'=2,'x'=4] {'z','yl','x'}, dimensions={0} | all-to-all | bytes 524288 | tf_op jit(solution)/shard_map/all_to_all | solution.py:357
  47.8 2.2 %all_gather.3.window_ref = bf16[2048,128]{1,0:T(8,128)(2,1)S(1)} all-gather(bf16[1024,128]{1,0:T(8,128)(2,1)S(1)} %bitcast.18), channel_id=1, replica_groups=mesh['yh'=4,'core'=2,'z'=8,'yl'=2,'x'=4] {'core'}, dimensions={0}, use_global_device_ids=true | all-gather | bytes 786432 | tf_op jit(solution)/shard_map/all_gather | solution.py:358
  50.0 0.9 history.1
  50.9 14.0 %all_to_all.27 = s16[16,56,128]{2,1,0:T(8,128)(2,1)S(1)} all-to-all(s16[16,56,128]{2,1,0:T(8,128)(2,1)S(1)} %history.1), channel_id=1, replica_groups=mesh['yh'=4,'core'=2,'z'=8,'yl'=2,'x'=4] {'z','yl'}, dimensions={0} | all-to-all | bytes 458752 | tf_op jit(solution)/shard_map/all_to_all | solution.py:368
  64.9 0.1 broadcast_in_dim.20
  65.0 15.9 %all_to_all.28.hist_ref = s16[4,16,56,128]{3,2,1,0:T(8,128)(2,1)S(1)} all-to-all(s16[4,16,56,128]{3,2,1,0:T(8,128)(2,1)S(1)} %broadcast_in_dim.20), channel_id=1, replica_groups=mesh['yh'=4,'core'=2,'z'=8,'yl'=2,'x'=4] {'x'}, dimensions={0} | all-to-all | bytes 1835008 | tf_op jit(solution)/shard_map/all_to_all | solution.py:304
  80.9 2.3 %first.1 = (f32[4,384,128]{2,1,0:T(8,128)S(1)}, bf16[3072,256]{1,0:T(8,128)(2,1)S(1)}, bf16[4,3,4,128,128]{4,3,2,1,0:T(8,128)(2,1)S(1)}) custom-call(s16[4,16,56,128]{3,2,1,0:T(8,128)(2,1)S(1)} %all_to_all.28.hist_ref, s32[4,24]{1,0:T(4,128)} %bitcast.20, bf16[8,3,4,128,128]{4,3,2,1,0:T(8,128)(2,1)} %bitcast.17), custom_call_target="tpu_custom_call" | custom-call | flops 402653184 | bytes 1572864 | tf_op jit(solution)/shard_map/first/pallas_call | solution.py:166
  83.3 1.9 %collective-permute-start = (f32[4,384,128]{2,1,0:T(8,128)S(1)}, f32[4,384,128]{2,1,0:T(8,128)S(1)}, u32[]{:S(2)}, u32[]{:S(2)}) collective-permute-start(f32[4,384,128]{2,1,0:T(8,128)S(1)} %get-tuple-element.24), channel_id=1, source_target_pairs={{0,64},{64,0},{1,65},{65,1},{2,66},{66,2},{3,67},{67,3},{4,68},{68... | collective-permute-start | bytes 2359304 | tf_op jit(solution)/shard_map/ppermute | solution.py:182
  85.2 1.3 %second.1 = (f32[4,384,128]{2,1,0:T(8,128)S(1)}, f32[48,128]{1,0:T(8,128)S(1)}) custom-call(bf16[3072,256]{1,0:T(8,128)(2,1)S(1)} %get-tuple-element.20.split_ref, bf16[4,3,4,128,128]{4,3,2,1,0:T(8,128)(2,1)S(1)} %get-tuple-element.21.mine_ref, s32[8,64]{1,0:T(8,128)S(1)} %get-tuple-element.22.plane_ref, s32[4,24]{1,0:T(4,128)} %bitcast.21), custom_call_target="tpu_custom_call" | custom-call | flops 402653184 | bytes 1572864 | tf_op jit(solution)/shard_map/second/pallas_call | solution.py:183
  86.5 0.9 collective-permute-done.come_ref
  87.4 0.3 pack.1
  87.8 19.0 %all_to_all.29.parts_ref = s16[4,392,128]{2,1,0:T(8,128)(2,1)S(1)} all-to-all(s16[4,392,128]{2,1,0:T(8,128)(2,1)S(1)} %pack.1), channel_id=1, replica_groups=mesh['yh'=4,'core'=2,'z'=8,'yl'=2,'x'=4] {'yh'}, dimensions={0} | all-to-all | bytes 802816 | tf_op jit(solution)/shard_map/all_to_all | solution.py:371
  106.8 0.9 ranges.1
Async XLA Ops:
  83.3 4.2 %collective-permute-start = (f32[4,384,128]{2,1,0:T(8,128)S(1)}, f32[4,384,128]{2,1,0:T(8,128)S(1)}, u32[]{:S(2)}, u32[]{:S(2)}) collective-permute-start(f32[4,384,128]{2,1,0:T(8,128)S(1)} %get-tuple-element.24), channel_id=1, source_target_pairs={{0,64},{64,0},{1,65},{65,1},{2,66},{66,2},{3,67},{67,3},{4,68},{68... | collective-permute-start | bytes 2359304 | tf_op jit(solution)/shard_map/ppermute | solution.py:182

commit v8 on v7

--- a/solution.py
+++ b/solution.py
@@ -1,3 +1,5 @@
+import functools
+
 import jax
 import jax.numpy as jnp
 from jax import lax
@@ -333,15 +335,16 @@
     )(owner, *(far(x) for x in (whole, *others)))
 
 
-def pick_kernel(tile_ref, offered_ref, out_ref):
-    piece = offered_ref[jnp.max(tile_ref[...])]
+def pick_kernel(shift, tile_ref, offered_ref, out_ref):
+    owner = jnp.max(tile_ref[...])
+    piece = offered_ref[lax.rem(lax.shift_right_logical(owner, shift), offered_ref.shape[0])]
     for i in range(out_ref.shape[0]):
         out_ref[i] = piece
 
 
-def pick_piece(offered, tile):
+def pick_piece(offered, tile, shift):
     return pl.pallas_call(
-        pick_kernel,
+        functools.partial(pick_kernel, shift),
         out_shape=jax.ShapeDtypeStruct(offered.shape, offered.dtype),
         in_specs=[pl.BlockSpec(memory_space=pltpu.VMEM)] * 2,
         out_specs=pl.BlockSpec(memory_space=pltpu.VMEM),
@@ -350,11 +353,14 @@
     )(tile, offered)
 
 
-def fetch_window(half, tile):
-    count = lax.axis_size(ROW)
-    pieces = half.reshape(count, half.shape[0] // count, half.shape[1])
-    offered = lax.all_to_all(pieces, ROW, 0, 0)
-    whole_half = lax.all_to_all(pick_piece(offered, tile), ROW, 0, 0).reshape(half.shape)
+def fetch_window(half, tile, owner):
+    plane = lax.axis_size(ROW[1:])
+    shift = plane.bit_length() - 1
+    pieces = half.reshape(plane, half.shape[0] // plane, half.shape[1])
+    mine = lax.axis_index(ROW[0]) == lax.shift_right_logical(owner, shift)
+    offered = lax.cond(mine, lambda x: lax.all_to_all(x, ROW[1:], 0, 0), lambda x: x, pieces)
+    offered = lax.all_to_all(pick_piece(offered, tile, 0), ROW[0], 0, 0)
+    whole_half = lax.all_to_all(pick_piece(offered, tile, shift), ROW[1:], 0, 0).reshape(half.shape)
     return lax.all_gather(whole_half, "core", axis=0, tiled=True)
 
 
@@ -363,7 +369,7 @@
     half, part, rates, decays, planes, tile = stage(
         owner_id, load_windows[0], participation, frequency[None], damping[None], planes
     )
-    window = fetch_window(half, tile)
+    window = fetch_window(half, tile, owner_id[0])
     copies = make_history(window, part, rates, decays, lax.axis_size(ROW[:2]))
     column = lax.all_to_all(copies, ROW[:2], 0, 0)
     hist = gather_over(column, ROW[2])

time: 108 us -> 98.3 us (0.910)
  blocking collectives: 96.3 us -> 86.2 us
    all_to_all x2 -> x3, blocking collectives: 45.2 us -> 36.7 us  [the longest x1 14.1 us: fetch_window(): lax.all_to_all(x, ROW[1:], 0, 0)]
    all_to_all x1, blocking collectives: 19 us -> 16.6 us  [body(): parts = lax.all_to_all(pack_sums(own, come), 'yh', 0, 0)]
where the time goes in v8:
time: 98.3 us; the launch traced here: 97.9 us
  blocking collectives  86.2 us (88%)
  Pallas kernels  7.32 us (7%)
  starting transfers between devices  1.92 us (2%)
  between operations  1.35 us (1%)
    all_to_all x1, blocking collectives, body(): parts = lax.all_to_all(pack_sums(own, come), 'yh', 0, 0)  16.6 us
    all_to_all x1, blocking collectives, gather_over(): return lax.all_to_all(copies, axes, 0, 0)  15.8 us
    all_to_all x1, blocking collectives, body(): column = lax.all_to_all(copies, ROW[:2], 0, 0)  14.9 us
    all_to_all x1, blocking collectives, fetch_window(): lax.all_to_all(x, ROW[1:], 0, 0)  14.1 us
    all_to_all x1, blocking collectives, fetch_window(): offered = lax.all_to_all(pick_piece(offered, tile, 0), ROW[0], 0, 0)  12.9 us
    all_to_all x1, blocking collectives, fetch_window(): lax.all_to_all(pick_piece(offered, tile, shift), ROW[1:], 0, 0)  9.8 us
    pallas_call x1, Pallas kernels, recover(): pl.pallas_call(first_kernel, out_shape=(half, jax.ShapeDtypeStruct((acros...  2.33 us
    all_gather x1, blocking collectives, fetch_window(): return lax.all_gather(whole_half, 'core', axis=0, tiled=True)  2.17 us
  transfers between devices with their start and end apart: 1, of which 1 were waited for; matrix products, arithmetic and copies ran while one was open for 0% of the time, Pallas kernels for 1%

profile of v8, /device:TPU:8, one launch (start us, length us, event | category | flops | bytes accessed | tf_op | source)
XLA Modules:
  0.0 97.9 jit_solution(15453972305986842828)
XLA Ops:
  1.3 1.1 %stage.1 = (bf16[1024,128]{1,0:T(8,128)(2,1)S(1)}, bf16[48,2048]{1,0:T(8,128)(2,1)S(1)}, f32[1,48]{1,0:T(1,128)S(1)}, f32[1,48]{1,0:T(1,128)S(1)}, s32[8,64]{1,0:T(8,128)S(1)}, /*index=5*/s32[8,128]{1,0:T(8,128)S(1)}) custom-call(s32[1]{0:T(128)S(6)} %copy.12.owner_ref, bf16[2048,128]{1,0:T(8,128)(2,1)} %bitcast.21, bf16[48,2048]{1,0:T(8,128)(2,1)} %refs_0_.1, ...), custom_call_target="tpu_custom_call" | custom-call | tf_op jit(solution)/shard_map/stage/pallas_call | solution.py:327
  2.4 14.1 %conditional.1 = (bf16[8,128,128]{2,1,0:T(8,128)(2,1)S(1)}) conditional(s32[]{:T(128)} %convert_element_type.3, bf16[8,128,128]{2,1,0:T(8,128)(2,1)S(1)} %bitcast.19, bf16[8,128,128]{2,1,0:T(8,128)(2,1)S(1)} %bitcast.20), branch_computations={%region_0.0_spmd, %region_1.0_spmd} | conditional | bytes 1048584 | solution.py:361
  2.4 14.1 %all_to_all.29 = bf16[8,128,128]{2,1,0:T(8,128)(2,1)S(1)} all-to-all(bf16[8,128,128]{2,1,0:T(8,128)(2,1)S(1)} %copy.13), channel_id=1, replica_groups=mesh['yh'=4,'core'=2,'z'=8,'yl'=2,'x'=4] {'yl','x'}, dimensions={0} | all-to-all | bytes 524288 | tf_op jit(solution)/shard_map/cond/branch_1_fun/all_to_all | solution.py:361
  16.5 0.2 pick.2
  16.7 12.9 %all_to_all.30.offered_ref = bf16[8,128,128]{2,1,0:T(8,128)(2,1)S(1)} all-to-all(bf16[8,128,128]{2,1,0:T(8,128)(2,1)S(1)} %pick.2), channel_id=1, replica_groups=mesh['yh'=4,'core'=2,'z'=8,'yl'=2,'x'=4] {'z'}, dimensions={0} | all-to-all | bytes 524288 | tf_op jit(solution)/shard_map/all_to_all | solution.py:362
  29.6 0.2 pick.3
  29.8 9.8 %all_to_all.31 = bf16[8,128,128]{2,1,0:T(8,128)(2,1)S(1)} all-to-all(bf16[8,128,128]{2,1,0:T(8,128)(2,1)S(1)} %pick.3), channel_id=1, replica_groups=mesh['yh'=4,'core'=2,'z'=8,'yl'=2,'x'=4] {'yl','x'}, dimensions={0} | all-to-all | bytes 524288 | tf_op jit(solution)/shard_map/all_to_all | solution.py:363
  39.6 2.2 %all_gather.3.window_ref = bf16[2048,128]{1,0:T(8,128)(2,1)S(1)} all-gather(bf16[1024,128]{1,0:T(8,128)(2,1)S(1)} %bitcast.18), channel_id=1, replica_groups=mesh['yh'=4,'core'=2,'z'=8,'yl'=2,'x'=4] {'core'}, dimensions={0}, use_global_device_ids=true | all-gather | bytes 786432 | tf_op jit(solution)/shard_map/all_gather | solution.py:364
  41.8 0.9 history.1
  42.7 14.9 %all_to_all.32 = s16[16,56,128]{2,1,0:T(8,128)(2,1)S(1)} all-to-all(s16[16,56,128]{2,1,0:T(8,128)(2,1)S(1)} %history.1), channel_id=1, replica_groups=mesh['yh'=4,'core'=2,'z'=8,'yl'=2,'x'=4] {'z','yl'}, dimensions={0} | all-to-all | bytes 458752 | tf_op jit(solution)/shard_map/all_to_all | solution.py:374
  57.5 0.1 broadcast_in_dim.20
  57.7 15.8 %all_to_all.33.hist_ref = s16[4,16,56,128]{3,2,1,0:T(8,128)(2,1)S(1)} all-to-all(s16[4,16,56,128]{3,2,1,0:T(8,128)(2,1)S(1)} %broadcast_in_dim.20), channel_id=1, replica_groups=mesh['yh'=4,'core'=2,'z'=8,'yl'=2,'x'=4] {'x'}, dimensions={0} | all-to-all | bytes 1835008 | tf_op jit(solution)/shard_map/all_to_all | solution.py:306
  73.4 2.3 %first.1 = (f32[4,384,128]{2,1,0:T(8,128)S(1)}, bf16[3072,256]{1,0:T(8,128)(2,1)S(1)}, bf16[4,3,4,128,128]{4,3,2,1,0:T(8,128)(2,1)S(1)}) custom-call(s16[4,16,56,128]{3,2,1,0:T(8,128)(2,1)S(1)} %all_to_all.33.hist_ref, s32[4,24]{1,0:T(4,128)} %bitcast.22, bf16[8,3,4,128,128]{4,3,2,1,0:T(8,128)(2,1)} %bitcast.17), custom_call_target="tpu_custom_call" | custom-call | flops 402653184 | bytes 1572864 | tf_op jit(solution)/shard_map/first/pallas_call | solution.py:168
  75.8 1.9 %collective-permute-start = (f32[4,384,128]{2,1,0:T(8,128)S(1)}, f32[4,384,128]{2,1,0:T(8,128)S(1)}, u32[]{:S(2)}, u32[]{:S(2)}) collective-permute-start(f32[4,384,128]{2,1,0:T(8,128)S(1)} %get-tuple-element.29), channel_id=1, source_target_pairs={{0,64},{64,0},{1,65},{65,1},{2,66},{66,2},{3,67},{67,3},{4,68},{68... | collective-permute-start | bytes 2359304 | tf_op jit(solution)/shard_map/ppermute | solution.py:184
  77.7 1.3 %second.1 = (f32[4,384,128]{2,1,0:T(8,128)S(1)}, f32[48,128]{1,0:T(8,128)S(1)}) custom-call(bf16[3072,256]{1,0:T(8,128)(2,1)S(1)} %get-tuple-element.25.split_ref, bf16[4,3,4,128,128]{4,3,2,1,0:T(8,128)(2,1)S(1)} %get-tuple-element.26.mine_ref, s32[8,64]{1,0:T(8,128)S(1)} %get-tuple-element.27.plane_ref, s32[4,24]{1,0:T(4,128)} %bitcast.23), custom_call_target="tpu_custom_call" | custom-call | flops 402653184 | bytes 1572864 | tf_op jit(solution)/shard_map/second/pallas_call | solution.py:185
  79.0 0.9 collective-permute-done.come_ref
  80.0 0.3 pack.1
  80.3 16.6 %all_to_all.34.parts_ref = s16[4,392,128]{2,1,0:T(8,128)(2,1)S(1)} all-to-all(s16[4,392,128]{2,1,0:T(8,128)(2,1)S(1)} %pack.1), channel_id=1, replica_groups=mesh['yh'=4,'core'=2,'z'=8,'yl'=2,'x'=4] {'yh'}, dimensions={0} | all-to-all | bytes 802816 | tf_op jit(solution)/shard_map/all_to_all | solution.py:377
  96.9 0.9 ranges.1
  (1 shorter events, 0.0 us)
Async XLA Ops:
  75.8 4.2 %collective-permute-start = (f32[4,384,128]{2,1,0:T(8,128)S(1)}, f32[4,384,128]{2,1,0:T(8,128)S(1)}, u32[]{:S(2)}, u32[]{:S(2)}) collective-permute-start(f32[4,384,128]{2,1,0:T(8,128)S(1)} %get-tuple-element.29), channel_id=1, source_target_pairs={{0,64},{64,0},{1,65},{65,1},{2,66},{66,2},{3,67},{67,3},{4,68},{68... | collective-permute-start | bytes 2359304 | tf_op jit(solution)/shard_map/ppermute | solution.py:184

commit v9 on v8

--- a/solution.py
+++ b/solution.py
@@ -342,10 +342,10 @@
         out_ref[i] = piece
 
 
-def pick_piece(offered, tile, shift):
+def pick_piece(offered, tile, shift, count):
     return pl.pallas_call(
         functools.partial(pick_kernel, shift),
-        out_shape=jax.ShapeDtypeStruct(offered.shape, offered.dtype),
+        out_shape=jax.ShapeDtypeStruct((count,) + offered.shape[1:], offered.dtype),
         in_specs=[pl.BlockSpec(memory_space=pltpu.VMEM)] * 2,
         out_specs=pl.BlockSpec(memory_space=pltpu.VMEM),
         compiler_params=pltpu.CompilerParams(vmem_limit_bytes=8 << 20),
@@ -354,14 +354,19 @@
 
 
 def fetch_window(half, tile, owner):
-    plane = lax.axis_size(ROW[1:])
+    plane, along = lax.axis_size(ROW[1:]), lax.axis_size(ROW[0])
     shift = plane.bit_length() - 1
+    near = ("core",) + ROW[1:]
+
+    def scatter(pieces, tile):
+        return pick_piece(lax.all_to_all(pieces, ROW[1:], 0, 0), tile, 0, along)
+
     pieces = half.reshape(plane, half.shape[0] // plane, half.shape[1])
     mine = lax.axis_index(ROW[0]) == lax.shift_right_logical(owner, shift)
-    offered = lax.cond(mine, lambda x: lax.all_to_all(x, ROW[1:], 0, 0), lambda x: x, pieces)
-    offered = lax.all_to_all(pick_piece(offered, tile, 0), ROW[0], 0, 0)
-    whole_half = lax.all_to_all(pick_piece(offered, tile, shift), ROW[1:], 0, 0).reshape(half.shape)
-    return lax.all_gather(whole_half, "core", axis=0, tiled=True)
+    copies = lax.cond(mine, scatter, lambda pieces, tile: pieces, pieces, tile)
+    offered = lax.all_to_all(copies, ROW[0], 0, 0)
+    window = lax.all_to_all(pick_piece(offered, tile, shift, lax.axis_size(near)), near, 0, 0)
+    return window.reshape(-1, half.shape[1])
 
 
 def body(load_windows, owner_id, participation, frequency, damping, recovery, pattern, plane_table):

time: 98.3 us -> 108 us (1.099)
  blocking collectives: 86.2 us -> 96 us
    all_to_all x3 -> x2, blocking collectives: 36.7 us -> 46.1 us  [the longest x1 32.2 us: fetch_window(): offered = lax.all_to_all(copies, ROW[0], 0, 0)]
    all_to_all x1, blocking collectives: 16.6 us -> 19.6 us  [body(): parts = lax.all_to_all(pack_sums(own, come), 'yh', 0, 0)]
    all_gather x1 -> x0, blocking collectives: 2.17 us -> none  [fetch_window(): return lax.all_gather(whole_half, 'core', axis=0, tiled=True)]
where the time goes in v9:
time: 108 us; the launch traced here: 107 us
  blocking collectives  96 us (89%)
  Pallas kernels  7.12 us (7%)
  starting transfers between devices  1.92 us (2%)
  between operations  1.35 us (1%)
    all_to_all x1, blocking collectives, fetch_window(): offered = lax.all_to_all(copies, ROW[0], 0, 0)  32.2 us
    all_to_all x1, blocking collectives, body(): parts = lax.all_to_all(pack_sums(own, come), 'yh', 0, 0)  19.6 us
    all_to_all x1, blocking collectives, gather_over(): return lax.all_to_all(copies, axes, 0, 0)  15.8 us
    all_to_all x1, blocking collectives, body(): column = lax.all_to_all(copies, ROW[:2], 0, 0)  14.6 us
    all_to_all x1, blocking collectives, fetch_window(): lax.all_to_all(pick_piece(offered, tile, shift, lax.axis_size(near)), nea...  13.8 us
    pallas_call x1, Pallas kernels, recover(): pl.pallas_call(first_kernel, out_shape=(half, jax.ShapeDtypeStruct((acros...  2.33 us
  transfers between devices with their start and end apart: 1, of which 1 were waited for; matrix products, arithmetic and copies ran while one was open for 0% of the time, Pallas kernels for 1%

profile of v9, /device:TPU:8, one launch (start us, length us, event | category | flops | bytes accessed | tf_op | source)
XLA Modules:
  0.0 107.5 jit_solution(1327985625709614373)
XLA Ops:
  1.3 1.1 stage.1
  2.4 32.2 %all_to_all.30.offered_ref = bf16[8,128,128]{2,1,0:T(8,128)(2,1)S(1)} all-to-all(bf16[8,128,128]{2,1,0:T(8,128)(2,1)S(1)} %get-tuple-element.38), channel_id=1, replica_groups=mesh['yh'=4,'core'=2,'z'=8,'yl'=2,'x'=4] {'z'}, dimensions={0} | all-to-all | bytes 524288 | tf_op jit(solution)/shard_map/all_to_all | solution.py:367
  34.6 0.3 pick.3
  34.9 13.8 %all_to_all.31 = bf16[16,128,128]{2,1,0:T(8,128)(2,1)S(1)} all-to-all(bf16[16,128,128]{2,1,0:T(8,128)(2,1)S(1)} %pick.3), channel_id=1, replica_groups=mesh['yh'=4,'core'=2,'z'=8,'yl'=2,'x'=4] {'core','yl','x'}, dimensions={0} | all-to-all | bytes 1048576 | tf_op jit(solution)/shard_map/all_to_all | solution.py:368
  48.7 0.9 history.1
  49.6 14.6 %all_to_all.32 = s16[16,56,128]{2,1,0:T(8,128)(2,1)S(1)} all-to-all(s16[16,56,128]{2,1,0:T(8,128)(2,1)S(1)} %history.1), channel_id=1, replica_groups=mesh['yh'=4,'core'=2,'z'=8,'yl'=2,'x'=4] {'z','yl'}, dimensions={0} | all-to-all | bytes 458752 | tf_op jit(solution)/shard_map/all_to_all | solution.py:379
  64.2 0.1 broadcast_in_dim.20
  64.3 15.8 %all_to_all.33.hist_ref = s16[4,16,56,128]{3,2,1,0:T(8,128)(2,1)S(1)} all-to-all(s16[4,16,56,128]{3,2,1,0:T(8,128)(2,1)S(1)} %broadcast_in_dim.20), channel_id=1, replica_groups=mesh['yh'=4,'core'=2,'z'=8,'yl'=2,'x'=4] {'x'}, dimensions={0} | all-to-all | bytes 1835008 | tf_op jit(solution)/shard_map/all_to_all | solution.py:306
  80.1 2.3 %first.1 = (f32[4,384,128]{2,1,0:T(8,128)S(1)}, bf16[3072,256]{1,0:T(8,128)(2,1)S(1)}, bf16[4,3,4,128,128]{4,3,2,1,0:T(8,128)(2,1)S(1)}) custom-call(s16[4,16,56,128]{3,2,1,0:T(8,128)(2,1)S(1)} %all_to_all.33.hist_ref, s32[4,24]{1,0:T(4,128)} %bitcast.22, bf16[8,3,4,128,128]{4,3,2,1,0:T(8,128)(2,1)} %bitcast.18), custom_call_target="tpu_custom_call" | custom-call | flops 402653184 | bytes 1572864 | tf_op jit(solution)/shard_map/first/pallas_call | solution.py:168
  82.4 1.9 %collective-permute-start = (f32[4,384,128]{2,1,0:T(8,128)S(1)}, f32[4,384,128]{2,1,0:T(8,128)S(1)}, u32[]{:S(2)}, u32[]{:S(2)}) collective-permute-start(f32[4,384,128]{2,1,0:T(8,128)S(1)} %get-tuple-element.34), channel_id=1, source_target_pairs={{0,64},{64,0},{1,65},{65,1},{2,66},{66,2},{3,67},{67,3},{4,68},{68... | collective-permute-start | bytes 2359304 | tf_op jit(solution)/shard_map/ppermute | solution.py:184
  84.3 1.3 %second.1 = (f32[4,384,128]{2,1,0:T(8,128)S(1)}, f32[48,128]{1,0:T(8,128)S(1)}) custom-call(bf16[3072,256]{1,0:T(8,128)(2,1)S(1)} %get-tuple-element.30.split_ref, bf16[4,3,4,128,128]{4,3,2,1,0:T(8,128)(2,1)S(1)} %get-tuple-element.31.mine_ref, s32[8,64]{1,0:T(8,128)S(1)} %get-tuple-element.32.plane_ref, s32[4,24]{1,0:T(4,128)} %bitcast.23), custom_call_target="tpu_custom_call" | custom-call | flops 402653184 | bytes 1572864 | tf_op jit(solution)/shard_map/second/pallas_call | solution.py:185
  85.6 0.9 collective-permute-done.come_ref
  86.6 0.3 pack.1
  86.9 19.6 %all_to_all.34.parts_ref = s16[4,392,128]{2,1,0:T(8,128)(2,1)S(1)} all-to-all(s16[4,392,128]{2,1,0:T(8,128)(2,1)S(1)} %pack.1), channel_id=1, replica_groups=mesh['yh'=4,'core'=2,'z'=8,'yl'=2,'x'=4] {'yh'}, dimensions={0} | all-to-all | bytes 802816 | tf_op jit(solution)/shard_map/all_to_all | solution.py:382
  106.5 0.9 ranges.1
  (1 shorter events, 0.0 us)
Async XLA Ops:
  82.4 4.2 %collective-permute-start = (f32[4,384,128]{2,1,0:T(8,128)S(1)}, f32[4,384,128]{2,1,0:T(8,128)S(1)}, u32[]{:S(2)}, u32[]{:S(2)}) collective-permute-start(f32[4,384,128]{2,1,0:T(8,128)S(1)} %get-tuple-element.34), channel_id=1, source_target_pairs={{0,64},{64,0},{1,65},{65,1},{2,66},{66,2},{3,67},{67,3},{4,68},{68... | collective-permute-start | bytes 2359304 | tf_op jit(solution)/shard_map/ppermute | solution.py:184

commit v10 on v9

--- a/solution.py
+++ b/solution.py
@@ -9,6 +9,7 @@
 from jax.sharding import PartitionSpec as P
 
 ROW = ("z", "yl", "x")
+FIRST, THEN = ROW[:1], ROW[1:]
 CODE_ROWS = 8
 LEVELS = 32760.0
 PLANES = 64
@@ -45,11 +46,19 @@
     return rows_ref[...].T[:modes]
 
 
-def history_kernel(window_ref, part_ref, rate_ref, decay_ref, out_ref, rows_ref):
+def history_kernel(window_ref, *refs):
+    away, (out_ref, *near, rows_ref, sems) = refs[:3], refs[3:]
+    fetches = [pltpu.make_async_copy(a, b, sems.at[i]) for i, (a, b) in enumerate(zip(away, near))]
+    for fetch in fetches:
+        fetch.start()
+    part_ref, rate_ref, decay_ref = near
+    fetches[1].wait()
+    fetches[2].wait()
+    table = mode_table(rate_ref[...], decay_ref[...], rows_ref)
+    fetches[0].wait()
     forces = jnp.dot(part_ref[...], window_ref[...], preferred_element_type=jnp.float32)
     modes, steps = forces.shape
     doublings = steps.bit_length() - 1
-    table = mode_table(rate_ref[...], decay_ref[...], rows_ref)
     lane = lax.broadcasted_iota(jnp.int32, forces.shape, 1)
     re, im = forces, jnp.zeros_like(forces)
     for d in range(doublings):
@@ -76,15 +85,21 @@
     return pl.pallas_call(
         history_kernel,
         out_shape=jax.ShapeDtypeStruct((count, modes + CODE_ROWS, steps), jnp.int16),
-        in_specs=[pl.BlockSpec(memory_space=pltpu.VMEM)] * 4,
+        in_specs=[pl.BlockSpec(memory_space=pltpu.VMEM)] + [pl.BlockSpec(memory_space=pl.ANY)] * 3,
         out_specs=pl.BlockSpec(memory_space=pltpu.VMEM),
-        scratch_shapes=[pltpu.VMEM((128, 128), jnp.float32)],
+        scratch_shapes=[
+            pltpu.VMEM(participation.shape, participation.dtype),
+            pltpu.VMEM(frequency.shape, frequency.dtype),
+            pltpu.VMEM(damping.shape, damping.dtype),
+            pltpu.VMEM((128, 128), jnp.float32),
+            pltpu.SemaphoreType.DMA((3,)),
+        ],
         compiler_params=pltpu.CompilerParams(vmem_limit_bytes=16 << 20),
         cost_estimate=pl.CostEstimate(
             flops=2 * modes * channels * steps, bytes_accessed=2 * (channels * (modes + steps)), transcendentals=0
         ),
         name="history",
-    )(window, participation, frequency, damping)
+    )(window, *(far(x) for x in (participation, frequency, damping)))
 
 
 def product(picks_ref, side, coeff_ref, split_ref, out_ref, fetches):
@@ -140,9 +155,14 @@
         fetch.wait()
 
 
-def second_kernel(split_ref, mine_ref, plane_ref, picks_far, own_ref, coeffs_ref, picks_ref, rows_ref, picks_sem):
+def second_kernel(
+    split_ref, mine_ref, planes_far, picks_far, own_ref, coeffs_ref, picks_ref, plane_ref, rows_ref, picks_sem, planes_sem
+):
     fetch_picks = pltpu.make_async_copy(picks_far, picks_ref, picks_sem)
+    fetch_planes = pltpu.make_async_copy(planes_far, plane_ref, planes_sem)
     fetch_picks.start()
+    fetch_planes.start()
+    fetch_planes.wait()
     plane_rows(plane_ref[...], rows_ref, coeffs_ref)
     fetch_picks.wait()
     product(picks_ref, lax.axis_index("core"), mine_ref, split_ref, own_ref, [])
@@ -185,13 +205,19 @@
     own, coeffs = pl.pallas_call(
         second_kernel,
         out_shape=(half, jax.ShapeDtypeStruct((6 * planes.shape[0], 128), jnp.float32)),
-        in_specs=[near, near, near, away],
+        in_specs=[near, near, away, away],
         out_specs=(near,) * 2,
-        scratch_shapes=scratch + [pltpu.VMEM((6 * planes.shape[0], 128), jnp.float32), pltpu.SemaphoreType.DMA],
+        scratch_shapes=scratch
+        + [
+            pltpu.VMEM(planes.shape, planes.dtype),
+            pltpu.VMEM((6 * planes.shape[0], 128), jnp.float32),
+            pltpu.SemaphoreType.DMA,
+            pltpu.SemaphoreType.DMA,
+        ],
         compiler_params=pltpu.CompilerParams(vmem_limit_bytes=24 << 20),
         cost_estimate=cost,
         name="second",
-    )(split, mine, planes, far(picks))
+    )(split, mine, far(planes), far(picks))
     return own, come, coeffs
 
 
@@ -306,78 +332,69 @@
     return lax.all_to_all(copies, axes, 0, 0)
 
 
-def stage_kernel(owner_ref, whole_ref, *refs):
-    count = (len(refs) - 3) // 2
-    away, (half_ref, *near, tile_ref, sems) = refs[:count], refs[count:]
+def half_kernel(whole_ref, half_ref, sem):
     rows = half_ref.shape[0]
     start = pl.multiple_of(lax.axis_index("core") * rows, rows)
-    fetches = [pltpu.make_async_copy(whole_ref.at[pl.ds(start, rows)], half_ref, sems.at[count])]
-    fetches += [pltpu.make_async_copy(a, b, sems.at[i]) for i, (a, b) in enumerate(zip(away, near))]
-    for fetch in fetches:
-        fetch.start()
-    tile_ref[...] = jnp.full(tile_ref.shape, owner_ref[0], jnp.int32)
-    for fetch in fetches:
-        fetch.wait()
-
-
-def stage(owner, whole, *others):
+    fetch = pltpu.make_async_copy(whole_ref.at[pl.ds(start, rows)], half_ref, sem)
+    fetch.start()
+    fetch.wait()
+
+
+def take_half(whole):
     channels, steps = whole.shape
-    copied = [jax.ShapeDtypeStruct((channels // 2, steps), whole.dtype)]
-    copied += [jax.ShapeDtypeStruct(x.shape, x.dtype) for x in others]
     return pl.pallas_call(
-        stage_kernel,
-        out_shape=(*copied, jax.ShapeDtypeStruct((8, 128), jnp.int32)),
-        in_specs=[pl.BlockSpec(memory_space=pltpu.SMEM)] + [pl.BlockSpec(memory_space=pl.ANY)] * len(copied),
-        out_specs=(pl.BlockSpec(memory_space=pltpu.VMEM),) * (1 + len(copied)),
-        scratch_shapes=[pltpu.SemaphoreType.DMA((len(copied),))],
+        half_kernel,
+        out_shape=jax.ShapeDtypeStruct((channels // 2, steps), whole.dtype),
+        in_specs=[pl.BlockSpec(memory_space=pl.ANY)],
+        out_specs=pl.BlockSpec(memory_space=pltpu.VMEM),
+        scratch_shapes=[pltpu.SemaphoreType.DMA],
         compiler_params=pltpu.CompilerParams(vmem_limit_bytes=8 << 20),
-        name="stage",
-    )(owner, *(far(x) for x in (whole, *others)))
-
-
-def pick_kernel(shift, tile_ref, offered_ref, out_ref):
-    owner = jnp.max(tile_ref[...])
-    piece = offered_ref[lax.rem(lax.shift_right_logical(owner, shift), offered_ref.shape[0])]
+        name="half",
+    )(far(whole))
+
+
+def pick_kernel(shift, owner_ref, offered_ref, out_ref):
+    piece = offered_ref[lax.rem(lax.shift_right_logical(owner_ref[0], shift), offered_ref.shape[0])]
     for i in range(out_ref.shape[0]):
         out_ref[i] = piece
 
 
-def pick_piece(offered, tile, shift, count):
+def pick_piece(offered, owner, shift, count):
     return pl.pallas_call(
         functools.partial(pick_kernel, shift),
         out_shape=jax.ShapeDtypeStruct((count,) + offered.shape[1:], offered.dtype),
-        in_specs=[pl.BlockSpec(memory_space=pltpu.VMEM)] * 2,
+        in_specs=[pl.BlockSpec(memory_space=pltpu.SMEM), pl.BlockSpec(memory_space=pltpu.VMEM)],
         out_specs=pl.BlockSpec(memory_space=pltpu.VMEM),
         compiler_params=pltpu.CompilerParams(vmem_limit_bytes=8 << 20),
         name="pick",
-    )(tile, offered)
-
-
-def fetch_window(half, tile, owner):
+    )(owner, offered)
+
+
+def fetch_window(whole, owner):
+    channels, steps = whole.shape
     plane, along = lax.axis_size(ROW[1:]), lax.axis_size(ROW[0])
     shift = plane.bit_length() - 1
-    near = ("core",) + ROW[1:]
-
-    def scatter(pieces, tile):
-        return pick_piece(lax.all_to_all(pieces, ROW[1:], 0, 0), tile, 0, along)
-
-    pieces = half.reshape(plane, half.shape[0] // plane, half.shape[1])
-    mine = lax.axis_index(ROW[0]) == lax.shift_right_logical(owner, shift)
-    copies = lax.cond(mine, scatter, lambda pieces, tile: pieces, pieces, tile)
-    offered = lax.all_to_all(copies, ROW[0], 0, 0)
-    window = lax.all_to_all(pick_piece(offered, tile, shift, lax.axis_size(near)), near, 0, 0)
-    return window.reshape(-1, half.shape[1])
+    rows = channels // 2 // plane
+
+    def scatter(whole, owner):
+        pieces = take_half(whole).reshape(plane, rows, steps)
+        return pick_piece(lax.all_to_all(pieces, ROW[1:], 0, 0), owner, 0, along)
+
+    def nothing(whole, owner):
+        return jnp.zeros((along, rows, steps), whole.dtype)
+
+    mine = lax.axis_index(ROW[0]) == lax.shift_right_logical(owner[0], shift)
+    offered = lax.all_to_all(lax.cond(mine, scatter, nothing, whole, owner), ROW[0], 0, 0)
+    whole_half = lax.all_to_all(pick_piece(offered, owner, shift, plane), ROW[1:], 0, 0)
+    return lax.all_gather(whole_half.reshape(plane * rows, steps), "core", axis=0, tiled=True)
 
 
 def body(load_windows, owner_id, participation, frequency, damping, recovery, pattern, plane_table):
     planes = plane_table[0, 0].T
-    half, part, rates, decays, planes, tile = stage(
-        owner_id, load_windows[0], participation, frequency[None], damping[None], planes
-    )
-    window = fetch_window(half, tile, owner_id[0])
-    copies = make_history(window, part, rates, decays, lax.axis_size(ROW[:2]))
-    column = lax.all_to_all(copies, ROW[:2], 0, 0)
-    hist = gather_over(column, ROW[2])
+    window = fetch_window(load_windows[0], owner_id)
+    copies = make_history(window, participation, frequency[None], damping[None], lax.axis_size(FIRST))
+    column = lax.all_to_all(copies, FIRST, 0, 0)
+    hist = gather_over(column, THEN)
     own, come, coeffs = recover(hist, recovery[0, 0], pattern[0, 0].T, planes, lax.axis_size(("yh", "core")))
     parts = lax.all_to_all(pack_sums(own, come), "yh", 0, 0)
     stress, plane_range = finish(parts, coeffs, planes.shape[0])

time: 108 us -> 106 us (0.981)
  blocking collectives: 96 us -> 94.4 us
    all_to_all x3, blocking collectives: 60.6 us -> 55.1 us  [the longest x1 33.6 us: fetch_window(): lax.all_to_all(lax.cond(mine, scatter, nothing, whole, owner), ROW[0], 0, 0)]
    all_gather x0 -> x1, blocking collectives: none -> 2.17 us  [fetch_window(): lax.all_gather(whole_half.reshape(plane * rows, steps), 'core', axis=0, t...]
    all_to_all x1, blocking collectives: 19.6 us -> 21 us  [body(): parts = lax.all_to_all(pack_sums(own, come), 'yh', 0, 0)]
where the time goes in v10:
time: 106 us
  blocking collectives  94.4 us (89%)
  Pallas kernels  6.89 us (6%)
  starting transfers between devices  1.92 us (2%)
  between operations  1.35 us (1%)
    all_to_all x1, blocking collectives, fetch_window(): lax.all_to_all(lax.cond(mine, scatter, nothing, whole, owner), ROW[0], 0, 0)  33.6 us
    all_to_all x1, blocking collectives, body(): parts = lax.all_to_all(pack_sums(own, come), 'yh', 0, 0)  21 us
    all_to_all x1, blocking collectives, gather_over(): return lax.all_to_all(copies, axes, 0, 0)  16.1 us
    all_to_all x1, blocking collectives, body(): column = lax.all_to_all(copies, FIRST, 0, 0)  11.7 us
    all_to_all x1, blocking collectives, fetch_window(): lax.all_to_all(pick_piece(offered, owner, shift, plane), ROW[1:], 0, 0)  9.82 us
    pallas_call x1, Pallas kernels, recover(): pl.pallas_call(first_kernel, out_shape=(half, jax.ShapeDtypeStruct((acros...  2.33 us
    all_gather x1, blocking collectives, fetch_window(): lax.all_gather(whole_half.reshape(plane * rows, steps), 'core', axis=0, t...  2.17 us
  transfers between devices with their start and end apart: 1, of which 1 were waited for; matrix products, arithmetic and copies ran while one was open for 0% of the time, Pallas kernels for 1%

profile of v10, /device:TPU:8, one launch (start us, length us, event | category | flops | bytes accessed | tf_op | source)
XLA Modules:
  0.0 105.5 jit_solution(12010472180981965776)
XLA Ops:
  1.3 0.1 conditional.1
  1.3 33.6 %all_to_all.30.offered_ref = bf16[8,128,128]{2,1,0:T(8,128)(2,1)S(1)} all-to-all(bf16[8,128,128]{2,1,0:T(8,128)(2,1)S(1)} %get-tuple-element.28), channel_id=1, replica_groups=mesh['yh'=4,'core'=2,'z'=8,'yl'=2,'x'=4] {'z'}, dimensions={0} | all-to-all | bytes 524288 | tf_op jit(solution)/shard_map/all_to_all | solution.py:387
  35.0 9.8 %all_to_all.31 = bf16[8,128,128]{2,1,0:T(8,128)(2,1)S(1)} all-to-all(bf16[8,128,128]{2,1,0:T(8,128)(2,1)S(1)} %pick.3), channel_id=1, replica_groups=mesh['yh'=4,'core'=2,'z'=8,'yl'=2,'x'=4] {'yl','x'}, dimensions={0} | all-to-all | bytes 524288 | tf_op jit(solution)/shard_map/all_to_all | solution.py:388
  44.8 2.2 %all_gather.3.window_ref = bf16[2048,128]{1,0:T(8,128)(2,1)S(1)} all-gather(bf16[1024,128]{1,0:T(8,128)(2,1)S(1)} %bitcast.19), channel_id=1, replica_groups=mesh['yh'=4,'core'=2,'z'=8,'yl'=2,'x'=4] {'core'}, dimensions={0}, use_global_device_ids=true | all-gather | bytes 786432 | tf_op jit(solution)/shard_map/all_gather | solution.py:389
  47.0 1.8 %history.1 = s16[8,56,128]{2,1,0:T(8,128)(2,1)S(1)} custom-call(bf16[2048,128]{1,0:T(8,128)(2,1)S(1)} %all_gather.3.window_ref, bf16[48,2048]{1,0:T(8,128)(2,1)} %refs_0_.1, f32[1,48]{1,0:T(1,128)} %bitcast.24, f32[1,48]{1,0:T(1,128)} %bitcast.25), custom_call_target="tpu_custom_call" | custom-call | flops 25165824 | bytes 720896 | tf_op jit(solution)/shard_map/history/pallas_call | solution.py:85
  48.8 11.7 %all_to_all.32 = s16[8,56,128]{2,1,0:T(8,128)(2,1)S(1)} all-to-all(s16[8,56,128]{2,1,0:T(8,128)(2,1)S(1)} %history.1), channel_id=1, replica_groups=mesh['yh'=4,'core'=2,'z'=8,'yl'=2,'x'=4] {'z'}, dimensions={0} | all-to-all | bytes 229376 | tf_op jit(solution)/shard_map/all_to_all | solution.py:396
  60.4 0.1 broadcast_in_dim.20
  60.6 16.1 %all_to_all.33.hist_ref = s16[8,8,56,128]{3,2,1,0:T(8,128)(2,1)S(1)} all-to-all(s16[8,8,56,128]{3,2,1,0:T(8,128)(2,1)S(1)} %broadcast_in_dim.20), channel_id=1, replica_groups=mesh['yh'=4,'core'=2,'z'=8,'yl'=2,'x'=4] {'yl','x'}, dimensions={0} | all-to-all | bytes 1835008 | tf_op jit(solution)/shard_map/all_to_all | solution.py:332
  76.7 2.3 %first.1 = (f32[4,384,128]{2,1,0:T(8,128)S(1)}, bf16[3072,256]{1,0:T(8,128)(2,1)S(1)}, bf16[4,3,4,128,128]{4,3,2,1,0:T(8,128)(2,1)S(1)}) custom-call(s16[8,8,56,128]{3,2,1,0:T(8,128)(2,1)S(1)} %all_to_all.33.hist_ref, s32[4,24]{1,0:T(4,128)} %bitcast.21, bf16[8,3,4,128,128]{4,3,2,1,0:T(8,128)(2,1)} %bitcast.18), custom_call_target="tpu_custom_call" | custom-call | flops 402653184 | bytes 1572864 | tf_op jit(solution)/shard_map/first/pallas_call | solution.py:188
  79.0 1.9 %collective-permute-start = (f32[4,384,128]{2,1,0:T(8,128)S(1)}, f32[4,384,128]{2,1,0:T(8,128)S(1)}, u32[]{:S(2)}, u32[]{:S(2)}) collective-permute-start(f32[4,384,128]{2,1,0:T(8,128)S(1)} %get-tuple-element.22), channel_id=1, source_target_pairs={{0,64},{64,0},{1,65},{65,1},{2,66},{66,2},{3,67},{67,3},{4,68},{68... | collective-permute-start | bytes 2359304 | tf_op jit(solution)/shard_map/ppermute | solution.py:204
  81.0 1.5 %second.1 = (f32[4,384,128]{2,1,0:T(8,128)S(1)}, f32[48,128]{1,0:T(8,128)S(1)}) custom-call(bf16[3072,256]{1,0:T(8,128)(2,1)S(1)} %get-tuple-element.19.split_ref, bf16[4,3,4,128,128]{4,3,2,1,0:T(8,128)(2,1)S(1)} %get-tuple-element.20.mine_ref, s32[8,64]{1,0:T(8,128)} %bitcast.23, s32[4,24]{1,0:T(4,128)} %bitcast.22), custom_call_target="tpu_custom_call" | custom-call | flops 402653184 | bytes 1572864 | tf_op jit(solution)/shard_map/second/pallas_call | solution.py:205
  82.4 0.8 collective-permute-done.come_ref
  83.2 0.3 pack.1
  83.6 21.0 %all_to_all.34.parts_ref = s16[4,392,128]{2,1,0:T(8,128)(2,1)S(1)} all-to-all(s16[4,392,128]{2,1,0:T(8,128)(2,1)S(1)} %pack.1), channel_id=1, replica_groups=mesh['yh'=4,'core'=2,'z'=8,'yl'=2,'x'=4] {'yh'}, dimensions={0} | all-to-all | bytes 802816 | tf_op jit(solution)/shard_map/all_to_all | solution.py:399
  104.6 0.9 ranges.1
  (2 shorter events, 0.1 us)
Async XLA Ops:
  79.0 4.2 %collective-permute-start = (f32[4,384,128]{2,1,0:T(8,128)S(1)}, f32[4,384,128]{2,1,0:T(8,128)S(1)}, u32[]{:S(2)}, u32[]{:S(2)}) collective-permute-start(f32[4,384,128]{2,1,0:T(8,128)S(1)} %get-tuple-element.22), channel_id=1, source_target_pairs={{0,64},{64,0},{1,65},{65,1},{2,66},{66,2},{3,67},{67,3},{4,68},{68... | collective-permute-start | bytes 2359304 | tf_op jit(solution)/shard_map/ppermute | solution.py:204

commit v11 on v10

--- a/solution.py
+++ b/solution.py
@@ -47,15 +47,8 @@
 
 
 def history_kernel(window_ref, *refs):
-    away, (out_ref, *near, rows_ref, sems) = refs[:3], refs[3:]
-    fetches = [pltpu.make_async_copy(a, b, sems.at[i]) for i, (a, b) in enumerate(zip(away, near))]
-    for fetch in fetches:
-        fetch.start()
-    part_ref, rate_ref, decay_ref = near
-    fetches[1].wait()
-    fetches[2].wait()
+    part_ref, rate_ref, decay_ref, out_ref, rows_ref = refs
     table = mode_table(rate_ref[...], decay_ref[...], rows_ref)
-    fetches[0].wait()
     forces = jnp.dot(part_ref[...], window_ref[...], preferred_element_type=jnp.float32)
     modes, steps = forces.shape
     doublings = steps.bit_length() - 1
@@ -85,21 +78,15 @@
     return pl.pallas_call(
         history_kernel,
         out_shape=jax.ShapeDtypeStruct((count, modes + CODE_ROWS, steps), jnp.int16),
-        in_specs=[pl.BlockSpec(memory_space=pltpu.VMEM)] + [pl.BlockSpec(memory_space=pl.ANY)] * 3,
+        in_specs=[pl.BlockSpec(memory_space=pltpu.VMEM)] * 4,
         out_specs=pl.BlockSpec(memory_space=pltpu.VMEM),
-        scratch_shapes=[
-            pltpu.VMEM(participation.shape, participation.dtype),
-            pltpu.VMEM(frequency.shape, frequency.dtype),
-            pltpu.VMEM(damping.shape, damping.dtype),
-            pltpu.VMEM((128, 128), jnp.float32),
-            pltpu.SemaphoreType.DMA((3,)),
-        ],
+        scratch_shapes=[pltpu.VMEM((128, 128), jnp.float32)],
         compiler_params=pltpu.CompilerParams(vmem_limit_bytes=16 << 20),
         cost_estimate=pl.CostEstimate(
             flops=2 * modes * channels * steps, bytes_accessed=2 * (channels * (modes + steps)), transcendentals=0
         ),
         name="history",
-    )(window, *(far(x) for x in (participation, frequency, damping)))
+    )(window, participation, frequency, damping)
 
 
 def product(picks_ref, side, coeff_ref, split_ref, out_ref, fetches):

time: 106 us -> 98.5 us (0.929)
  blocking collectives: 94.4 us -> 87.9 us
    all_to_all x1, blocking collectives: 33.6 us -> 27.1 us  [fetch_window(): lax.all_to_all(lax.cond(mine, scatter, nothing, whole, owner), ROW[0], 0, 0)]
where the time goes in v11:
time: 98.5 us; the launch traced here: 98.1 us
  blocking collectives  87.9 us (89%)
  Pallas kernels  5.94 us (6%)
  starting transfers between devices  1.92 us (2%)
  between operations  1.37 us (1%)
    all_to_all x1, blocking collectives, fetch_window(): lax.all_to_all(lax.cond(mine, scatter, nothing, whole, owner), ROW[0], 0, 0)  27.1 us
    all_to_all x1, blocking collectives, body(): parts = lax.all_to_all(pack_sums(own, come), 'yh', 0, 0)  21 us
    all_to_all x1, blocking collectives, gather_over(): return lax.all_to_all(copies, axes, 0, 0)  16.1 us
    all_to_all x1, blocking collectives, body(): column = lax.all_to_all(copies, FIRST, 0, 0)  11.7 us
    all_to_all x1, blocking collectives, fetch_window(): lax.all_to_all(pick_piece(offered, owner, shift, plane), ROW[1:], 0, 0)  9.82 us
    pallas_call x1, Pallas kernels, recover(): pl.pallas_call(first_kernel, out_shape=(half, jax.ShapeDtypeStruct((acros...  2.33 us
    all_gather x1, blocking collectives, fetch_window(): lax.all_gather(whole_half.reshape(plane * rows, steps), 'core', axis=0, t...  2.17 us
  transfers between devices with their start and end apart: 1, of which 1 were waited for; matrix products, arithmetic and copies ran while one was open for 0% of the time, Pallas kernels for 1%

profile of v11, /device:TPU:8, one launch (start us, length us, event | category | flops | bytes accessed | tf_op | source)
XLA Modules:
  0.0 98.1 jit_solution(17736391802549321992)
XLA Ops:
  1.3 0.1 conditional.1
  1.3 0.0 copy-start
  1.4 0.0 copy-start.1
  1.4 0.0 copy-start.2
  1.4 27.1 %all_to_all.30.offered_ref = bf16[8,128,128]{2,1,0:T(8,128)(2,1)S(1)} all-to-all(bf16[8,128,128]{2,1,0:T(8,128)(2,1)S(1)} %get-tuple-element.28), channel_id=1, replica_groups=mesh['yh'=4,'core'=2,'z'=8,'yl'=2,'x'=4] {'z'}, dimensions={0} | all-to-all | bytes 524288 | tf_op jit(solution)/shard_map/all_to_all | solution.py:374
  28.5 9.8 %all_to_all.31 = bf16[8,128,128]{2,1,0:T(8,128)(2,1)S(1)} all-to-all(bf16[8,128,128]{2,1,0:T(8,128)(2,1)S(1)} %pick.3), channel_id=1, replica_groups=mesh['yh'=4,'core'=2,'z'=8,'yl'=2,'x'=4] {'yl','x'}, dimensions={0} | all-to-all | bytes 524288 | tf_op jit(solution)/shard_map/all_to_all | solution.py:375
  38.3 2.2 %all_gather.3.window_ref = bf16[2048,128]{1,0:T(8,128)(2,1)S(1)} all-gather(bf16[1024,128]{1,0:T(8,128)(2,1)S(1)} %bitcast.21), channel_id=1, replica_groups=mesh['yh'=4,'core'=2,'z'=8,'yl'=2,'x'=4] {'core'}, dimensions={0}, use_global_device_ids=true | all-gather | bytes 786432 | tf_op jit(solution)/shard_map/all_gather | solution.py:376
  40.5 0.0 copy-done
  40.5 0.0 copy-done.1
  40.5 0.0 copy-done.2
  40.5 0.9 history.1
  41.4 11.7 %all_to_all.32 = s16[8,56,128]{2,1,0:T(8,128)(2,1)S(1)} all-to-all(s16[8,56,128]{2,1,0:T(8,128)(2,1)S(1)} %history.1), channel_id=1, replica_groups=mesh['yh'=4,'core'=2,'z'=8,'yl'=2,'x'=4] {'z'}, dimensions={0} | all-to-all | bytes 229376 | tf_op jit(solution)/shard_map/all_to_all | solution.py:383
  53.0 0.1 broadcast_in_dim.20
  53.2 16.1 %all_to_all.33.hist_ref = s16[8,8,56,128]{3,2,1,0:T(8,128)(2,1)S(1)} all-to-all(s16[8,8,56,128]{3,2,1,0:T(8,128)(2,1)S(1)} %broadcast_in_dim.20), channel_id=1, replica_groups=mesh['yh'=4,'core'=2,'z'=8,'yl'=2,'x'=4] {'yl','x'}, dimensions={0} | all-to-all | bytes 1835008 | tf_op jit(solution)/shard_map/all_to_all | solution.py:319
  69.3 2.3 %first.1 = (f32[4,384,128]{2,1,0:T(8,128)S(1)}, bf16[3072,256]{1,0:T(8,128)(2,1)S(1)}, bf16[4,3,4,128,128]{4,3,2,1,0:T(8,128)(2,1)S(1)}) custom-call(s16[8,8,56,128]{3,2,1,0:T(8,128)(2,1)S(1)} %all_to_all.33.hist_ref, s32[4,24]{1,0:T(4,128)} %bitcast.23, bf16[8,3,4,128,128]{4,3,2,1,0:T(8,128)(2,1)} %bitcast.20), custom_call_target="tpu_custom_call" | custom-call | flops 402653184 | bytes 1572864 | tf_op jit(solution)/shard_map/first/pallas_call | solution.py:175
  71.6 1.9 %collective-permute-start = (f32[4,384,128]{2,1,0:T(8,128)S(1)}, f32[4,384,128]{2,1,0:T(8,128)S(1)}, u32[]{:S(2)}, u32[]{:S(2)}) collective-permute-start(f32[4,384,128]{2,1,0:T(8,128)S(1)} %get-tuple-element.22), channel_id=1, source_target_pairs={{0,64},{64,0},{1,65},{65,1},{2,66},{66,2},{3,67},{67,3},{4,68},{68... | collective-permute-start | bytes 2359304 | tf_op jit(solution)/shard_map/ppermute | solution.py:191
  73.5 1.4 %second.1 = (f32[4,384,128]{2,1,0:T(8,128)S(1)}, f32[48,128]{1,0:T(8,128)S(1)}) custom-call(bf16[3072,256]{1,0:T(8,128)(2,1)S(1)} %get-tuple-element.19.split_ref, bf16[4,3,4,128,128]{4,3,2,1,0:T(8,128)(2,1)S(1)} %get-tuple-element.20.mine_ref, s32[8,64]{1,0:T(8,128)} %bitcast.25, s32[4,24]{1,0:T(4,128)} %bitcast.24), custom_call_target="tpu_custom_call" | custom-call | flops 402653184 | bytes 1572864 | tf_op jit(solution)/shard_map/second/pallas_call | solution.py:192
  75.0 0.8 collective-permute-done.come_ref
  75.8 0.3 pack.1
  76.2 21.0 %all_to_all.34.parts_ref = s16[4,392,128]{2,1,0:T(8,128)(2,1)S(1)} all-to-all(s16[4,392,128]{2,1,0:T(8,128)(2,1)S(1)} %pack.1), channel_id=1, replica_groups=mesh['yh'=4,'core'=2,'z'=8,'yl'=2,'x'=4] {'yh'}, dimensions={0} | all-to-all | bytes 802816 | tf_op jit(solution)/shard_map/all_to_all | solution.py:386
  97.2 0.9 ranges.1
  (2 shorter events, 0.1 us)
Async XLA Ops:
  1.3 39.1 %copy-start = (bf16[48,2048]{1,0:T(8,128)(2,1)S(1)}, bf16[48,2048]{1,0:T(8,128)(2,1)}, u32[]{:S(2)}) copy-start(bf16[48,2048]{1,0:T(8,128)(2,1)} %refs_0_.1) | copy-start | bytes 589828
  1.4 39.1 %copy-start.1 = (f32[48]{0:T(128)S(1)}, f32[48]{0:T(128)}, u32[]{:S(2)}) copy-start(f32[48]{0:T(128)} %param.13) | copy-start | bytes 580
  1.4 39.1 %copy-start.2 = (f32[48]{0:T(128)S(1)}, f32[48]{0:T(128)}, u32[]{:S(2)}) copy-start(f32[48]{0:T(128)} %param.14) | copy-start | bytes 580
  71.6 4.2 %collective-permute-start = (f32[4,384,128]{2,1,0:T(8,128)S(1)}, f32[4,384,128]{2,1,0:T(8,128)S(1)}, u32[]{:S(2)}, u32[]{:S(2)}) collective-permute-start(f32[4,384,128]{2,1,0:T(8,128)S(1)} %get-tuple-element.22), channel_id=1, source_target_pairs={{0,64},{64,0},{1,65},{65,1},{2,66},{66,2},{3,67},{67,3},{4,68},{68... | collective-permute-start | bytes 2359304 | tf_op jit(solution)/shard_map/ppermute | solution.py:191

commit v12 on v11

--- a/solution.py
+++ b/solution.py
@@ -89,32 +89,22 @@
     )(window, participation, frequency, damping)
 
 
-def product(picks_ref, side, coeff_ref, split_ref, out_ref, fetches):
-    groups, per_slab, picked, height, width = coeff_ref.shape
-    steps = out_ref.shape[2]
+def product(picks_ref, side, coeff_ref, split_ref, out_ref):
+    per_slab, picked, height, width = coeff_ref.shape[1:]
+    groups, _, steps = out_ref.shape
     for g in range(groups):
-        if fetches:
-            fetches[g].wait()
         for r in range(per_slab):
             block = (2 * g + side) * per_slab + r
-            left = jnp.concatenate([coeff_ref[g, r, k] for k in range(picked)], axis=1)
+            left = jnp.concatenate([coeff_ref[2 * g + side, r, k] for k in range(picked)], axis=1)
             starts = [pl.multiple_of(picks_ref[k, block] * width, width) for k in range(picked)]
             right = jnp.concatenate([split_ref[pl.ds(start, width), :] for start in starts], axis=0)
             both = jnp.dot(left, right, preferred_element_type=jnp.float32)
             out_ref[g, r * height : (r + 1) * height, :] = both[:, :steps] + both[:, steps:]
 
 
-def first_kernel(hist_ref, picks_far, far_ref, other_ref, split_ref, mine_ref, theirs_ref, picks_ref, sems, picks_sem):
-    core = lax.axis_index("core")
-    groups = mine_ref.shape[0]
-    fetches = [[], []]
+def first_kernel(hist_ref, picks_far, coeff_ref, other_ref, split_ref, picks_ref, picks_sem):
     fetch_picks = pltpu.make_async_copy(picks_far, picks_ref, picks_sem)
     fetch_picks.start()
-    for i, (near, side) in enumerate([(theirs_ref, 1 - core), (mine_ref, core)]):
-        for g in range(groups):
-            fetch = pltpu.make_async_copy(far_ref.at[2 * g + side], near.at[g], sems.at[i, g])
-            fetch.start()
-            fetches[i].append(fetch)
     across, along, rows, steps = hist_ref.shape
     sources = across * along
     modes = rows - CODE_ROWS
@@ -137,13 +127,11 @@
         split_ref[s * modes : (s + 1) * modes, :steps] = high
         split_ref[s * modes : (s + 1) * modes, steps:] = low
     fetch_picks.wait()
-    product(picks_ref, 1 - core, theirs_ref, split_ref, other_ref, fetches[0])
-    for fetch in fetches[1]:
-        fetch.wait()
+    product(picks_ref, 1 - lax.axis_index("core"), coeff_ref, split_ref, other_ref)
 
 
 def second_kernel(
-    split_ref, mine_ref, planes_far, picks_far, own_ref, coeffs_ref, picks_ref, plane_ref, rows_ref, picks_sem, planes_sem
+    split_ref, coeff_ref, planes_far, picks_far, own_ref, coeffs_ref, picks_ref, plane_ref, rows_ref, picks_sem, planes_sem
 ):
     fetch_picks = pltpu.make_async_copy(picks_far, picks_ref, picks_sem)
     fetch_planes = pltpu.make_async_copy(planes_far, plane_ref, planes_sem)
@@ -152,7 +140,7 @@
     fetch_planes.wait()
     plane_rows(plane_ref[...], rows_ref, coeffs_ref)
     fetch_picks.wait()
-    product(picks_ref, lax.axis_index("core"), mine_ref, split_ref, own_ref, [])
+    product(picks_ref, lax.axis_index("core"), coeff_ref, split_ref, own_ref)
 
 
 def far(x):
@@ -164,7 +152,6 @@
     blocks, picked, height, width = coeff_blocks.shape
     slabs = coeff_blocks.reshape(groups, blocks // groups, picked, height, width)
     half = jax.ShapeDtypeStruct((groups // 2, blocks // groups * height, steps), jnp.float32)
-    half_slabs = (groups // 2,) + slabs.shape[1:]
     cost = pl.CostEstimate(
         flops=2 * blocks * picked * height * width * steps,
         bytes_accessed=blocks * picked * height * width,
@@ -172,22 +159,19 @@
     )
     near, away = pl.BlockSpec(memory_space=pltpu.VMEM), pl.BlockSpec(memory_space=pl.ANY)
     scratch = [pltpu.SMEM(picks.shape, picks.dtype)]
-    other, split, mine = pl.pallas_call(
+    other, split = pl.pallas_call(
         first_kernel,
         out_shape=(
             half,
             jax.ShapeDtypeStruct((across * along * (rows - CODE_ROWS), 2 * steps), jnp.bfloat16),
-            jax.ShapeDtypeStruct(half_slabs, slabs.dtype),
         ),
-        in_specs=[near, away, away],
-        out_specs=(near,) * 3,
-        scratch_shapes=[pltpu.VMEM(half_slabs, slabs.dtype)]
-        + scratch
-        + [pltpu.SemaphoreType.DMA((2, groups // 2)), pltpu.SemaphoreType.DMA],
+        in_specs=[near, away, near],
+        out_specs=(near,) * 2,
+        scratch_shapes=scratch + [pltpu.SemaphoreType.DMA],
         compiler_params=pltpu.CompilerParams(vmem_limit_bytes=24 << 20),
         cost_estimate=cost,
         name="first",
-    )(hist, far(picks), far(slabs))
+    )(hist, far(picks), slabs)
     come = lax.ppermute(other, "core", [(0, 1), (1, 0)])
     own, coeffs = pl.pallas_call(
         second_kernel,
@@ -204,7 +188,7 @@
         compiler_params=pltpu.CompilerParams(vmem_limit_bytes=24 << 20),
         cost_estimate=cost,
         name="second",
-    )(split, mine, far(planes), far(picks))
+    )(split, slabs, far(planes), far(picks))
     return own, come, coeffs
 
 

time: 98.5 us -> 104 us (1.056)
  blocking collectives: 87.9 us -> 94.7 us
    all_to_all x1, blocking collectives: 27.1 us -> 33.9 us  [fetch_window(): lax.all_to_all(lax.cond(mine, scatter, nothing, whole, owner), ROW[0], 0, 0)]
where the time goes in v12:
time: 104 us
  blocking collectives  94.7 us (91%)
  Pallas kernels  4.96 us (5%)
  starting transfers between devices  1.92 us (2%)
  between operations  1.42 us (1%)
    all_to_all x1, blocking collectives, fetch_window(): lax.all_to_all(lax.cond(mine, scatter, nothing, whole, owner), ROW[0], 0, 0)  33.9 us
    all_to_all x1, blocking collectives, body(): parts = lax.all_to_all(pack_sums(own, come), 'yh', 0, 0)  21 us
    all_to_all x1, blocking collectives, gather_over(): return lax.all_to_all(copies, axes, 0, 0)  16.1 us
    all_to_all x1, blocking collectives, body(): column = lax.all_to_all(copies, FIRST, 0, 0)  11.7 us
    all_to_all x1, blocking collectives, fetch_window(): lax.all_to_all(pick_piece(offered, owner, shift, plane), ROW[1:], 0, 0)  9.82 us
    all_gather x1, blocking collectives, fetch_window(): lax.all_gather(whole_half.reshape(plane * rows, steps), 'core', axis=0, t...  2.17 us
  transfers between devices with their start and end apart: 1, of which 1 were waited for; matrix products, arithmetic and copies ran while one was open for 0% of the time, Pallas kernels for 1%

profile of v12, /device:TPU:8, one launch (start us, length us, event | category | flops | bytes accessed | tf_op | source)
XLA Modules:
  0.0 104.0 jit_solution(8274623207788102875)
XLA Ops:
  0.6 0.0 copy-start.3
  0.6 0.0 copy-start.2
  0.7 0.0 copy-start.1
  1.4 0.1 conditional.1
  1.4 0.0 copy-start
  1.4 33.9 %all_to_all.30.offered_ref = bf16[8,128,128]{2,1,0:T(8,128)(2,1)S(1)} all-to-all(bf16[8,128,128]{2,1,0:T(8,128)(2,1)S(1)} %get-tuple-element.26), channel_id=1, replica_groups=mesh['yh'=4,'core'=2,'z'=8,'yl'=2,'x'=4] {'z'}, dimensions={0} | all-to-all | bytes 524288 | tf_op jit(solution)/shard_map/all_to_all | solution.py:358
  35.3 9.8 %all_to_all.31 = bf16[8,128,128]{2,1,0:T(8,128)(2,1)S(1)} all-to-all(bf16[8,128,128]{2,1,0:T(8,128)(2,1)S(1)} %pick.3), channel_id=1, replica_groups=mesh['yh'=4,'core'=2,'z'=8,'yl'=2,'x'=4] {'yl','x'}, dimensions={0} | all-to-all | bytes 524288 | tf_op jit(solution)/shard_map/all_to_all | solution.py:359
  45.2 2.2 %all_gather.3.window_ref = bf16[2048,128]{1,0:T(8,128)(2,1)S(1)} all-gather(bf16[1024,128]{1,0:T(8,128)(2,1)S(1)} %bitcast.22), channel_id=1, replica_groups=mesh['yh'=4,'core'=2,'z'=8,'yl'=2,'x'=4] {'core'}, dimensions={0}, use_global_device_ids=true | all-gather | bytes 786432 | tf_op jit(solution)/shard_map/all_gather | solution.py:360
  47.3 0.0 copy-done.3
  47.3 0.0 copy-done.2
  47.3 0.0 copy-done.1
  47.3 0.9 history.1
  48.2 11.7 %all_to_all.32 = s16[8,56,128]{2,1,0:T(8,128)(2,1)S(1)} all-to-all(s16[8,56,128]{2,1,0:T(8,128)(2,1)S(1)} %history.1), channel_id=1, replica_groups=mesh['yh'=4,'core'=2,'z'=8,'yl'=2,'x'=4] {'z'}, dimensions={0} | all-to-all | bytes 229376 | tf_op jit(solution)/shard_map/all_to_all | solution.py:367
  59.9 0.1 broadcast_in_dim.20
  60.0 16.1 %all_to_all.33.hist_ref = s16[8,8,56,128]{3,2,1,0:T(8,128)(2,1)S(1)} all-to-all(s16[8,8,56,128]{3,2,1,0:T(8,128)(2,1)S(1)} %broadcast_in_dim.20), channel_id=1, replica_groups=mesh['yh'=4,'core'=2,'z'=8,'yl'=2,'x'=4] {'yl','x'}, dimensions={0} | all-to-all | bytes 1835008 | tf_op jit(solution)/shard_map/all_to_all | solution.py:303
  76.1 0.0 copy-done
  76.1 1.3 %first.1 = (f32[4,384,128]{2,1,0:T(8,128)S(1)}, bf16[3072,256]{1,0:T(8,128)(2,1)S(1)}) custom-call(s16[8,8,56,128]{3,2,1,0:T(8,128)(2,1)S(1)} %all_to_all.33.hist_ref, s32[4,24]{1,0:T(4,128)} %bitcast.24, bf16[8,3,4,128,128]{4,3,2,1,0:T(8,128)(2,1)S(1)} %bitcast.17), custom_call_target="tpu_custom_call" | custom-call | flops 402653184 | bytes 1572864 | tf_op jit(solution)/shard_map/first/pallas_call | solution.py:162
  77.5 1.9 %collective-permute-start = (f32[4,384,128]{2,1,0:T(8,128)S(1)}, f32[4,384,128]{2,1,0:T(8,128)S(1)}, u32[]{:S(2)}, u32[]{:S(2)}) collective-permute-start(f32[4,384,128]{2,1,0:T(8,128)S(1)} %get-tuple-element.20), channel_id=1, source_target_pairs={{0,64},{64,0},{1,65},{65,1},{2,66},{66,2},{3,67},{67,3},{4,68},{68... | collective-permute-start | bytes 2359304 | tf_op jit(solution)/shard_map/ppermute | solution.py:175
  79.4 1.5 %second.1 = (f32[4,384,128]{2,1,0:T(8,128)S(1)}, f32[48,128]{1,0:T(8,128)S(1)}) custom-call(bf16[3072,256]{1,0:T(8,128)(2,1)S(1)} %get-tuple-element.18.split_ref, bf16[8,3,4,128,128]{4,3,2,1,0:T(8,128)(2,1)S(1)} %bitcast.18, s32[8,64]{1,0:T(8,128)} %bitcast.26, s32[4,24]{1,0:T(4,128)} %bitcast.25), custom_call_target="tpu_custom_call" | custom-call | flops 402653184 | bytes 1572864 | tf_op jit(solution)/shard_map/second/pallas_call | solution.py:176
  80.9 0.8 collective-permute-done.come_ref
  81.6 0.3 pack.1
  82.0 21.0 %all_to_all.34.parts_ref = s16[4,392,128]{2,1,0:T(8,128)(2,1)S(1)} all-to-all(s16[4,392,128]{2,1,0:T(8,128)(2,1)S(1)} %pack.1), channel_id=1, replica_groups=mesh['yh'=4,'core'=2,'z'=8,'yl'=2,'x'=4] {'yh'}, dimensions={0} | all-to-all | bytes 802816 | tf_op jit(solution)/shard_map/all_to_all | solution.py:370
  103.0 0.9 ranges.1
  (2 shorter events, 0.1 us)
Async XLA Ops:
  0.6 46.7 %copy-start.3 = (f32[48]{0:T(128)S(1)}, f32[48]{0:T(128)}, u32[]{:S(2)}) copy-start(f32[48]{0:T(128)} %param.14) | copy-start | bytes 580
  0.6 46.7 %copy-start.2 = (f32[48]{0:T(128)S(1)}, f32[48]{0:T(128)}, u32[]{:S(2)}) copy-start(f32[48]{0:T(128)} %param.13) | copy-start | bytes 580
  0.7 46.7 %copy-start.1 = (bf16[48,2048]{1,0:T(8,128)(2,1)S(1)}, bf16[48,2048]{1,0:T(8,128)(2,1)}, u32[]{:S(2)}) copy-start(bf16[48,2048]{1,0:T(8,128)(2,1)} %refs_0_.1) | copy-start | bytes 589828
  1.4 74.7 %copy-start = (bf16[1,1,24,4,128,128]{5,4,3,2,1,0:T(8,128)(2,1)S(1)}, bf16[1,1,24,4,128,128]{5,4,3,2,1,0:T(8,128)(2,1)}, u32[]{:S(2)}) copy-start(bf16[1,1,24,4,128,128]{5,4,3,2,1,0:T(8,128)(2,1)} %param.15) | copy-start | bytes 9437188
  77.5 4.2 %collective-permute-start = (f32[4,384,128]{2,1,0:T(8,128)S(1)}, f32[4,384,128]{2,1,0:T(8,128)S(1)}, u32[]{:S(2)}, u32[]{:S(2)}) collective-permute-start(f32[4,384,128]{2,1,0:T(8,128)S(1)} %get-tuple-element.20), channel_id=1, source_target_pairs={{0,64},{64,0},{1,65},{65,1},{2,66},{66,2},{3,67},{67,3},{4,68},{68... | collective-permute-start | bytes 2359304 | tf_op jit(solution)/shard_map/ppermute | solution.py:175
